TPU v7x, 32 devices: a whole 2x2x4 slice. The times are simulated.
32 devices in a mesh: groups: 2 (over y), tm: 4 (over z), space: 2 (over x), yz: 2 (over core).
Axes of the slice: x: 2, y: 2, z: 4, core: 2. Of those that a mesh axis runs over, the one named last changes fastest.
Arguments:
- initial: float32 [96, 32, 128], P(('groups', 'space'), 'yz'), parts along dimension 0, may hold values from -6 to 6
- diffusion: float32 [96, 32, 128], P(('groups', 'space'), 'yz'), parts along dimension 0, may hold values from 0.008 to 0.024
- velocity: float32 [3, 96, 32, 128], P(None, ('groups', 'space'), 'yz'), parts along dimension 1, may hold values from -0.013 to 0.013
- control: float32 [4, 96, 32, 128], P('tm', ('groups', 'space'), 'yz'), parts along dimension 1, may hold values from -0.6 to 0.6
- target: float32 [4, 96, 32, 128], P('tm', ('groups', 'space'), 'yz'), parts along dimension 1, may hold values from -6 to 6
- state_guess: float32 [4, 96, 32, 128], P('tm', ('groups', 'space'), 'yz'), parts along dimension 1, may hold values from -6 to 6
- adjoint_guess: float32 [4, 96, 32, 128], P('tm', ('groups', 'space'), 'yz'), parts along dimension 1, may hold values from -6 to 6
Outputs:
- state_new: float32 [4, 96, 32, 128], P('tm', ('groups', 'space'), 'yz'), parts along dimension 1
- gradient: float32 [4, 96, 32, 128], P('tm', ('groups', 'space'), 'yz'), parts along dimension 1
There are 2 independent parts, one for each index of `groups`. A program takes and returns all parts, laid end to end along the dimension named above; each array names one. Nothing has to cross between parts.
All inputs are finite; a program needn't handle non-finite values.
Results may differ from a plain program's by a relative error of at most 0.00002.
Values sent between devices are 32-bit elements; how exact they have to be, the bound alone decides.
No kernel may reach another device: no remote copies, remote signals or barrier semaphores. Data moves between devices by JAX's collectives and lax.ppermute only.
A program may use at most 64 MiB of HBM per device.

v0:
```python
import jax
import jax.numpy as jnp
from jax import lax
from jax.sharding import PartitionSpec as P

STEPS = 6


def extended(array, sides, width):
    for axis, dim in sides:
        peers, length = (lax.axis_size(axis), array.shape[dim])
        up = [(i, (i + 1) % peers) for i in range(peers - 1)]
        down = [(j, i) for i, j in up]
        last = lax.slice_in_dim(array, length - width, length, axis=dim)
        first = lax.slice_in_dim(array, 0, width, axis=dim)
        before = lax.ppermute(last, axis, up)
        after = lax.ppermute(first, axis, down)
        array = jnp.concatenate([before, array, after], axis=dim)
    return array


def passed_along(block, axis, distance):
    devices = range(lax.axis_size(axis))
    route = [(i - distance, i) for i in devices if i - distance in devices]
    return lax.ppermute(block, axis, route)


def depth_pad(field):
    return jnp.pad(field, ((0, 0), (0, 0), (1, 1)))


def local_map(padded, coefficients, factor, adjoint):
    centre = padded[1:-1, 1:-1, :]
    if adjoint:
        spread = coefficients[0] * padded
        carried = coefficients[1:4] * padded
        inner_spread = spread[1:-1, 1:-1, :]
        deep = depth_pad(inner_spread)
        laplace = (
            spread[2:, 1:-1, :]
            + spread[:-2, 1:-1, :]
            + spread[1:-1, 2:, :]
            + spread[1:-1, :-2, :]
            + deep[:, :, 2:]
            + deep[:, :, :-2]
            - 6.0 * inner_spread
        )
        deep_carry = depth_pad(carried[2, 1:-1, 1:-1, :])
        transport = (
            carried[0, 2:, 1:-1, :]
            - carried[0, :-2, 1:-1, :]
            + (carried[1, 1:-1, 2:, :] - carried[1, 1:-1, :-2, :])
            + (deep_carry[:, :, 2:] - deep_carry[:, :, :-2])
        )
        return (centre + factor * (laplace + transport)) * coefficients[4, 1:-1, 1:-1, :]
    inner = coefficients[:, 1:-1, 1:-1, :]
    deep = depth_pad(centre)
    laplace = (
        padded[2:, 1:-1, :]
        + padded[:-2, 1:-1, :]
        + padded[1:-1, 2:, :]
        + padded[1:-1, :-2, :]
        + deep[:, :, 2:]
        + deep[:, :, :-2]
        - 6.0 * centre
    )
    transport = (
        inner[1] * (padded[2:, 1:-1, :] - padded[:-2, 1:-1, :])
        + inner[2] * (padded[1:-1, 2:, :] - padded[1:-1, :-2, :])
        + inner[3] * (deep[:, :, 2:] - deep[:, :, :-2])
    )
    return centre + factor * (inner[0] * laplace - transport)


def halo_cells(field):
    return extended(field, (("space", 0), ("yz", 1)), 1)


def coefficient_window(rim_coefficients, offset):
    return rim_coefficients[
        :,
        offset : rim_coefficients.shape[1] - offset,
        offset : rim_coefficients.shape[2] - offset,
        :,
    ]


def coarse_chain(residual, near_coefficients, adjoint, direction):
    factor = float(STEPS)

    def one_turn(turn_index, correction):
        moved = local_map(halo_cells(correction), near_coefficients, factor, adjoint)
        arrived = passed_along(moved, "tm", direction)
        return residual + arrived

    return lax.fori_loop(0, lax.axis_size("tm") - 1, one_turn, residual)


def local(initial, diffusion, velocity, control, target, state_guess, adjoint_guess):
    rim_depth = max(lax.axis_size("tm") // 2, STEPS)
    source = control[0]
    guess_state = state_guess[0]
    guess_adjoint = adjoint_guess[0]
    stacked = jnp.concatenate([diffusion[None], velocity, jnp.ones_like(diffusion)[None]], 0)
    rim_coefficients = extended(stacked, (("space", 1), ("yz", 2)), rim_depth)
    near_coefficients = coefficient_window(rim_coefficients, rim_depth - 1)
    arrived = passed_along(guess_state, "tm", 1)
    fine = jnp.where(lax.axis_index("tm") == 0, initial, arrived)
    sweep = guess_adjoint
    for step_index in range(STEPS):
        fine = local_map(halo_cells(fine), near_coefficients, 1.0, False) + source
    for step_index in range(STEPS):
        sweep = local_map(halo_cells(sweep), near_coefficients, 1.0, True)
    state_residual = fine - guess_state
    state_new = guess_state + coarse_chain(state_residual, near_coefficients, False, 1)
    from_next = passed_along(sweep, "tm", -1)
    adjoint_residual = from_next + state_new - target[0] - guess_adjoint
    multiplier = guess_adjoint + coarse_chain(adjoint_residual, near_coefficients, True, -1)
    running_sum = multiplier
    for step_index in range(STEPS - 1):
        multiplier = local_map(halo_cells(multiplier), near_coefficients, 1.0, True)
        running_sum = running_sum + multiplier
    gradient = running_sum / float(STEPS) + 0.5 * source
    return (state_new[None], gradient[None])


def solution(mesh):
    return jax.shard_map(
        local,
        mesh=mesh,
        in_specs=(
            P(("groups", "space"), "yz", None),
            P(("groups", "space"), "yz", None),
            P(None, ("groups", "space"), "yz", None),
            P("tm", ("groups", "space"), "yz", None),
            P("tm", ("groups", "space"), "yz", None),
            P("tm", ("groups", "space"), "yz", None),
            P("tm", ("groups", "space"), "yz", None),
        ),
        out_specs=(
            P("tm", ("groups", "space"), "yz", None),
            P("tm", ("groups", "space"), "yz", None),
        ),
        check_vma=False,
    )
```

profile of v0, /device:TPU:17, one launch (start us, length us, event | category | flops | bytes accessed | tf_op | source)
XLA Modules:
  0.0 365.2 jit_solution(18016390392129287426)
XLA Ops:
  1.7 3.2 collective-permute-start.10
  4.9 4.4 %collective-permute-done.10 = f32[24,16,128]{2,0,1:T(8,128)S(1)} collective-permute-done((f32[24,16,128]{2,0,1:T(8,128)S(1)}, f32[24,16,128]{2,0,1:T(8,128)S(1)}, u32[]{:S(2)}, u32[]{:S(2)}) %collective-permute-start.10) | collective-permute-done | bytes 196640 | tf_op jit(solution)/shard_map/ppermute | solution.py:25
  11.7 4.0 %collective-permute-start.12 = (f32[1,16,128]{2,0,1:T(1,128)S(1)}, f32[1,16,128]{2,0,1:T(1,128)S(1)}, u32[]{:S(2)}, u32[]{:S(2)}) collective-permute-start(f32[1,16,128]{2,0,1:T(1,128)S(1)} %get-tuple-element.245), channel_id=1, source_target_pairs={{0,2},{1,3},{4,6},{5,7},{8,10},{9,11},{12,14},{13,15},{16,18},{17,... | collective-permute-start | bytes 24584 | tf_op jit(solution)/shard_map/ppermute | solution.py:16
  16.5 4.6 %collective-permute-start.13 = (f32[26,1,128]{2,0,1:T(8,128)S(1)}, f32[26,1,128]{2,0,1:T(8,128)S(1)}, u32[]{:S(2)}, u32[]{:S(2)}) collective-permute-start(f32[26,1,128]{2,0,1:T(8,128)S(1)} %get-tuple-element.209), channel_id=1, source_target_pairs={{1,0},{3,2},{5,4},{7,6},{9,8},{11,10},{13,12},{15,14},{17,16},{19,... | collective-permute-start | bytes 39944 | tf_op jit(solution)/shard_map/ppermute | solution.py:17
  26.8 4.0 %collective-permute-start.16 = (f32[1,16,128]{2,0,1:T(1,128)S(1)}, f32[1,16,128]{2,0,1:T(1,128)S(1)}, u32[]{:S(2)}, u32[]{:S(2)}) collective-permute-start(f32[1,16,128]{2,0,1:T(1,128)S(1)} %get-tuple-element.243), channel_id=1, source_target_pairs={{0,2},{1,3},{4,6},{5,7},{8,10},{9,11},{12,14},{13,15},{16,18},{17,... | collective-permute-start | bytes 24584 | tf_op jit(solution)/shard_map/ppermute | solution.py:16
  31.5 3.7 %collective-permute-start.17 = (f32[26,1,128]{2,0,1:T(8,128)S(1)}, f32[26,1,128]{2,0,1:T(8,128)S(1)}, u32[]{:S(2)}, u32[]{:S(2)}) collective-permute-start(f32[26,1,128]{2,0,1:T(8,128)S(1)} %get-tuple-element.207), channel_id=1, source_target_pairs={{1,0},{3,2},{5,4},{7,6},{9,8},{11,10},{13,12},{15,14},{17,16},{19,... | collective-permute-start | bytes 39944 | tf_op jit(solution)/shard_map/ppermute | solution.py:17
  38.8 3.9 %collective-permute-start.35 = (f32[5,6,16,128]{3,1,2,0:T(8,128)S(1)}, f32[5,6,16,128]{3,1,2,0:T(8,128)S(1)}, u32[]{:S(2)}, u32[]{:S(2)}) collective-permute-start(f32[5,6,16,128]{3,1,2,0:T(8,128)S(1)} %get-tuple-element.152), channel_id=1, source_target_pairs={{0,2},{1,3},{4,6},{5,7},{8,10},{9,11},{12,14},{13,15},{16,18},{17,... | collective-permute-start | bytes 737288 | tf_op jit(solution)/shard_map/ppermute | solution.py:16
  45.4 4.0 %collective-permute-start.20 = (f32[1,16,128]{2,0,1:T(1,128)S(1)}, f32[1,16,128]{2,0,1:T(1,128)S(1)}, u32[]{:S(2)}, u32[]{:S(2)}) collective-permute-start(f32[1,16,128]{2,0,1:T(1,128)S(1)} %get-tuple-element.241), channel_id=1, source_target_pairs={{0,2},{1,3},{4,6},{5,7},{8,10},{9,11},{12,14},{13,15},{16,18},{17,... | collective-permute-start | bytes 24584 | tf_op jit(solution)/shard_map/ppermute | solution.py:16
  49.7 3.8 %collective-permute-done.36 = f32[5,6,16,128]{3,1,2,0:T(8,128)S(1)} collective-permute-done((f32[5,6,16,128]{3,1,2,0:T(8,128)S(1)}, f32[5,6,16,128]{3,1,2,0:T(8,128)S(1)}, u32[]{:S(2)}, u32[]{:S(2)}) %collective-permute-start.36) | collective-permute-done | bytes 245792 | tf_op jit(solution)/shard_map/ppermute | solution.py:17
  56.0 3.3 collective-permute-start.38
  73.1 3.8 %collective-permute-start.43 = (f32[1,16,128]{2,0,1:T(1,128)S(1)}, f32[1,16,128]{2,0,1:T(1,128)S(1)}, u32[]{:S(2)}, u32[]{:S(2)}) collective-permute-start(f32[1,16,128]{2,0,1:T(1,128)S(1)} %get-tuple-element.229), channel_id=1, source_target_pairs={{0,2},{1,3},{4,6},{5,7},{8,10},{9,11},{12,14},{13,15},{16,18},{17,... | collective-permute-start | bytes 24584 | tf_op jit(solution)/shard_map/ppermute | solution.py:16
  79.5 4.0 %collective-permute-start.24 = (f32[1,16,128]{2,0,1:T(1,128)S(1)}, f32[1,16,128]{2,0,1:T(1,128)S(1)}, u32[]{:S(2)}, u32[]{:S(2)}) collective-permute-start(f32[1,16,128]{2,0,1:T(1,128)S(1)} %get-tuple-element.239), channel_id=1, source_target_pairs={{0,2},{1,3},{4,6},{5,7},{8,10},{9,11},{12,14},{13,15},{16,18},{17,... | collective-permute-start | bytes 24584 | tf_op jit(solution)/shard_map/ppermute | solution.py:16
  84.9 3.1 collective-permute-start.46
  99.5 4.5 %collective-permute-start.50 = (f32[26,1,128]{2,0,1:T(8,128)S(1)}, f32[26,1,128]{2,0,1:T(8,128)S(1)}, u32[]{:S(2)}, u32[]{:S(2)}) collective-permute-start(f32[26,1,128]{2,0,1:T(8,128)S(1)} %get-tuple-element.194), channel_id=1, source_target_pairs={{1,0},{3,2},{5,4},{7,6},{9,8},{11,10},{13,12},{15,14},{17,16},{19,... | collective-permute-start | bytes 39944 | tf_op jit(solution)/shard_map/ppermute | solution.py:17
  105.3 4.0 %collective-permute-start.28 = (f32[1,16,128]{2,0,1:T(1,128)S(1)}, f32[1,16,128]{2,0,1:T(1,128)S(1)}, u32[]{:S(2)}, u32[]{:S(2)}) collective-permute-start(f32[1,16,128]{2,0,1:T(1,128)S(1)} %get-tuple-element.237), channel_id=1, source_target_pairs={{0,2},{1,3},{4,6},{5,7},{8,10},{9,11},{12,14},{13,15},{16,18},{17,... | collective-permute-start | bytes 24584 | tf_op jit(solution)/shard_map/ppermute | solution.py:16
  121.3 4.3 %collective-permute-start.55 = (f32[1,16,128]{2,0,1:T(1,128)S(1)}, f32[1,16,128]{2,0,1:T(1,128)S(1)}, u32[]{:S(2)}, u32[]{:S(2)}) collective-permute-start(f32[1,16,128]{2,0,1:T(1,128)S(1)} %get-tuple-element.223), channel_id=1, source_target_pairs={{0,2},{1,3},{4,6},{5,7},{8,10},{9,11},{12,14},{13,15},{16,18},{17,... | collective-permute-start | bytes 24584 | tf_op jit(solution)/shard_map/ppermute | solution.py:16
  128.2 4.0 %collective-permute-start.32 = (f32[1,16,128]{2,0,1:T(1,128)S(1)}, f32[1,16,128]{2,0,1:T(1,128)S(1)}, u32[]{:S(2)}, u32[]{:S(2)}) collective-permute-start(f32[1,16,128]{2,0,1:T(1,128)S(1)} %get-tuple-element.235), channel_id=1, source_target_pairs={{0,2},{1,3},{4,6},{5,7},{8,10},{9,11},{12,14},{13,15},{16,18},{17,... | collective-permute-start | bytes 24584 | tf_op jit(solution)/shard_map/ppermute | solution.py:16
  133.6 3.1 collective-permute-start.58
  148.2 4.5 %collective-permute-start.62 = (f32[26,1,128]{2,0,1:T(8,128)S(1)}, f32[26,1,128]{2,0,1:T(8,128)S(1)}, u32[]{:S(2)}, u32[]{:S(2)}) collective-permute-start(f32[26,1,128]{2,0,1:T(8,128)S(1)} %get-tuple-element.188), channel_id=1, source_target_pairs={{1,0},{3,2},{5,4},{7,6},{9,8},{11,10},{13,12},{15,14},{17,16},{19,... | collective-permute-start | bytes 39944 | tf_op jit(solution)/shard_map/ppermute | solution.py:17
  157.4 68.7 %while.24 = (s32[]{:T(128)}, f32[24,16,128]{2,1,0:T(8,128)S(1)}, f32[5,26,18,128]{3,2,1,0:T(8,128)S(1)}, f32[24,16,128]{2,1,0:T(8,128)S(1)}, s32[]{:T(128)}) while((s32[]{:T(128)}, f32[24,16,128]{2,1,0:T(8,128)S(1)}, f32[5,26,18,128]{3,2,1,0:T(8,128)S(1)}, f32[24,16,128]{2,1,0:T(8,128)S(1)}, s32[]{:T(128)}) %tuple.120), condition=%wide.region_1.2_spmd, body=%wide.region_0.1_spmd.sunk | while | flops 1179650 | bytes 4282657 | solution.py:96
  160.2 3.5 collective-permute-done.1
  164.9 3.1 collective-permute-start.3
  169.8 3.7 %collective-permute-start.4 = (f32[24,16,128]{2,1,0:T(8,128)}, f32[24,16,128]{2,1,0:T(8,128)S(1)}, u32[]{:S(2)}, u32[]{:S(2)}) collective-permute-start(f32[24,16,128]{2,1,0:T(8,128)} %fusion.162), channel_id=1, source_target_pairs={{0,4},{4,8},{8,12},{1,5},{5,9},{9,13},{2,6},{6,10},{10,14},{3,7},{... | collective-permute-start | bytes 589832 | tf_op jit(solution)/shard_map/while/body/eval_jaxpr/ppermute | solution.py:25
  173.5 4.6 %collective-permute-done.4 = f32[24,16,128]{2,1,0:T(8,128)S(1)} collective-permute-done((f32[24,16,128]{2,1,0:T(8,128)}, f32[24,16,128]{2,1,0:T(8,128)S(1)}, u32[]{:S(2)}, u32[]{:S(2)}) %collective-permute-start.4) | collective-permute-done | bytes 196640 | tf_op jit(solution)/shard_map/while/body/eval_jaxpr/ppermute | solution.py:25
  182.4 3.1 collective-permute-done.1
  186.8 4.5 %collective-permute-start.3 = (f32[26,1,128]{2,1,0:T(1,128)S(1)}, f32[26,1,128]{2,1,0:T(1,128)S(1)}, u32[]{:S(2)}, u32[]{:S(2)}) collective-permute-start(f32[26,1,128]{2,1,0:T(1,128)S(1)} %get-tuple-element.306), channel_id=1, source_target_pairs={{1,0},{3,2},{5,4},{7,6},{9,8},{11,10},{13,12},{15,14},{17,16},{19,... | collective-permute-start | bytes 39944 | tf_op jit(solution)/shard_map/while/body/eval_jaxpr/ppermute | solution.py:17
  193.0 3.7 %collective-permute-start.4 = (f32[24,16,128]{2,1,0:T(8,128)}, f32[24,16,128]{2,1,0:T(8,128)S(1)}, u32[]{:S(2)}, u32[]{:S(2)}) collective-permute-start(f32[24,16,128]{2,1,0:T(8,128)} %fusion.162), channel_id=1, source_target_pairs={{0,4},{4,8},{8,12},{1,5},{5,9},{9,13},{2,6},{6,10},{10,14},{3,7},{... | collective-permute-start | bytes 589832 | tf_op jit(solution)/shard_map/while/body/eval_jaxpr/ppermute | solution.py:25
  196.7 4.6 %collective-permute-done.4 = f32[24,16,128]{2,1,0:T(8,128)S(1)} collective-permute-done((f32[24,16,128]{2,1,0:T(8,128)}, f32[24,16,128]{2,1,0:T(8,128)S(1)}, u32[]{:S(2)}, u32[]{:S(2)}) %collective-permute-start.4) | collective-permute-done | bytes 196640 | tf_op jit(solution)/shard_map/while/body/eval_jaxpr/ppermute | solution.py:25
  210.0 4.5 %collective-permute-start.3 = (f32[26,1,128]{2,1,0:T(1,128)S(1)}, f32[26,1,128]{2,1,0:T(1,128)S(1)}, u32[]{:S(2)}, u32[]{:S(2)}) collective-permute-start(f32[26,1,128]{2,1,0:T(1,128)S(1)} %get-tuple-element.306), channel_id=1, source_target_pairs={{1,0},{3,2},{5,4},{7,6},{9,8},{11,10},{13,12},{15,14},{17,16},{19,... | collective-permute-start | bytes 39944 | tf_op jit(solution)/shard_map/while/body/eval_jaxpr/ppermute | solution.py:17
  216.3 3.7 %collective-permute-start.4 = (f32[24,16,128]{2,1,0:T(8,128)}, f32[24,16,128]{2,1,0:T(8,128)S(1)}, u32[]{:S(2)}, u32[]{:S(2)}) collective-permute-start(f32[24,16,128]{2,1,0:T(8,128)} %fusion.162), channel_id=1, source_target_pairs={{0,4},{4,8},{8,12},{1,5},{5,9},{9,13},{2,6},{6,10},{10,14},{3,7},{... | collective-permute-start | bytes 589832 | tf_op jit(solution)/shard_map/while/body/eval_jaxpr/ppermute | solution.py:25
  219.9 4.6 %collective-permute-done.4 = f32[24,16,128]{2,1,0:T(8,128)S(1)} collective-permute-done((f32[24,16,128]{2,1,0:T(8,128)}, f32[24,16,128]{2,1,0:T(8,128)S(1)}, u32[]{:S(2)}, u32[]{:S(2)}) %collective-permute-start.4) | collective-permute-done | bytes 196640 | tf_op jit(solution)/shard_map/while/body/eval_jaxpr/ppermute | solution.py:25
  228.4 73.6 %while.25 = (s32[]{:T(128)}, f32[24,16,128]{2,1,0:T(8,128)S(1)}, f32[5,26,18,128]{3,2,1,0:T(8,128)S(1)}, f32[24,16,128]{2,1,0:T(8,128)S(1)}, s32[]{:T(128)}) while((s32[]{:T(128)}, f32[24,16,128]{2,1,0:T(8,128)S(1)}, f32[5,26,18,128]{3,2,1,0:T(8,128)S(1)}, f32[24,16,128]{2,1,0:T(8,128)S(1)}, s32[]{:T(128)}) %tuple.126), condition=%wide.region_3.4_spmd, body=%wide.region_2.3_spmd.sunk | while | flops 1195010 | bytes 8825121 | solution.py:96
  234.2 4.5 %collective-permute-start.7 = (f32[26,1,128]{2,1,0:T(1,128)S(1)}, f32[26,1,128]{2,1,0:T(1,128)S(1)}, u32[]{:S(2)}, u32[]{:S(2)}) collective-permute-start(f32[26,1,128]{2,1,0:T(1,128)S(1)} %get-tuple-element.313), channel_id=1, source_target_pairs={{1,0},{3,2},{5,4},{7,6},{9,8},{11,10},{13,12},{15,14},{17,16},{19,... | collective-permute-start | bytes 39944 | tf_op jit(solution)/shard_map/while/body/eval_jaxpr/ppermute | solution.py:17
  244.9 6.5 %collective-permute-done.9 = f32[24,16,128]{2,1,0:T(8,128)S(1)} collective-permute-done((f32[24,16,128]{2,1,0:T(8,128)}, f32[24,16,128]{2,1,0:T(8,128)S(1)}, u32[]{:S(2)}, u32[]{:S(2)}) %collective-permute-start.9) | collective-permute-done | bytes 196640 | tf_op jit(solution)/shard_map/while/body/eval_jaxpr/ppermute | solution.py:25
  258.9 4.3 %collective-permute-start.7 = (f32[26,1,128]{2,1,0:T(1,128)S(1)}, f32[26,1,128]{2,1,0:T(1,128)S(1)}, u32[]{:S(2)}, u32[]{:S(2)}) collective-permute-start(f32[26,1,128]{2,1,0:T(1,128)S(1)} %get-tuple-element.313), channel_id=1, source_target_pairs={{1,0},{3,2},{5,4},{7,6},{9,8},{11,10},{13,12},{15,14},{17,16},{19,... | collective-permute-start | bytes 39944 | tf_op jit(solution)/shard_map/while/body/eval_jaxpr/ppermute | solution.py:17
  269.4 6.5 %collective-permute-done.9 = f32[24,16,128]{2,1,0:T(8,128)S(1)} collective-permute-done((f32[24,16,128]{2,1,0:T(8,128)}, f32[24,16,128]{2,1,0:T(8,128)S(1)}, u32[]{:S(2)}, u32[]{:S(2)}) %collective-permute-start.9) | collective-permute-done | bytes 196640 | tf_op jit(solution)/shard_map/while/body/eval_jaxpr/ppermute | solution.py:25
  283.3 4.3 %collective-permute-start.7 = (f32[26,1,128]{2,1,0:T(1,128)S(1)}, f32[26,1,128]{2,1,0:T(1,128)S(1)}, u32[]{:S(2)}, u32[]{:S(2)}) collective-permute-start(f32[26,1,128]{2,1,0:T(1,128)S(1)} %get-tuple-element.313), channel_id=1, source_target_pairs={{1,0},{3,2},{5,4},{7,6},{9,8},{11,10},{13,12},{15,14},{17,16},{19,... | collective-permute-start | bytes 39944 | tf_op jit(solution)/shard_map/while/body/eval_jaxpr/ppermute | solution.py:17
  293.8 6.5 %collective-permute-done.9 = f32[24,16,128]{2,1,0:T(8,128)S(1)} collective-permute-done((f32[24,16,128]{2,1,0:T(8,128)}, f32[24,16,128]{2,1,0:T(8,128)S(1)}, u32[]{:S(2)}, u32[]{:S(2)}) %collective-permute-start.9) | collective-permute-done | bytes 196640 | tf_op jit(solution)/shard_map/while/body/eval_jaxpr/ppermute | solution.py:25
  305.8 3.1 collective-permute-done.65
  310.2 4.3 %collective-permute-start.67 = (f32[26,1,128]{2,0,1:T(8,128)S(1)}, f32[26,1,128]{2,0,1:T(8,128)S(1)}, u32[]{:S(2)}, u32[]{:S(2)}) collective-permute-start(f32[26,1,128]{2,0,1:T(8,128)S(1)} %get-tuple-element.186), channel_id=1, source_target_pairs={{1,0},{3,2},{5,4},{7,6},{9,8},{11,10},{13,12},{15,14},{17,16},{19,... | collective-permute-start | bytes 39944 | tf_op jit(solution)/shard_map/ppermute | solution.py:17
  318.5 3.1 collective-permute-done.69
  322.9 3.7 %collective-permute-start.71 = (f32[26,1,128]{2,0,1:T(8,128)S(1)}, f32[26,1,128]{2,0,1:T(8,128)S(1)}, u32[]{:S(2)}, u32[]{:S(2)}) collective-permute-start(f32[26,1,128]{2,0,1:T(8,128)S(1)} %get-tuple-element.184), channel_id=1, source_target_pairs={{1,0},{3,2},{5,4},{7,6},{9,8},{11,10},{13,12},{15,14},{17,16},{19,... | collective-permute-start | bytes 39944 | tf_op jit(solution)/shard_map/ppermute | solution.py:17
  330.6 3.1 collective-permute-done.73
  335.0 3.7 %collective-permute-start.75 = (f32[26,1,128]{2,0,1:T(8,128)S(1)}, f32[26,1,128]{2,0,1:T(8,128)S(1)}, u32[]{:S(2)}, u32[]{:S(2)}) collective-permute-start(f32[26,1,128]{2,0,1:T(8,128)S(1)} %get-tuple-element.182), channel_id=1, source_target_pairs={{1,0},{3,2},{5,4},{7,6},{9,8},{11,10},{13,12},{15,14},{17,16},{19,... | collective-permute-start | bytes 39944 | tf_op jit(solution)/shard_map/ppermute | solution.py:17
  342.8 3.1 collective-permute-done.77
  347.2 3.7 %collective-permute-start.79 = (f32[26,1,128]{2,0,1:T(8,128)S(1)}, f32[26,1,128]{2,0,1:T(8,128)S(1)}, u32[]{:S(2)}, u32[]{:S(2)}) collective-permute-start(f32[26,1,128]{2,0,1:T(8,128)S(1)} %get-tuple-element.180), channel_id=1, source_target_pairs={{1,0},{3,2},{5,4},{7,6},{9,8},{11,10},{13,12},{15,14},{17,16},{19,... | collective-permute-start | bytes 39944 | tf_op jit(solution)/shard_map/ppermute | solution.py:17
  354.9 3.1 collective-permute-done.81
  359.3 3.7 %collective-permute-start.83 = (f32[26,1,128]{2,0,1:T(8,128)S(1)}, f32[26,1,128]{2,0,1:T(8,128)S(1)}, u32[]{:S(2)}, u32[]{:S(2)}) collective-permute-start(f32[26,1,128]{2,0,1:T(8,128)S(1)} %get-tuple-element.178), channel_id=1, source_target_pairs={{1,0},{3,2},{5,4},{7,6},{9,8},{11,10},{13,12},{15,14},{17,16},{19,... | collective-permute-start | bytes 39944 | tf_op jit(solution)/shard_map/ppermute | solution.py:17
  (365 shorter events, 177.6 us)
Async XLA Ops:
  1.7 7.7 %collective-permute-start.10 = (f32[24,16,128]{2,0,1:T(8,128)S(1)}, f32[24,16,128]{2,0,1:T(8,128)S(1)}, u32[]{:S(2)}, u32[]{:S(2)}) collective-permute-start(f32[24,16,128]{2,0,1:T(8,128)S(1)} %bitcast.203), channel_id=1, source_target_pairs={{0,4},{4,8},{8,12},{1,5},{5,9},{9,13},{2,6},{6,10},{10,14},{3,7},{... | collective-permute-start | bytes 589832 | tf_op jit(solution)/shard_map/ppermute | solution.py:25
  16.5 7.2 %collective-permute-start.13 = (f32[26,1,128]{2,0,1:T(8,128)S(1)}, f32[26,1,128]{2,0,1:T(8,128)S(1)}, u32[]{:S(2)}, u32[]{:S(2)}) collective-permute-start(f32[26,1,128]{2,0,1:T(8,128)S(1)} %get-tuple-element.209), channel_id=1, source_target_pairs={{1,0},{3,2},{5,4},{7,6},{9,8},{11,10},{13,12},{15,14},{17,16},{19,... | collective-permute-start | bytes 39944 | tf_op jit(solution)/shard_map/ppermute | solution.py:17
  38.8 10.9 %collective-permute-start.35 = (f32[5,6,16,128]{3,1,2,0:T(8,128)S(1)}, f32[5,6,16,128]{3,1,2,0:T(8,128)S(1)}, u32[]{:S(2)}, u32[]{:S(2)}) collective-permute-start(f32[5,6,16,128]{3,1,2,0:T(8,128)S(1)} %get-tuple-element.152), channel_id=1, source_target_pairs={{0,2},{1,3},{4,6},{5,7},{8,10},{9,11},{12,14},{13,15},{16,18},{17,... | collective-permute-start | bytes 737288 | tf_op jit(solution)/shard_map/ppermute | solution.py:16
  42.7 10.7 %collective-permute-start.36 = (f32[5,6,16,128]{3,1,2,0:T(8,128)S(1)}, f32[5,6,16,128]{3,1,2,0:T(8,128)S(1)}, u32[]{:S(2)}, u32[]{:S(2)}) collective-permute-start(f32[5,6,16,128]{3,1,2,0:T(8,128)S(1)} %get-tuple-element.153), channel_id=1, source_target_pairs={{2,0},{3,1},{6,4},{7,5},{10,8},{11,9},{14,12},{15,13},{18,16},{19,... | collective-permute-start | bytes 737288 | tf_op jit(solution)/shard_map/ppermute | solution.py:17
  44.1 16.7 %collective-permute-start.19 = (f32[1,16,128]{2,0,1:T(1,128)S(1)}, f32[1,16,128]{2,0,1:T(1,128)S(1)}, u32[]{:S(2)}, u32[]{:S(2)}) collective-permute-start(f32[1,16,128]{2,0,1:T(1,128)S(1)} %get-tuple-element.242), channel_id=1, source_target_pairs={{2,0},{3,1},{6,4},{7,5},{10,8},{11,9},{14,12},{15,13},{18,16},{19,... | collective-permute-start | bytes 24584 | tf_op jit(solution)/shard_map/ppermute | solution.py:17
  45.4 16.7 %collective-permute-start.20 = (f32[1,16,128]{2,0,1:T(1,128)S(1)}, f32[1,16,128]{2,0,1:T(1,128)S(1)}, u32[]{:S(2)}, u32[]{:S(2)}) collective-permute-start(f32[1,16,128]{2,0,1:T(1,128)S(1)} %get-tuple-element.241), channel_id=1, source_target_pairs={{0,2},{1,3},{4,6},{5,7},{8,10},{9,11},{12,14},{13,15},{16,18},{17,... | collective-permute-start | bytes 24584 | tf_op jit(solution)/shard_map/ppermute | solution.py:16
  54.7 15.9 %collective-permute-start.37 = (f32[5,36,6,128]{3,1,2,0:T(8,128)}, f32[5,36,6,128]{3,1,2,0:T(8,128)S(1)}, u32[]{:S(2)}, u32[]{:S(2)}) collective-permute-start(f32[5,36,6,128]{3,1,2,0:T(8,128)} %get-tuple-element.150), channel_id=1, source_target_pairs={{0,1},{2,3},{4,5},{6,7},{8,9},{10,11},{12,13},{14,15},{16,17},{18,... | collective-permute-start | bytes 1658888 | tf_op jit(solution)/shard_map/ppermute | solution.py:16
  56.0 14.7 %collective-permute-start.38 = (f32[5,36,6,128]{3,1,2,0:T(8,128)}, f32[5,36,6,128]{3,1,2,0:T(8,128)S(1)}, u32[]{:S(2)}, u32[]{:S(2)}) collective-permute-start(f32[5,36,6,128]{3,1,2,0:T(8,128)} %get-tuple-element.151), channel_id=1, source_target_pairs={{1,0},{3,2},{5,4},{7,6},{9,8},{11,10},{13,12},{15,14},{17,16},{19,... | collective-permute-start | bytes 1658888 | tf_op jit(solution)/shard_map/ppermute | solution.py:17
  63.6 6.2 %collective-permute-start.22 = (f32[26,1,128]{2,0,1:T(8,128)S(1)}, f32[26,1,128]{2,0,1:T(8,128)S(1)}, u32[]{:S(2)}, u32[]{:S(2)}) collective-permute-start(f32[26,1,128]{2,0,1:T(8,128)S(1)} %get-tuple-element.206), channel_id=1, source_target_pairs={{0,1},{2,3},{4,5},{6,7},{8,9},{10,11},{12,13},{14,15},{16,17},{18,... | collective-permute-start | bytes 39944 | tf_op jit(solution)/shard_map/ppermute | solution.py:16
  73.1 10.4 %collective-permute-start.43 = (f32[1,16,128]{2,0,1:T(1,128)S(1)}, f32[1,16,128]{2,0,1:T(1,128)S(1)}, u32[]{:S(2)}, u32[]{:S(2)}) collective-permute-start(f32[1,16,128]{2,0,1:T(1,128)S(1)} %get-tuple-element.229), channel_id=1, source_target_pairs={{0,2},{1,3},{4,6},{5,7},{8,10},{9,11},{12,14},{13,15},{16,18},{17,... | collective-permute-start | bytes 24584 | tf_op jit(solution)/shard_map/ppermute | solution.py:16
  76.9 6.6 %collective-permute-start.44 = (f32[1,16,128]{2,0,1:T(1,128)S(1)}, f32[1,16,128]{2,0,1:T(1,128)S(1)}, u32[]{:S(2)}, u32[]{:S(2)}) collective-permute-start(f32[1,16,128]{2,0,1:T(1,128)S(1)} %get-tuple-element.230), channel_id=1, source_target_pairs={{2,0},{3,1},{6,4},{7,5},{10,8},{11,9},{14,12},{15,13},{18,16},{19,... | collective-permute-start | bytes 24584 | tf_op jit(solution)/shard_map/ppermute | solution.py:17
  78.2 9.7 %collective-permute-start.23 = (f32[1,16,128]{2,0,1:T(1,128)S(1)}, f32[1,16,128]{2,0,1:T(1,128)S(1)}, u32[]{:S(2)}, u32[]{:S(2)}) collective-permute-start(f32[1,16,128]{2,0,1:T(1,128)S(1)} %get-tuple-element.240), channel_id=1, source_target_pairs={{2,0},{3,1},{6,4},{7,5},{10,8},{11,9},{14,12},{15,13},{18,16},{19,... | collective-permute-start | bytes 24584 | tf_op jit(solution)/shard_map/ppermute | solution.py:17
  79.5 8.4 %collective-permute-start.24 = (f32[1,16,128]{2,0,1:T(1,128)S(1)}, f32[1,16,128]{2,0,1:T(1,128)S(1)}, u32[]{:S(2)}, u32[]{:S(2)}) collective-permute-start(f32[1,16,128]{2,0,1:T(1,128)S(1)} %get-tuple-element.239), channel_id=1, source_target_pairs={{0,2},{1,3},{4,6},{5,7},{8,10},{9,11},{12,14},{13,15},{16,18},{17,... | collective-permute-start | bytes 24584 | tf_op jit(solution)/shard_map/ppermute | solution.py:16
  83.6 7.0 %collective-permute-start.45 = (f32[26,1,128]{2,0,1:T(8,128)S(1)}, f32[26,1,128]{2,0,1:T(8,128)S(1)}, u32[]{:S(2)}, u32[]{:S(2)}) collective-permute-start(f32[26,1,128]{2,0,1:T(8,128)S(1)} %get-tuple-element.195), channel_id=1, source_target_pairs={{0,1},{2,3},{4,5},{6,7},{8,9},{10,11},{12,13},{14,15},{16,17},{18,... | collective-permute-start | bytes 39944 | tf_op jit(solution)/shard_map/ppermute | solution.py:16
  84.9 5.8 %collective-permute-start.46 = (f32[26,1,128]{2,0,1:T(8,128)S(1)}, f32[26,1,128]{2,0,1:T(8,128)S(1)}, u32[]{:S(2)}, u32[]{:S(2)}) collective-permute-start(f32[26,1,128]{2,0,1:T(8,128)S(1)} %get-tuple-element.196), channel_id=1, source_target_pairs={{1,0},{3,2},{5,4},{7,6},{9,8},{11,10},{13,12},{15,14},{17,16},{19,... | collective-permute-start | bytes 39944 | tf_op jit(solution)/shard_map/ppermute | solution.py:17
  88.0 7.1 %collective-permute-start.25 = (f32[26,1,128]{2,0,1:T(8,128)S(1)}, f32[26,1,128]{2,0,1:T(8,128)S(1)}, u32[]{:S(2)}, u32[]{:S(2)}) collective-permute-start(f32[26,1,128]{2,0,1:T(8,128)S(1)} %get-tuple-element.203), channel_id=1, source_target_pairs={{1,0},{3,2},{5,4},{7,6},{9,8},{11,10},{13,12},{15,14},{17,16},{19,... | collective-permute-start | bytes 39944 | tf_op jit(solution)/shard_map/ppermute | solution.py:17
  89.3 5.8 %collective-permute-start.26 = (f32[26,1,128]{2,0,1:T(8,128)S(1)}, f32[26,1,128]{2,0,1:T(8,128)S(1)}, u32[]{:S(2)}, u32[]{:S(2)}) collective-permute-start(f32[26,1,128]{2,0,1:T(8,128)S(1)} %get-tuple-element.204), channel_id=1, source_target_pairs={{0,1},{2,3},{4,5},{6,7},{8,9},{10,11},{12,13},{14,15},{16,17},{18,... | collective-permute-start | bytes 39944 | tf_op jit(solution)/shard_map/ppermute | solution.py:16
  98.2 11.1 %collective-permute-start.49 = (f32[26,1,128]{2,0,1:T(8,128)S(1)}, f32[26,1,128]{2,0,1:T(8,128)S(1)}, u32[]{:S(2)}, u32[]{:S(2)}) collective-permute-start(f32[26,1,128]{2,0,1:T(8,128)S(1)} %get-tuple-element.193), channel_id=1, source_target_pairs={{0,1},{2,3},{4,5},{6,7},{8,9},{10,11},{12,13},{14,15},{16,17},{18,... | collective-permute-start | bytes 39944 | tf_op jit(solution)/shard_map/ppermute | solution.py:16
  99.5 9.8 %collective-permute-start.50 = (f32[26,1,128]{2,0,1:T(8,128)S(1)}, f32[26,1,128]{2,0,1:T(8,128)S(1)}, u32[]{:S(2)}, u32[]{:S(2)}) collective-permute-start(f32[26,1,128]{2,0,1:T(8,128)S(1)} %get-tuple-element.194), channel_id=1, source_target_pairs={{1,0},{3,2},{5,4},{7,6},{9,8},{11,10},{13,12},{15,14},{17,16},{19,... | collective-permute-start | bytes 39944 | tf_op jit(solution)/shard_map/ppermute | solution.py:17
  104.0 8.4 %collective-permute-start.27 = (f32[1,16,128]{2,0,1:T(1,128)S(1)}, f32[1,16,128]{2,0,1:T(1,128)S(1)}, u32[]{:S(2)}, u32[]{:S(2)}) collective-permute-start(f32[1,16,128]{2,0,1:T(1,128)S(1)} %get-tuple-element.238), channel_id=1, source_target_pairs={{2,0},{3,1},{6,4},{7,5},{10,8},{11,9},{14,12},{15,13},{18,16},{19,... | collective-permute-start | bytes 24584 | tf_op jit(solution)/shard_map/ppermute | solution.py:17
  105.3 7.2 %collective-permute-start.28 = (f32[1,16,128]{2,0,1:T(1,128)S(1)}, f32[1,16,128]{2,0,1:T(1,128)S(1)}, u32[]{:S(2)}, u32[]{:S(2)}) collective-permute-start(f32[1,16,128]{2,0,1:T(1,128)S(1)} %get-tuple-element.237), channel_id=1, source_target_pairs={{0,2},{1,3},{4,6},{5,7},{8,10},{9,11},{12,14},{13,15},{16,18},{17,... | collective-permute-start | bytes 24584 | tf_op jit(solution)/shard_map/ppermute | solution.py:16
  109.8 5.8 %collective-permute-start.51 = (f32[1,16,128]{2,0,1:T(1,128)S(1)}, f32[1,16,128]{2,0,1:T(1,128)S(1)}, u32[]{:S(2)}, u32[]{:S(2)}) collective-permute-start(f32[1,16,128]{2,0,1:T(1,128)S(1)} %get-tuple-element.225), channel_id=1, source_target_pairs={{0,2},{1,3},{4,6},{5,7},{8,10},{9,11},{12,14},{13,15},{16,18},{17,... | collective-permute-start | bytes 24584 | tf_op jit(solution)/shard_map/ppermute | solution.py:16
  112.4 7.5 %collective-permute-start.29 = (f32[26,1,128]{2,0,1:T(8,128)S(1)}, f32[26,1,128]{2,0,1:T(8,128)S(1)}, u32[]{:S(2)}, u32[]{:S(2)}) collective-permute-start(f32[26,1,128]{2,0,1:T(8,128)S(1)} %get-tuple-element.201), channel_id=1, source_target_pairs={{1,0},{3,2},{5,4},{7,6},{9,8},{11,10},{13,12},{15,14},{17,16},{19,... | collective-permute-start | bytes 39944 | tf_op jit(solution)/shard_map/ppermute | solution.py:17
  114.3 5.7 %collective-permute-start.30 = (f32[26,1,128]{2,0,1:T(8,128)S(1)}, f32[26,1,128]{2,0,1:T(8,128)S(1)}, u32[]{:S(2)}, u32[]{:S(2)}) collective-permute-start(f32[26,1,128]{2,0,1:T(8,128)S(1)} %get-tuple-element.202), channel_id=1, source_target_pairs={{0,1},{2,3},{4,5},{6,7},{8,9},{10,11},{12,13},{14,15},{16,17},{18,... | collective-permute-start | bytes 39944 | tf_op jit(solution)/shard_map/ppermute | solution.py:16
  121.3 10.9 %collective-permute-start.55 = (f32[1,16,128]{2,0,1:T(1,128)S(1)}, f32[1,16,128]{2,0,1:T(1,128)S(1)}, u32[]{:S(2)}, u32[]{:S(2)}) collective-permute-start(f32[1,16,128]{2,0,1:T(1,128)S(1)} %get-tuple-element.223), channel_id=1, source_target_pairs={{0,2},{1,3},{4,6},{5,7},{8,10},{9,11},{12,14},{13,15},{16,18},{17,... | collective-permute-start | bytes 24584 | tf_op jit(solution)/shard_map/ppermute | solution.py:16
  125.6 6.6 %collective-permute-start.56 = (f32[1,16,128]{2,0,1:T(1,128)S(1)}, f32[1,16,128]{2,0,1:T(1,128)S(1)}, u32[]{:S(2)}, u32[]{:S(2)}) collective-permute-start(f32[1,16,128]{2,0,1:T(1,128)S(1)} %get-tuple-element.224), channel_id=1, source_target_pairs={{2,0},{3,1},{6,4},{7,5},{10,8},{11,9},{14,12},{15,13},{18,16},{19,... | collective-permute-start | bytes 24584 | tf_op jit(solution)/shard_map/ppermute | solution.py:17
  126.9 9.7 %collective-permute-start.31 = (f32[1,16,128]{2,0,1:T(1,128)S(1)}, f32[1,16,128]{2,0,1:T(1,128)S(1)}, u32[]{:S(2)}, u32[]{:S(2)}) collective-permute-start(f32[1,16,128]{2,0,1:T(1,128)S(1)} %get-tuple-element.236), channel_id=1, source_target_pairs={{2,0},{3,1},{6,4},{7,5},{10,8},{11,9},{14,12},{15,13},{18,16},{19,... | collective-permute-start | bytes 24584 | tf_op jit(solution)/shard_map/ppermute | solution.py:17
  128.2 8.4 %collective-permute-start.32 = (f32[1,16,128]{2,0,1:T(1,128)S(1)}, f32[1,16,128]{2,0,1:T(1,128)S(1)}, u32[]{:S(2)}, u32[]{:S(2)}) collective-permute-start(f32[1,16,128]{2,0,1:T(1,128)S(1)} %get-tuple-element.235), channel_id=1, source_target_pairs={{0,2},{1,3},{4,6},{5,7},{8,10},{9,11},{12,14},{13,15},{16,18},{17,... | collective-permute-start | bytes 24584 | tf_op jit(solution)/shard_map/ppermute | solution.py:16
  132.3 7.0 %collective-permute-start.57 = (f32[26,1,128]{2,0,1:T(8,128)S(1)}, f32[26,1,128]{2,0,1:T(8,128)S(1)}, u32[]{:S(2)}, u32[]{:S(2)}) collective-permute-start(f32[26,1,128]{2,0,1:T(8,128)S(1)} %get-tuple-element.189), channel_id=1, source_target_pairs={{0,1},{2,3},{4,5},{6,7},{8,9},{10,11},{12,13},{14,15},{16,17},{18,... | collective-permute-start | bytes 39944 | tf_op jit(solution)/shard_map/ppermute | solution.py:16
  133.6 5.7 %collective-permute-start.58 = (f32[26,1,128]{2,0,1:T(8,128)S(1)}, f32[26,1,128]{2,0,1:T(8,128)S(1)}, u32[]{:S(2)}, u32[]{:S(2)}) collective-permute-start(f32[26,1,128]{2,0,1:T(8,128)S(1)} %get-tuple-element.190), channel_id=1, source_target_pairs={{1,0},{3,2},{5,4},{7,6},{9,8},{11,10},{13,12},{15,14},{17,16},{19,... | collective-permute-start | bytes 39944 | tf_op jit(solution)/shard_map/ppermute | solution.py:17
  136.7 7.1 %collective-permute-start.33 = (f32[26,1,128]{2,0,1:T(8,128)S(1)}, f32[26,1,128]{2,0,1:T(8,128)S(1)}, u32[]{:S(2)}, u32[]{:S(2)}) collective-permute-start(f32[26,1,128]{2,0,1:T(8,128)S(1)} %get-tuple-element.199), channel_id=1, source_target_pairs={{1,0},{3,2},{5,4},{7,6},{9,8},{11,10},{13,12},{15,14},{17,16},{19,... | collective-permute-start | bytes 39944 | tf_op jit(solution)/shard_map/ppermute | solution.py:17
  138.0 5.8 %collective-permute-start.34 = (f32[26,1,128]{2,0,1:T(8,128)S(1)}, f32[26,1,128]{2,0,1:T(8,128)S(1)}, u32[]{:S(2)}, u32[]{:S(2)}) collective-permute-start(f32[26,1,128]{2,0,1:T(8,128)S(1)} %get-tuple-element.200), channel_id=1, source_target_pairs={{0,1},{2,3},{4,5},{6,7},{8,9},{10,11},{12,13},{14,15},{16,17},{18,... | collective-permute-start | bytes 39944 | tf_op jit(solution)/shard_map/ppermute | solution.py:16
  146.9 7.0 %collective-permute-start.61 = (f32[26,1,128]{2,0,1:T(8,128)S(1)}, f32[26,1,128]{2,0,1:T(8,128)S(1)}, u32[]{:S(2)}, u32[]{:S(2)}) collective-permute-start(f32[26,1,128]{2,0,1:T(8,128)S(1)} %get-tuple-element.187), channel_id=1, source_target_pairs={{0,1},{2,3},{4,5},{6,7},{8,9},{10,11},{12,13},{14,15},{16,17},{18,... | collective-permute-start | bytes 39944 | tf_op jit(solution)/shard_map/ppermute | solution.py:16
  148.2 5.7 %collective-permute-start.62 = (f32[26,1,128]{2,0,1:T(8,128)S(1)}, f32[26,1,128]{2,0,1:T(8,128)S(1)}, u32[]{:S(2)}, u32[]{:S(2)}) collective-permute-start(f32[26,1,128]{2,0,1:T(8,128)S(1)} %get-tuple-element.188), channel_id=1, source_target_pairs={{1,0},{3,2},{5,4},{7,6},{9,8},{11,10},{13,12},{15,14},{17,16},{19,... | collective-permute-start | bytes 39944 | tf_op jit(solution)/shard_map/ppermute | solution.py:17
  155.2 71.0 %collective-permute-start.63 = (f32[24,16,128]{2,0,1:T(8,128)}, f32[24,16,128]{2,0,1:T(8,128)}, u32[]{:S(2)}, u32[]{:S(2)}) collective-permute-start(f32[24,16,128]{2,0,1:T(8,128)} %fusion.55), channel_id=1, source_target_pairs={{4,0},{8,4},{12,8},{5,1},{9,5},{13,9},{6,2},{10,6},{14,10},{7,3},{... | collective-permute-start | bytes 589832 | tf_op jit(solution)/shard_map/ppermute | solution.py:25
  169.8 8.2 %collective-permute-start.4 = (f32[24,16,128]{2,1,0:T(8,128)}, f32[24,16,128]{2,1,0:T(8,128)S(1)}, u32[]{:S(2)}, u32[]{:S(2)}) collective-permute-start(f32[24,16,128]{2,1,0:T(8,128)} %fusion.162), channel_id=1, source_target_pairs={{0,4},{4,8},{8,12},{1,5},{5,9},{9,13},{2,6},{6,10},{10,14},{3,7},{... | collective-permute-start | bytes 589832 | tf_op jit(solution)/shard_map/while/body/eval_jaxpr/ppermute | solution.py:25
  185.5 5.8 %collective-permute-start.2 = (f32[26,1,128]{2,1,0:T(1,128)S(1)}, f32[26,1,128]{2,1,0:T(1,128)S(1)}, u32[]{:S(2)}, u32[]{:S(2)}) collective-permute-start(f32[26,1,128]{2,1,0:T(1,128)S(1)} %get-tuple-element.305), channel_id=1, source_target_pairs={{0,1},{2,3},{4,5},{6,7},{8,9},{10,11},{12,13},{14,15},{16,17},{18,... | collective-permute-start | bytes 39944 | tf_op jit(solution)/shard_map/while/body/eval_jaxpr/ppermute | solution.py:16
  193.0 8.2 %collective-permute-start.4 = (f32[24,16,128]{2,1,0:T(8,128)}, f32[24,16,128]{2,1,0:T(8,128)S(1)}, u32[]{:S(2)}, u32[]{:S(2)}) collective-permute-start(f32[24,16,128]{2,1,0:T(8,128)} %fusion.162), channel_id=1, source_target_pairs={{0,4},{4,8},{8,12},{1,5},{5,9},{9,13},{2,6},{6,10},{10,14},{3,7},{... | collective-permute-start | bytes 589832 | tf_op jit(solution)/shard_map/while/body/eval_jaxpr/ppermute | solution.py:25
  208.7 5.8 %collective-permute-start.2 = (f32[26,1,128]{2,1,0:T(1,128)S(1)}, f32[26,1,128]{2,1,0:T(1,128)S(1)}, u32[]{:S(2)}, u32[]{:S(2)}) collective-permute-start(f32[26,1,128]{2,1,0:T(1,128)S(1)} %get-tuple-element.305), channel_id=1, source_target_pairs={{0,1},{2,3},{4,5},{6,7},{8,9},{10,11},{12,13},{14,15},{16,17},{18,... | collective-permute-start | bytes 39944 | tf_op jit(solution)/shard_map/while/body/eval_jaxpr/ppermute | solution.py:16
  216.3 8.2 %collective-permute-start.4 = (f32[24,16,128]{2,1,0:T(8,128)}, f32[24,16,128]{2,1,0:T(8,128)S(1)}, u32[]{:S(2)}, u32[]{:S(2)}) collective-permute-start(f32[24,16,128]{2,1,0:T(8,128)} %fusion.162), channel_id=1, source_target_pairs={{0,4},{4,8},{8,12},{1,5},{5,9},{9,13},{2,6},{6,10},{10,14},{3,7},{... | collective-permute-start | bytes 589832 | tf_op jit(solution)/shard_map/while/body/eval_jaxpr/ppermute | solution.py:25
  234.2 5.8 %collective-permute-start.7 = (f32[26,1,128]{2,1,0:T(1,128)S(1)}, f32[26,1,128]{2,1,0:T(1,128)S(1)}, u32[]{:S(2)}, u32[]{:S(2)}) collective-permute-start(f32[26,1,128]{2,1,0:T(1,128)S(1)} %get-tuple-element.313), channel_id=1, source_target_pairs={{1,0},{3,2},{5,4},{7,6},{9,8},{11,10},{13,12},{15,14},{17,16},{19,... | collective-permute-start | bytes 39944 | tf_op jit(solution)/shard_map/while/body/eval_jaxpr/ppermute | solution.py:17
  243.0 8.4 %collective-permute-start.9 = (f32[24,16,128]{2,1,0:T(8,128)}, f32[24,16,128]{2,1,0:T(8,128)S(1)}, u32[]{:S(2)}, u32[]{:S(2)}) collective-permute-start(f32[24,16,128]{2,1,0:T(8,128)} %fusion.165), channel_id=1, source_target_pairs={{4,0},{8,4},{12,8},{5,1},{9,5},{13,9},{6,2},{10,6},{14,10},{7,3},{... | collective-permute-start | bytes 589832 | tf_op jit(solution)/shard_map/while/body/eval_jaxpr/ppermute | solution.py:25
  258.9 5.6 %collective-permute-start.7 = (f32[26,1,128]{2,1,0:T(1,128)S(1)}, f32[26,1,128]{2,1,0:T(1,128)S(1)}, u32[]{:S(2)}, u32[]{:S(2)}) collective-permute-start(f32[26,1,128]{2,1,0:T(1,128)S(1)} %get-tuple-element.313), channel_id=1, source_target_pairs={{1,0},{3,2},{5,4},{7,6},{9,8},{11,10},{13,12},{15,14},{17,16},{19,... | collective-permute-start | bytes 39944 | tf_op jit(solution)/shard_map/while/body/eval_jaxpr/ppermute | solution.py:17
  267.4 8.4 %collective-permute-start.9 = (f32[24,16,128]{2,1,0:T(8,128)}, f32[24,16,128]{2,1,0:T(8,128)S(1)}, u32[]{:S(2)}, u32[]{:S(2)}) collective-permute-start(f32[24,16,128]{2,1,0:T(8,128)} %fusion.165), channel_id=1, source_target_pairs={{4,0},{8,4},{12,8},{5,1},{9,5},{13,9},{6,2},{10,6},{14,10},{7,3},{... | collective-permute-start | bytes 589832 | tf_op jit(solution)/shard_map/while/body/eval_jaxpr/ppermute | solution.py:25
  283.3 5.6 %collective-permute-start.7 = (f32[26,1,128]{2,1,0:T(1,128)S(1)}, f32[26,1,128]{2,1,0:T(1,128)S(1)}, u32[]{:S(2)}, u32[]{:S(2)}) collective-permute-start(f32[26,1,128]{2,1,0:T(1,128)S(1)} %get-tuple-element.313), channel_id=1, source_target_pairs={{1,0},{3,2},{5,4},{7,6},{9,8},{11,10},{13,12},{15,14},{17,16},{19,... | collective-permute-start | bytes 39944 | tf_op jit(solution)/shard_map/while/body/eval_jaxpr/ppermute | solution.py:17
  291.9 8.4 %collective-permute-start.9 = (f32[24,16,128]{2,1,0:T(8,128)}, f32[24,16,128]{2,1,0:T(8,128)S(1)}, u32[]{:S(2)}, u32[]{:S(2)}) collective-permute-start(f32[24,16,128]{2,1,0:T(8,128)} %fusion.165), channel_id=1, source_target_pairs={{4,0},{8,4},{12,8},{5,1},{9,5},{13,9},{6,2},{10,6},{14,10},{7,3},{... | collective-permute-start | bytes 589832 | tf_op jit(solution)/shard_map/while/body/eval_jaxpr/ppermute | solution.py:25
  308.9 5.6 %collective-permute-start.66 = (f32[26,1,128]{2,0,1:T(8,128)S(1)}, f32[26,1,128]{2,0,1:T(8,128)S(1)}, u32[]{:S(2)}, u32[]{:S(2)}) collective-permute-start(f32[26,1,128]{2,0,1:T(8,128)S(1)} %get-tuple-element.185), channel_id=1, source_target_pairs={{0,1},{2,3},{4,5},{6,7},{8,9},{10,11},{12,13},{14,15},{16,17},{18,... | collective-permute-start | bytes 39944 | tf_op jit(solution)/shard_map/ppermute | solution.py:16
  358.0 5.7 %collective-permute-start.82 = (f32[26,1,128]{2,0,1:T(8,128)S(1)}, f32[26,1,128]{2,0,1:T(8,128)S(1)}, u32[]{:S(2)}, u32[]{:S(2)}) collective-permute-start(f32[26,1,128]{2,0,1:T(8,128)S(1)} %get-tuple-element.177), channel_id=1, source_target_pairs={{0,1},{2,3},{4,5},{6,7},{8,9},{10,11},{12,13},{14,15},{16,17},{18,... | collective-permute-start | bytes 39944 | tf_op jit(solution)/shard_map/ppermute | solution.py:16
  (74 other events, 409.4 us)
where the time goes:
time: 368 us; the launch traced here: 365 us
  starting transfers between devices  226 us (61%)
  waiting for transfers between devices  97.8 us (27%)
  other arithmetic  28.3 us (8%)
  local copies, waits for them, and re-layouts  10 us (3%)
    ppermute x48, starting transfers between devices, extended(): after = lax.ppermute(first, axis, down)  114 us
    ppermute x48, starting transfers between devices, extended(): before = lax.ppermute(last, axis, up)  89.8 us
    ppermute x48, waiting for transfers between devices, extended(): after = lax.ppermute(first, axis, down)  50.6 us
    ppermute x8, waiting for transfers between devices, passed_along(): return lax.ppermute(block, axis, route)  37.7 us
    ppermute x8, starting transfers between devices, passed_along(): return lax.ppermute(block, axis, route)  22.2 us
    ppermute x48, waiting for transfers between devices, extended(): before = lax.ppermute(last, axis, up)  9.49 us
  transfers between devices with their start and end apart: 104, of which 40 were waited for; matrix products, arithmetic and copies ran while one was open for 4% of the time, Pallas kernels for 0%

commit v1 on v0

--- a/solution.py
+++ b/solution.py
@@ -1,9 +1,22 @@
+import functools
+
 import jax
 import jax.numpy as jnp
 from jax import lax
+from jax.experimental import pallas as pl
+from jax.experimental.pallas import tpu as pltpu
 from jax.sharding import PartitionSpec as P
 
 STEPS = 6
+BLOCK = 4
+EDGE = 8
+COEF = 9
+LATE = 5
+MSG = 7
+FAR_X = 10
+FAR_E = 7
+RIMS = (COEF, COEF, COEF, COEF, 6, 6, 7, 1)
+STARTS = tuple(sum(RIMS[:i]) for i in range(len(RIMS)))
 
 
 def extended(array, sides, width):
@@ -76,15 +89,6 @@
     return extended(field, (("space", 0), ("yz", 1)), 1)
 
 
-def coefficient_window(rim_coefficients, offset):
-    return rim_coefficients[
-        :,
-        offset : rim_coefficients.shape[1] - offset,
-        offset : rim_coefficients.shape[2] - offset,
-        :,
-    ]
-
-
 def coarse_chain(residual, near_coefficients, adjoint, direction):
     factor = float(STEPS)
 
@@ -96,14 +100,12 @@
     return lax.fori_loop(0, lax.axis_size("tm") - 1, one_turn, residual)
 
 
-def local(initial, diffusion, velocity, control, target, state_guess, adjoint_guess):
-    rim_depth = max(lax.axis_size("tm") // 2, STEPS)
+def any_mesh(initial, diffusion, velocity, control, target, state_guess, adjoint_guess):
     source = control[0]
     guess_state = state_guess[0]
     guess_adjoint = adjoint_guess[0]
     stacked = jnp.concatenate([diffusion[None], velocity, jnp.ones_like(diffusion)[None]], 0)
-    rim_coefficients = extended(stacked, (("space", 1), ("yz", 2)), rim_depth)
-    near_coefficients = coefficient_window(rim_coefficients, rim_depth - 1)
+    near_coefficients = extended(stacked, (("space", 1), ("yz", 2)), 1)
     arrived = passed_along(guess_state, "tm", 1)
     fine = jnp.where(lax.axis_index("tm") == 0, initial, arrived)
     sweep = guess_adjoint
@@ -124,22 +126,480 @@
     return (state_new[None], gradient[None])
 
 
+def rolled(value, shift, axis):
+    return pltpu.roll(value, shift % value.shape[axis], axis)
+
+
+class Stencil:
+    NAMES = ("c0", "xp", "xm", "yp", "ym", "zp", "zm", "qyp", "qym", "qzp", "qzm")
+
+    def __init__(self, ref):
+        self.at = {name: ref.at[i] for i, name in enumerate(self.NAMES)}
+        self.ref = ref
+
+    def fill(self, rows, raw, space, core):
+        sign = (1 - 2 * space).astype(jnp.float32)
+
+        def one(r, carry):
+            d, u0, u1, u2 = raw(r)
+            u0 = u0 * sign
+            cell = lax.broadcasted_iota(jnp.int32, d.shape, 0)
+            depth = lax.broadcasted_iota(jnp.int32, d.shape, 1)
+            own = d.shape[0] - EDGE
+            top = (cell == own - 1) & (core == 1)
+            bottom = (cell == 0) & (core == 0)
+            last, first = depth == d.shape[1] - 1, depth == 0
+            zero = jnp.zeros_like(d)
+            values = {
+                "c0": 1.0 - 6.0 * d,
+                "xp": d - u0,
+                "xm": d + u0,
+                "yp": jnp.where(top, zero, d - u1),
+                "ym": jnp.where(bottom, zero, d + u1),
+                "zp": jnp.where(last, zero, d - u2),
+                "zm": jnp.where(first, zero, d + u2),
+                "qyp": jnp.where(top, zero, rolled(d + u1, -1, 0)),
+                "qym": jnp.where(bottom, zero, rolled(d - u1, 1, 0)),
+                "qzp": jnp.where(last, zero, rolled(d + u2, -1, 1)),
+                "qzm": jnp.where(first, zero, rolled(d - u2, 1, 1)),
+            }
+            for name in self.NAMES:
+                self.at[name][r + 1] = values[name]
+            return carry
+
+        for name in self.NAMES:
+            self.at[name][0] = jnp.zeros(self.ref.shape[2:], jnp.float32)
+        lax.fori_loop(0, rows, one, 0)
+
+    def both(self, v, start, adjoint):
+        here = pl.ds(start + 1, BLOCK)
+        at = self.at
+        c = v[1:-1]
+        if adjoint:
+            up, low = at["xm"][pl.ds(start + 2, BLOCK)], at["xp"][pl.ds(start, BLOCK)]
+            ends = [at[n][here] for n in ("qyp", "qym", "qzp", "qzm")]
+        else:
+            up, low = at["xp"][here], at["xm"][here]
+            ends = [at[n][here] for n in ("yp", "ym", "zp", "zm")]
+        around = up * v[2:] + low * v[:-2]
+        around = around + (ends[0] * rolled(c, -1, 1) + ends[1] * rolled(c, 1, 1))
+        around = around + (ends[2] * rolled(c, -1, 2) + ends[3] * rolled(c, 1, 2))
+        return around, at["c0"][here]
+
+    def fine(self, v, start, adjoint):
+        around, own = self.both(v, start, adjoint)
+        return own * v[1:-1] + around
+
+    def coarse(self, v, start, adjoint):
+        around, own = self.both(v, start, adjoint)
+        c = v[1:-1]
+        return c + float(STEPS) * (around + (own * c - c))
+
+
+def padded_rows(rows):
+    return -(-rows // BLOCK) * BLOCK + 2
+
+
+def blocks(rows, body):
+    def one(b, carry):
+        body(b * BLOCK)
+        return carry
+
+    lax.fori_loop(0, -(-rows // BLOCK), one, 0)
+
+
+def around_rows(ref, start):
+    return ref[pl.ds(start, BLOCK + 2)]
+
+
+def put(ref, start, value):
+    ref[pl.ds(start + 1, BLOCK)] = value
+
+
+def fine_kernel(rows, own, where_ref, d_ref, u_ref, control_ref, sg_ref, ag_ref, initial_ref, target_ref, xr_ref, ya_ref, yb_ref,
+                z_out, x_out, base_out, state_out, ext_out, coef, c_a, c_b, g_a, g_b, s_a, s_b, con, tar):
+    slab, space, core = where_ref[0], where_ref[1], where_ref[2]
+    flip = space == 1
+
+    def natural(r):
+        return jnp.where(flip, rows - 1 - r, r)
+
+    def mine(i, read, r):
+        at = natural(r)
+        return jnp.concatenate([read(at), ya_ref[i, at]], 0)
+
+    def rim(i, j):
+        at = STARTS[i] + jnp.where(flip, RIMS[i] - 1 - j, j)
+        return jnp.concatenate([xr_ref[at], yb_ref[at]], 0)
+
+    reads = (
+        lambda r: d_ref[r],
+        lambda r: u_ref[0, r],
+        lambda r: u_ref[1, r],
+        lambda r: u_ref[2, r],
+        lambda r: control_ref[0, r],
+        lambda r: sg_ref[0, r],
+    )
+    first = slab == 0
+
+    def load_own(r, carry):
+        for i in range(4):
+            ext_out[i, r] = mine(i, reads[i], r)
+        con[r + 1] = mine(4, reads[4], r)
+        g_a[r + 1] = mine(5, reads[5], r)
+        at = natural(r)
+        start = jnp.concatenate([initial_ref[at], ya_ref[6, at]], 0)
+        c_a[r + 1] = jnp.where(first, start, jnp.zeros_like(start))
+        s_a[r + 1] = jnp.concatenate([ag_ref[0, at], ya_ref[6, at]], 0)
+        tar[r + 1] = mine(7, lambda n: target_ref[0, n], r)
+        return carry
+
+    lax.fori_loop(0, rows, load_own, 0)
+    for j in range(COEF):
+        for i in range(4):
+            ext_out[i, rows + j] = rim(i, j)
+    for j in range(RIMS[4]):
+        con[rows + 1 + j] = rim(4, j)
+    for j in range(RIMS[5]):
+        g_a[rows + 1 + j] = rim(5, j)
+    for j in range(RIMS[6]):
+        start = rim(6, j)
+        c_a[rows + 1 + j] = jnp.where(first, start, jnp.zeros_like(start))
+        s_a[rows + 1 + j] = start
+    tar[rows + 1] = rim(7, 0)
+    zero_row = jnp.zeros(c_a.shape[1:], jnp.float32)
+    for ref in (c_a, c_b, g_a, g_b, s_a, s_b):
+        ref[0] = zero_row
+
+    stencil = Stencil(coef)
+    stencil.fill(rows + COEF, lambda r: [ext_out[i, r] for i in range(4)], space, core)
+
+    c, g, s = (c_a, c_b), (g_a, g_b), (s_a, s_b)
+    for step in range(STEPS):
+        now, later = step % 2, 1 - step % 2
+
+        def one(start, now=now, later=later):
+            put(c[later], start, stencil.fine(around_rows(c[now], start), start, False) + con[pl.ds(start + 1, BLOCK)])
+            put(g[later], start, stencil.fine(around_rows(g[now], start), start, False))
+            put(s[later], start, stencil.fine(around_rows(s[now], start), start, True))
+
+        blocks(rows + STEPS - step, one)
+    cc, dd = c_b, s_b
+
+    def differences(r, carry):
+        sg = mine(5, reads[5], r)
+        fine = c_a[r + 1]
+        gap = fine - sg
+        ag = jnp.concatenate([ag_ref[0, natural(r)], ya_ref[6, natural(r)]], 0)
+        state = sg + gap
+        rest = state - tar[r + 1] - ag
+        cc[r + 1] = gap
+        dd[r + 1] = rest
+        state_out[r] = state[:own]
+        base_out[r] = (ag + rest)[:own]
+        return carry
+
+    lax.fori_loop(0, rows, differences, 0)
+    sg = rim(5, 0)
+    gap = c_a[rows + 1] - sg
+    cc[rows + 1] = gap
+    dd[rows + 1] = (sg + gap) - tar[rows + 1] - rim(6, 0)
+
+    def pair(start):
+        x = g_a[pl.ds(start + 1, BLOCK)] + stencil.coarse(around_rows(cc, start), start, False)
+        e = s_a[pl.ds(start + 1, BLOCK)] + stencil.coarse(around_rows(dd, start), start, True)
+        z_out[pl.ds(start, BLOCK)] = x[:, :own]
+        z_out[pl.ds(rows + start, BLOCK)] = e[:, :own]
+
+    blocks(rows, pair)
+    for j in range(FAR_X):
+        x_out[j] = z_out[rows - 1 - j]
+    for j in range(FAR_E):
+        x_out[FAR_X + j] = z_out[2 * rows - 1 - j]
+    for j in range(LATE):
+        x_out[FAR_X + FAR_E + j] = base_out[rows - 1 - j]
+
+
+def pair_kernel(rows, own, where_ref, ext_ref, z_ref, x_ref, zr_ref, xr_ref, xzr_ref, ym_ref, yx_ref, yp_ref, yd_ref, base_ref, state_ref,
+                msg_out, base_out, state_out, coef, xa, xb, ea, eb, t0, t1, t2):
+    slab, space, core = where_ref[0], where_ref[1], where_ref[2]
+    odd = slab % 2 == 1
+    upper = slab >= 2
+    stencil = Stencil(coef)
+    stencil.fill(rows + COEF, lambda r: [ext_ref[i, r] for i in range(4)], space, core)
+
+    def gather(mine_ref, mine_y, other_ref, other_y, lower, upper_, at, to, count):
+        def one(r, carry):
+            mine = jnp.concatenate([mine_ref[at + r], mine_y[at + r]], 0)
+            other = jnp.concatenate([other_ref[at + r], other_y[at + r]], 0)
+            lower[to + r + 1] = jnp.where(odd, other, mine)
+            upper_[to + r + 1] = jnp.where(odd, mine, other)
+            return carry
+
+        lax.fori_loop(0, count, one, 0)
+
+    gather(z_ref, ym_ref, zr_ref, yp_ref, xa, xb, 0, 0, rows)
+    gather(z_ref, ym_ref, zr_ref, yp_ref, ea, eb, rows, 0, rows)
+    gather(xr_ref, yx_ref, xzr_ref, yd_ref, xa, xb, 0, rows, FAR_X)
+    gather(xr_ref, yx_ref, xzr_ref, yd_ref, ea, eb, FAR_X, rows, FAR_E)
+    zero_row = jnp.zeros(xa.shape[1:], jnp.float32)
+    for ref in (xa, xb, ea, eb, t0, t1, t2):
+        ref[0] = zero_row
+
+    def base_at(start):
+        return pl.ds(start, BLOCK)
+
+    for j in range(rows):
+        base_out[j] = base_ref[j]
+        state_out[j] = state_ref[j] + jnp.where(odd, xa[j + 1][:own], jnp.zeros_like(state_ref[j]))
+    for j in range(LATE):
+        base_out[rows + j] = xr_ref[FAR_X + FAR_E + j]
+
+    width = base_out.shape[0]
+
+    def add_base(value):
+        def one(r, carry):
+            base_out[r] = base_out[r] + value(r)[:own]
+            return carry
+
+        lax.fori_loop(0, rows + LATE, one, 0)
+
+    def send(value_ref):
+        def one(r, carry):
+            msg_out[r] = value_ref[r + 1][:own]
+            return carry
+
+        lax.fori_loop(0, rows + MSG, one, 0)
+
+    @pl.when(jnp.logical_not(upper))
+    def _():
+        def h(start):
+            put(t0, start, xb[pl.ds(start + 1, BLOCK)] + stencil.coarse(around_rows(xa, start), start, False))
+
+        blocks(rows + FAR_X - 1, h)
+        send(t0)
+
+        def ph(start):
+            put(t1, start, stencil.coarse(around_rows(t0, start), start, False))
+
+        blocks(rows + FAR_X - 2, ph)
+
+        def qph(start):
+            put(t2, start, t0[pl.ds(start + 1, BLOCK)] + stencil.coarse(around_rows(t1, start), start, True))
+
+        blocks(rows + FAR_X - 3, qph)
+
+        def nh(start):
+            put(t1, start, xa[pl.ds(start + 1, BLOCK)] + stencil.coarse(around_rows(t2, start), start, True))
+
+        blocks(rows + FAR_X - 4, nh)
+
+        @pl.when(odd)
+        def _():
+            add_base(lambda r: t1[r + 1])
+
+        @pl.when(jnp.logical_not(odd))
+        def _():
+            def q(start):
+                put(t2, start, eb[pl.ds(start + 1, BLOCK)] + stencil.coarse(around_rows(t1, start), start, True))
+
+            blocks(rows + LATE, q)
+            add_base(lambda r: t2[r + 1])
+
+    @pl.when(upper)
+    def _():
+        def q(start):
+            put(t0, start, eb[pl.ds(start + 1, BLOCK)] + stencil.coarse(around_rows(xa, start), start, True))
+
+        blocks(rows + FAR_E, q)
+
+        def qq(start):
+            put(t1, start, ea[pl.ds(start + 1, BLOCK)] + stencil.coarse(around_rows(t0, start), start, True))
+
+        blocks(rows + FAR_E - 1, qq)
+        send(t1)
+
+        @pl.when(odd)
+        def _():
+            add_base(lambda r: xa[r + 1])
+
+        @pl.when(jnp.logical_not(odd))
+        def _():
+            add_base(lambda r: t0[r + 1])
+
+
+def last_kernel(rows, own, where_ref, ext_ref, msg_ref, msg_y, base_ref, base_y, state_ref, control_ref,
+                state_out, gradient_out, coef, m, t0, t1, total):
+    slab, space, core = where_ref[0], where_ref[1], where_ref[2]
+    stencil = Stencil(coef)
+    stencil.fill(rows + MSG, lambda r: [ext_ref[i, r] for i in range(4)], space, core)
+
+    def load(r, carry):
+        m[r + 1] = jnp.concatenate([msg_ref[r], msg_y[r]], 0)
+        return carry
+
+    lax.fori_loop(0, rows + MSG, load, 0)
+    zero_row = jnp.zeros(m.shape[1:], jnp.float32)
+    for ref in (m, t0, t1):
+        ref[0] = zero_row
+
+    def moved(start):
+        put(t0, start, stencil.coarse(around_rows(m, start), start, False))
+
+    blocks(rows + MSG - 1, moved)
+
+    def state(r, carry):
+        at = jnp.where(space == 1, rows - 1 - r, r)
+        came = jnp.where(slab == 2, m[r + 1], jnp.where(slab == 3, t0[r + 1], zero_row))
+        state_out[0, at] = state_ref[r] + came[:own]
+        return carry
+
+    lax.fori_loop(0, rows, state, 0)
+
+    def source(r, carry):
+        m_row, t_row = m[r + 1], t0[r + 1]
+        total[r + 1] = jnp.where((slab == 1) | (slab == 2), m_row, jnp.where(slab == 3, t_row, zero_row))
+        t0[r + 1] = jnp.where(slab == 0, m_row, jnp.where(slab == 2, t_row, zero_row))
+        return carry
+
+    lax.fori_loop(0, rows + MSG - 1, source, 0)
+
+    def multiplier(start):
+        put(t1, start, total[pl.ds(start + 1, BLOCK)] + stencil.coarse(around_rows(t0, start), start, True))
+
+    blocks(rows + LATE, multiplier)
+
+    def add(r, carry):
+        value = t1[r + 1] + jnp.concatenate([base_ref[r], base_y[r]], 0)
+        t1[r + 1] = value
+        total[r + 1] = value
+        return carry
+
+    lax.fori_loop(0, rows + LATE, add, 0)
+
+    pair = (t1, t0)
+    for step in range(STEPS - 1):
+        now, later = pair[step % 2], pair[1 - step % 2]
+
+        def one(start, now=now, later=later):
+            value = stencil.fine(around_rows(now, start), start, True)
+            put(later, start, value)
+            put(total, start, total[pl.ds(start + 1, BLOCK)] + value)
+
+        blocks(rows + LATE - 1 - step, one)
+
+    def out(r, carry):
+        at = jnp.where(space == 1, rows - 1 - r, r)
+        gradient_out[0, at] = total[r + 1][:own] / float(STEPS) + 0.5 * control_ref[0, at]
+        return carry
+
+    lax.fori_loop(0, rows, out, 0)
+
+
+def whole(count):
+    return [pl.BlockSpec(memory_space=pltpu.VMEM)] * count
+
+
+def call(kernel, outs, scratch, cost, *args):
+    return pl.pallas_call(
+        kernel,
+        out_shape=[jax.ShapeDtypeStruct(shape, jnp.float32) for shape in outs],
+        in_specs=[pl.BlockSpec(memory_space=pltpu.SMEM)] + whole(len(args) - 1),
+        out_specs=whole(len(outs)),
+        scratch_shapes=[pltpu.VMEM(shape, jnp.float32) for shape in scratch],
+        compiler_params=pltpu.CompilerParams(vmem_limit_bytes=48 * 1024 * 1024),
+        cost_estimate=pl.CostEstimate(flops=cost, bytes_accessed=4000000, transcendentals=0),
+    )(*args)
+
+
+def swapped(block, axis):
+    return lax.ppermute(block, axis, [(0, 1), (1, 0)])
+
+
+def across(block, distance):
+    return lax.ppermute(block, "tm", [(i, i ^ distance) for i in range(4)])
+
+
+def across_turned(block, distance):
+    route = [(2 * i + j, 2 * (i ^ distance) + 1 - j) for i in range(4) for j in range(2)]
+    return lax.ppermute(block, ("tm", "space"), route)
+
+
+def four_slabs(initial, diffusion, velocity, control, target, state_guess, adjoint_guess):
+    rows, own, depth = diffusion.shape
+    wide = own + EDGE
+    slab, space, core = lax.axis_index("tm"), lax.axis_index("space"), lax.axis_index("yz")
+    where = jnp.stack([slab, space, core]).astype(jnp.int32)
+    start = jnp.where(slab == 0, initial, adjoint_guess[0])
+    fields = (diffusion, velocity[0], velocity[1], velocity[2], control[0], state_guess[0], start, target[0])
+
+    def edge(block):
+        return lax.dynamic_slice_in_dim(block, jnp.where(core == 0, own - EDGE, 0), EDGE, axis=block.ndim - 2)
+
+    x_send = jnp.concatenate(
+        [lax.dynamic_slice_in_dim(f, jnp.where(space == 0, rows - n, 0), n, axis=0) for f, n in zip(fields, RIMS)], 0
+    )
+    x_here = swapped(x_send, "space")
+    y_a = swapped(jnp.stack([edge(f) for f in fields]), "yz")
+    y_b = swapped(edge(x_here), "yz")
+
+    tall = padded_rows(rows + COEF + 3)
+    field = (tall, wide, depth)
+    coefs = (len(Stencil.NAMES), *field)
+    z_out, x_out, base, state, ext = call(
+        functools.partial(fine_kernel, rows, own),
+        [
+            (2 * rows, own, depth),
+            (FAR_X + FAR_E + LATE, own, depth),
+            (rows, own, depth),
+            (rows, own, depth),
+            (4, rows + COEF, wide, depth),
+        ],
+        [coefs] + [field] * 8,
+        20000000,
+        where, diffusion, velocity, control, state_guess, adjoint_guess, initial, target, x_here, y_a, y_b,
+    )
+    far = FAR_X + FAR_E
+    z_in = across(z_out, 1)
+    x_in = swapped(x_out, "space")
+    xz_in = across_turned(x_out[:far], 1)
+    y_all = swapped(edge(jnp.concatenate([z_out, z_in, x_in[:far], xz_in], 0)), "yz")
+    two = 2 * rows
+    msg, base, state = call(
+        functools.partial(pair_kernel, rows, own),
+        [(rows + MSG, own, depth), (rows + LATE, own, depth), (rows, own, depth)],
+        [coefs] + [field] * 7,
+        8000000,
+        where, ext, z_out, x_out, z_in, x_in, xz_in,
+        y_all[:two], y_all[2 * two : 2 * two + far], y_all[two : 2 * two], y_all[2 * two + far :], base, state,
+    )
+    msg_in = across(msg, 2)
+    y_last = swapped(edge(jnp.concatenate([msg_in, base], 0)), "yz")
+    state_new, gradient = call(
+        functools.partial(last_kernel, rows, own),
+        [(1, rows, own, depth), (1, rows, own, depth)],
+        [coefs] + [field] * 4,
+        7000000,
+        where, ext, msg_in, y_last[: rows + MSG], base, y_last[rows + MSG :], state, control,
+    )
+    return state_new, gradient
+
+
 def solution(mesh):
+    sizes = mesh.shape
+
+    def local(*args):
+        rows, own, depth = args[1].shape
+        fits = (sizes["tm"], sizes["space"], sizes["yz"]) == (4, 2, 2)
+        fits = fits and rows >= FAR_X and rows % BLOCK == 0 and own % 8 == 0 and own >= EDGE and depth % 128 == 0
+        return four_slabs(*args) if fits else any_mesh(*args)
+
+    field = P(("groups", "space"), "yz", None)
+    slabs = P("tm", ("groups", "space"), "yz", None)
     return jax.shard_map(
         local,
         mesh=mesh,
-        in_specs=(
-            P(("groups", "space"), "yz", None),
-            P(("groups", "space"), "yz", None),
-            P(None, ("groups", "space"), "yz", None),
-            P("tm", ("groups", "space"), "yz", None),
-            P("tm", ("groups", "space"), "yz", None),
-            P("tm", ("groups", "space"), "yz", None),
-            P("tm", ("groups", "space"), "yz", None),
-        ),
-        out_specs=(
-            P("tm", ("groups", "space"), "yz", None),
-            P("tm", ("groups", "space"), "yz", None),
-        ),
+        in_specs=(field, field, P(None, ("groups", "space"), "yz", None), slabs, slabs, slabs, slabs),
+        out_specs=(slabs, slabs),
         check_vma=False,
     )

time: 368 us -> 80.3 us (0.22)
  the two profiles are of different devices: /device:TPU:17 before, /device:TPU:0 now
where the time goes in v1:
time: 80.3 us; the launch traced here: 80.2 us
  waiting for transfers between devices  41.2 us (51%)
  Pallas kernels  29.1 us (36%)
  starting transfers between devices  7.07 us (9%)
  local copies, waits for them, and re-layouts  1.66 us (2%)
  between operations  0.97 us (1%)
    pallas_call x3, Pallas kernels, call(): pl.pallas_call(kernel, out_shape=[jax.ShapeDtypeStruct(shape, jnp.float32...  29.1 us
    ppermute x6, waiting for transfers between devices, swapped(): return lax.ppermute(block, axis, [(0, 1), (1, 0)])  19.6 us
    ppermute x2, waiting for transfers between devices, across(): return lax.ppermute(block, 'tm', [(i, i ^ distance) for i in range(4)])  14.4 us
    ppermute x1, waiting for transfers between devices, across_turned(): return lax.ppermute(block, ('tm', 'space'), route)  7.17 us
    ppermute x6, starting transfers between devices, swapped(): return lax.ppermute(block, axis, [(0, 1), (1, 0)])  4.78 us
    ppermute x2, starting transfers between devices, across(): return lax.ppermute(block, 'tm', [(i, i ^ distance) for i in range(4)])  2.06 us
  transfers between devices with their start and end apart: 9, of which 7 were waited for; matrix products, arithmetic and copies ran while one was open for 0% of the time, Pallas kernels for 0%

profile of v1, /device:TPU:0, one launch (start us, length us, event | category | flops | bytes accessed | tf_op | source)
XLA Modules:
  0.0 80.2 jit_solution(15586366927768026088)
XLA Ops:
  0.6 0.0 copy-start.4
  0.6 0.0 copy-start.1
  0.7 0.0 copy-start.5
  0.7 0.0 copy-start.2
  0.7 0.0 copy-start.3
  0.7 0.0 copy-start.6
  0.7 1.3 %fusion.4 = (f32[1,24,16,128]{3,2,1,0:T(8,128)S(1)}, f32[1,24,16,128]{3,2,1,0:T(8,128)S(1)}, f32[1,24,16,128]{3,2,1,0:T(8,128)S(1)}) fusion(f32[3,24,16,128]{3,2,1,0:T(8,128)} %u_ref.1), kind=kLoop, calls=%fused_computation.29 | loop fusion | bytes 1179648 | tf_op jit(solution)/shard_map/slice | solution.py:534
  2.0 0.0 copy-done.4
  2.1 0.0 copy-done.1
  2.1 0.0 copy-done.5
  2.2 0.0 copy-done.2
  2.2 0.0 copy-done.3
  2.2 0.0 copy-start
  2.3 0.0 copy-done.6
  2.3 3.0 %collective-permute-start = (f32[56,16,128]{2,1,0:T(8,128)S(1)}, f32[56,16,128]{2,1,0:T(8,128)S(1)}, u32[]{:S(2)}, u32[]{:S(2)}) collective-permute-start(f32[56,16,128]{2,1,0:T(8,128)S(1)} %constant_dynamic-update-slice_fusion), channel_id=1, source_target_pairs={{0,2},{2,0},{1,3},{3,1},{4,6},{6,4},{5,7},{7,5},{8,10},{10,8},{9,1... | collective-permute-start | bytes 1376264 | tf_op jit(solution)/shard_map/ppermute | solution.py:516
  5.5 0.1 collective-permute-start.1
  5.5 10.3 %collective-permute-done.xr_ref = f32[56,16,128]{2,1,0:T(8,128)S(1)} collective-permute-done((f32[56,16,128]{2,1,0:T(8,128)S(1)}, f32[56,16,128]{2,1,0:T(8,128)S(1)}, u32[]{:S(2)}, u32[]{:S(2)}) %collective-permute-start) | collective-permute-done | bytes 458784 | tf_op jit(solution)/shard_map/ppermute | solution.py:516
  15.8 0.1 collective-permute-start.2
  15.9 0.1 pad_add_fusion.where_ref
  16.0 1.4 %collective-permute-done.2.yb_ref = f32[56,8,128]{2,1,0:T(8,128)S(1)} collective-permute-done((f32[56,8,128]{2,1,0:T(8,128)S(1)}, f32[56,8,128]{2,1,0:T(8,128)S(1)}, u32[]{:S(2)}, u32[]{:S(2)}) %collective-permute-start.2) | collective-permute-done | bytes 229408 | tf_op jit(solution)/shard_map/ppermute | solution.py:516
  17.4 0.0 collective-permute-done.1.ya_ref
  17.4 0.0 copy-done
  17.4 11.1 %shard_map.86 = (f32[48,16,128]{2,1,0:T(8,128)S(1)}, f32[22,16,128]{2,1,0:T(8,128)S(1)}, f32[24,16,128]{2,1,0:T(8,128)S(1)}, f32[24,16,128]{2,1,0:T(8,128)S(1)}, f32[4,33,24,128]{3,2,1,0:T(8,128)S(1)}) custom-call(s32[3]{0:T(128)S(1)} %pad_add_fusion.where_ref, f32[24,16,128]{2,1,0:T(8,128)S(1)} %copy-done.4, f32[3,24,16,128]{3,2,1,0:T(8,128)S(1)} %copy-done, ...), custom_call_target="tpu_custom_call" | custom-call | flops 20000000 | bytes 4000000 | tf_op jit(solution)/shard_map/pallas_call | solution.py:504
  28.5 1.9 %collective-permute-start.3 = (f32[48,16,128]{2,1,0:T(8,128)S(1)}, f32[48,16,128]{2,1,0:T(8,128)S(1)}, u32[]{:S(2)}, u32[]{:S(2)}) collective-permute-start(f32[48,16,128]{2,1,0:T(8,128)S(1)} %get-tuple-element.11.z_ref), channel_id=1, source_target_pairs={{0,4},{4,0},{8,12},{12,8},{1,5},{5,1},{9,13},{13,9},{2,6},{6,2},{1... | collective-permute-start | bytes 1179656 | tf_op jit(solution)/shard_map/ppermute | solution.py:520
  30.4 1.5 %collective-permute-start.4 = (f32[22,16,128]{2,1,0:T(8,128)S(1)}, f32[22,16,128]{2,1,0:T(8,128)S(1)}, u32[]{:S(2)}, u32[]{:S(2)}) collective-permute-start(f32[22,16,128]{2,1,0:T(8,128)S(1)} %get-tuple-element.12.x_ref), channel_id=1, source_target_pairs={{0,2},{2,0},{1,3},{3,1},{4,6},{6,4},{5,7},{7,5},{8,10},{10,8},{9,1... | collective-permute-start | bytes 540680 | tf_op jit(solution)/shard_map/ppermute | solution.py:516
  31.9 0.2 collective-permute-start.5
  32.1 4.6 %collective-permute-done.4.xr_ref = f32[22,16,128]{2,1,0:T(8,128)S(1)} collective-permute-done((f32[22,16,128]{2,1,0:T(8,128)S(1)}, f32[22,16,128]{2,1,0:T(8,128)S(1)}, u32[]{:S(2)}, u32[]{:S(2)}) %collective-permute-start.4) | collective-permute-done | bytes 180256 | tf_op jit(solution)/shard_map/ppermute | solution.py:516
  36.7 7.2 %collective-permute-done.5.xzr_ref = f32[17,16,128]{2,1,0:T(8,128)S(1)} collective-permute-done((f32[17,16,128]{2,1,0:T(8,128)S(1)}, f32[17,16,128]{2,1,0:T(8,128)S(1)}, u32[]{:S(2)}, u32[]{:S(2)}) %collective-permute-start.5) | collective-permute-done | bytes 139296 | tf_op jit(solution)/shard_map/ppermute | solution.py:525
  43.9 0.0 collective-permute-done.3.zr_ref
  43.9 0.1 collective-permute-start.6
  44.0 1.9 %collective-permute-done.6 = f32[130,8,128]{2,1,0:T(8,128)S(1)} collective-permute-done((f32[130,8,128]{2,1,0:T(8,128)S(1)}, f32[130,8,128]{2,1,0:T(8,128)S(1)}, u32[]{:S(2)}, u32[]{:S(2)}) %collective-permute-start.6) | collective-permute-done | bytes 532512 | tf_op jit(solution)/shard_map/ppermute | solution.py:516
  45.9 8.2 %shard_map.87 = (f32[31,16,128]{2,1,0:T(8,128)S(1)}, f32[29,16,128]{2,1,0:T(8,128)S(1)}, f32[24,16,128]{2,1,0:T(8,128)S(1)}) custom-call(s32[3]{0:T(128)S(1)} %pad_add_fusion.where_ref, f32[4,33,24,128]{3,2,1,0:T(8,128)S(1)} %get-tuple-element.10.ext_ref, f32[48,16,128]{2,1,0:T(8,128)S(1)} %get-tuple-element.11.z_ref, ...), custom_call_target="tpu_custom_call" | custom-call | flops 8000000 | bytes 4000000 | tf_op jit(solution)/shard_map/pallas_call | solution.py:504
  54.2 0.2 collective-permute-start.7
  54.3 14.4 %collective-permute-done.7.msg_ref = f32[31,16,128]{2,1,0:T(8,128)S(1)} collective-permute-done((f32[31,16,128]{2,1,0:T(8,128)S(1)}, f32[31,16,128]{2,1,0:T(8,128)S(1)}, u32[]{:S(2)}, u32[]{:S(2)}) %collective-permute-start.7) | collective-permute-done | bytes 253984 | tf_op jit(solution)/shard_map/ppermute | solution.py:520
  68.8 0.1 collective-permute-start.8
  68.8 1.5 %collective-permute-done.8 = f32[60,8,128]{2,1,0:T(8,128)S(1)} collective-permute-done((f32[60,8,128]{2,1,0:T(8,128)S(1)}, f32[60,8,128]{2,1,0:T(8,128)S(1)}, u32[]{:S(2)}, u32[]{:S(2)}) %collective-permute-start.8) | collective-permute-done | bytes 245792 | tf_op jit(solution)/shard_map/ppermute | solution.py:516
  70.4 9.8 %shard_map.88 = (f32[1,24,16,128]{3,2,1,0:T(8,128)}, f32[1,24,16,128]{3,2,1,0:T(8,128)}) custom-call(s32[3]{0:T(128)S(1)} %pad_add_fusion.where_ref, f32[4,33,24,128]{3,2,1,0:T(8,128)S(1)} %get-tuple-element.10.ext_ref, f32[31,16,128]{2,1,0:T(8,128)S(1)} %collective-permute-done.7.msg_ref, f32[31,8,128]{2,1,0:T(8,128)S(1)} %slice.49.msg_y, ...), custom_call_target="tpu_custom_call" | custom-call | flops 7000000 | bytes 4000000 | tf_op jit(solution)/shard_map/pallas_call | solution.py:504
  (26 shorter events, 0.4 us)
Async XLA Ops:
  0.6 1.4 %copy-start.4 = (f32[24,16,128]{2,1,0:T(8,128)S(1)}, f32[24,16,128]{2,1,0:T(8,128)}, u32[]{:S(2)}) copy-start(f32[24,16,128]{2,1,0:T(8,128)} %d_ref.1) | copy-start | bytes 589828
  0.6 1.4 %copy-start.1 = (f32[1,24,16,128]{3,2,1,0:T(8,128)S(1)}, f32[1,24,16,128]{3,2,1,0:T(8,128)}, u32[]{:S(2)}) copy-start(f32[1,24,16,128]{3,2,1,0:T(8,128)} %control_ref.3) | copy-start | bytes 589828
  0.7 1.5 %copy-start.5 = (f32[1,24,16,128]{3,2,1,0:T(8,128)S(1)}, f32[1,24,16,128]{3,2,1,0:T(8,128)}, u32[]{:S(2)}) copy-start(f32[1,24,16,128]{3,2,1,0:T(8,128)} %sg_ref.1) | copy-start | bytes 589828
  0.7 1.5 %copy-start.2 = (f32[1,24,16,128]{3,2,1,0:T(8,128)S(1)}, f32[1,24,16,128]{3,2,1,0:T(8,128)}, u32[]{:S(2)}) copy-start(f32[1,24,16,128]{3,2,1,0:T(8,128)} %ag_ref.1) | copy-start | bytes 589828
  0.7 1.5 %copy-start.3 = (f32[24,16,128]{2,1,0:T(8,128)S(1)}, f32[24,16,128]{2,1,0:T(8,128)}, u32[]{:S(2)}) copy-start(f32[24,16,128]{2,1,0:T(8,128)} %initial_ref.1) | copy-start | bytes 589828
  0.7 1.6 %copy-start.6 = (f32[1,24,16,128]{3,2,1,0:T(8,128)S(1)}, f32[1,24,16,128]{3,2,1,0:T(8,128)}, u32[]{:S(2)}) copy-start(f32[1,24,16,128]{3,2,1,0:T(8,128)} %target_ref.1) | copy-start | bytes 589828
  2.2 15.2 %copy-start = (f32[3,24,16,128]{3,2,1,0:T(8,128)S(1)}, f32[3,24,16,128]{3,2,1,0:T(8,128)}, u32[]{:S(2)}) copy-start(f32[3,24,16,128]{3,2,1,0:T(8,128)} %u_ref.1) | copy-start | bytes 1769476
  2.3 13.5 %collective-permute-start = (f32[56,16,128]{2,1,0:T(8,128)S(1)}, f32[56,16,128]{2,1,0:T(8,128)S(1)}, u32[]{:S(2)}, u32[]{:S(2)}) collective-permute-start(f32[56,16,128]{2,1,0:T(8,128)S(1)} %constant_dynamic-update-slice_fusion), channel_id=1, source_target_pairs={{0,2},{2,0},{1,3},{3,1},{4,6},{6,4},{5,7},{7,5},{8,10},{10,8},{9,1... | collective-permute-start | bytes 1376264 | tf_op jit(solution)/shard_map/ppermute | solution.py:516
  5.5 11.9 %collective-permute-start.1 = (f32[8,24,8,128]{3,2,1,0:T(8,128)S(1)}, f32[8,24,8,128]{3,2,1,0:T(8,128)S(1)}, u32[]{:S(2)}, u32[]{:S(2)}) collective-permute-start(f32[8,24,8,128]{3,2,1,0:T(8,128)S(1)} %dynamic-slice_dynamic-update-slice_fusion), channel_id=1, source_target_pairs={{0,1},{1,0},{2,3},{3,2},{4,5},{5,4},{6,7},{7,6},{8,9},{9,8},{10,11... | collective-permute-start | bytes 2359304 | tf_op jit(solution)/shard_map/ppermute | solution.py:516
  15.8 1.6 %collective-permute-start.2 = (f32[56,8,128]{2,1,0:T(8,128)S(1)}, f32[56,8,128]{2,1,0:T(8,128)S(1)}, u32[]{:S(2)}, u32[]{:S(2)}) collective-permute-start(f32[56,8,128]{2,1,0:T(8,128)S(1)} %constant_dynamic-slice_fusion), channel_id=1, source_target_pairs={{0,1},{1,0},{2,3},{3,2},{4,5},{5,4},{6,7},{7,6},{8,9},{9,8},{10,11... | collective-permute-start | bytes 688136 | tf_op jit(solution)/shard_map/ppermute | solution.py:516
  28.5 15.4 %collective-permute-start.3 = (f32[48,16,128]{2,1,0:T(8,128)S(1)}, f32[48,16,128]{2,1,0:T(8,128)S(1)}, u32[]{:S(2)}, u32[]{:S(2)}) collective-permute-start(f32[48,16,128]{2,1,0:T(8,128)S(1)} %get-tuple-element.11.z_ref), channel_id=1, source_target_pairs={{0,4},{4,0},{8,12},{12,8},{1,5},{5,1},{9,13},{13,9},{2,6},{6,2},{1... | collective-permute-start | bytes 1179656 | tf_op jit(solution)/shard_map/ppermute | solution.py:520
  30.4 6.3 %collective-permute-start.4 = (f32[22,16,128]{2,1,0:T(8,128)S(1)}, f32[22,16,128]{2,1,0:T(8,128)S(1)}, u32[]{:S(2)}, u32[]{:S(2)}) collective-permute-start(f32[22,16,128]{2,1,0:T(8,128)S(1)} %get-tuple-element.12.x_ref), channel_id=1, source_target_pairs={{0,2},{2,0},{1,3},{3,1},{4,6},{6,4},{5,7},{7,5},{8,10},{10,8},{9,1... | collective-permute-start | bytes 540680 | tf_op jit(solution)/shard_map/ppermute | solution.py:516
  31.9 12.0 %collective-permute-start.5 = (f32[17,16,128]{2,1,0:T(8,128)S(1)}, f32[17,16,128]{2,1,0:T(8,128)S(1)}, u32[]{:S(2)}, u32[]{:S(2)}) collective-permute-start(f32[17,16,128]{2,1,0:T(8,128)S(1)} %slice.36), channel_id=1, source_target_pairs={{0,6},{2,4},{4,2},{6,0},{8,14},{10,12},{12,10},{14,8},{1,7},{3,5},... | collective-permute-start | bytes 417800 | tf_op jit(solution)/shard_map/ppermute | solution.py:525
  43.9 2.0 %collective-permute-start.6 = (f32[130,8,128]{2,1,0:T(8,128)S(1)}, f32[130,8,128]{2,1,0:T(8,128)S(1)}, u32[]{:S(2)}, u32[]{:S(2)}) collective-permute-start(f32[130,8,128]{2,1,0:T(8,128)S(1)} %fusion.2), channel_id=1, source_target_pairs={{0,1},{1,0},{2,3},{3,2},{4,5},{5,4},{6,7},{7,6},{8,9},{9,8},{10,11... | collective-permute-start | bytes 1597448 | tf_op jit(solution)/shard_map/ppermute | solution.py:516
  54.2 14.6 %collective-permute-start.7 = (f32[31,16,128]{2,1,0:T(8,128)S(1)}, f32[31,16,128]{2,1,0:T(8,128)S(1)}, u32[]{:S(2)}, u32[]{:S(2)}) collective-permute-start(f32[31,16,128]{2,1,0:T(8,128)S(1)} %get-tuple-element.15), channel_id=1, source_target_pairs={{0,8},{4,12},{8,0},{12,4},{1,9},{5,13},{9,1},{13,5},{2,10},{6,14},... | collective-permute-start | bytes 761864 | tf_op jit(solution)/shard_map/ppermute | solution.py:520
  68.8 1.6 %collective-permute-start.8 = (f32[60,8,128]{2,1,0:T(8,128)S(1)}, f32[60,8,128]{2,1,0:T(8,128)S(1)}, u32[]{:S(2)}, u32[]{:S(2)}) collective-permute-start(f32[60,8,128]{2,1,0:T(8,128)S(1)} %fusion.3), channel_id=1, source_target_pairs={{0,1},{1,0},{2,3},{3,2},{4,5},{5,4},{6,7},{7,6},{8,9},{9,8},{10,11... | collective-permute-start | bytes 737288 | tf_op jit(solution)/shard_map/ppermute | solution.py:516

commit v2 on v0

--- a/solution.py
+++ b/solution.py
@@ -1,9 +1,22 @@
+import functools
+
 import jax
 import jax.numpy as jnp
 from jax import lax
+from jax.experimental import pallas as pl
+from jax.experimental.pallas import tpu as pltpu
 from jax.sharding import PartitionSpec as P
 
 STEPS = 6
+SIDE = 8
+NEAR = 6
+LATE = 5
+MSG = 7
+FAR_X = 10
+FAR_E = 7
+COEF = FAR_X - 1
+RIMS = (NEAR, NEAR, NEAR, NEAR, NEAR, NEAR, NEAR + 1, 1)
+STARTS = tuple(sum(RIMS[:i]) for i in range(len(RIMS)))
 
 
 def extended(array, sides, width):
@@ -76,15 +89,6 @@
     return extended(field, (("space", 0), ("yz", 1)), 1)
 
 
-def coefficient_window(rim_coefficients, offset):
-    return rim_coefficients[
-        :,
-        offset : rim_coefficients.shape[1] - offset,
-        offset : rim_coefficients.shape[2] - offset,
-        :,
-    ]
-
-
 def coarse_chain(residual, near_coefficients, adjoint, direction):
     factor = float(STEPS)
 
@@ -96,14 +100,12 @@
     return lax.fori_loop(0, lax.axis_size("tm") - 1, one_turn, residual)
 
 
-def local(initial, diffusion, velocity, control, target, state_guess, adjoint_guess):
-    rim_depth = max(lax.axis_size("tm") // 2, STEPS)
+def any_mesh(initial, diffusion, velocity, control, target, state_guess, adjoint_guess):
     source = control[0]
     guess_state = state_guess[0]
     guess_adjoint = adjoint_guess[0]
     stacked = jnp.concatenate([diffusion[None], velocity, jnp.ones_like(diffusion)[None]], 0)
-    rim_coefficients = extended(stacked, (("space", 1), ("yz", 2)), rim_depth)
-    near_coefficients = coefficient_window(rim_coefficients, rim_depth - 1)
+    near_coefficients = extended(stacked, (("space", 1), ("yz", 2)), 1)
     arrived = passed_along(guess_state, "tm", 1)
     fine = jnp.where(lax.axis_index("tm") == 0, initial, arrived)
     sweep = guess_adjoint
@@ -124,22 +126,588 @@
     return (state_new[None], gradient[None])
 
 
+NAMES = ("c0", "xp", "xm", "yp", "ym", "zp", "zm", "qyp", "qym", "qzp", "qzm")
+CHUNK = 8
+
+
+class Rows:
+    def __init__(self, ref, wide, first=-1):
+        self.ref, self.wide, self.first = ref, wide, first
+
+    def read(self, row, count=1, shift=0):
+        return self.ref[pl.ds((row - self.first) * self.wide + shift, count * self.wide)]
+
+    def write(self, row, value):
+        self.ref[pl.ds((row - self.first) * self.wide, value.shape[0])] = value
+
+
+def shifted(value, step):
+    return pltpu.roll(value, step % value.shape[1], 1)
+
+
+def next_cells(value, step):
+    return pltpu.roll(value, step % value.shape[0], 0)
+
+
+class Stencil:
+    def __init__(self, ref, wide):
+        self.at = {name: Rows(ref.at[i], wide) for i, name in enumerate(NAMES)}
+
+    def fill(self, row, raw, space, core):
+        d, u0, u1, u2 = raw
+        u0 = u0 * (1 - 2 * space).astype(jnp.float32)
+        cell = lax.broadcasted_iota(jnp.int32, d.shape, 0)
+        depth = lax.broadcasted_iota(jnp.int32, d.shape, 1)
+        top = (cell == d.shape[0] - 1) & (core == 1)
+        bottom = (cell == 0) & (core == 0)
+        last, first = depth == d.shape[1] - 1, depth == 0
+        zero = jnp.zeros_like(d)
+        values = {
+            "c0": 1.0 - 6.0 * d,
+            "xp": d - u0,
+            "xm": d + u0,
+            "yp": jnp.where(top, zero, d - u1),
+            "ym": jnp.where(bottom, zero, d + u1),
+            "zp": jnp.where(last, zero, d - u2),
+            "zm": jnp.where(first, zero, d + u2),
+            "qyp": jnp.where(top, zero, next_cells(d + u1, -1)),
+            "qym": jnp.where(bottom, zero, next_cells(d - u1, 1)),
+            "qzp": jnp.where(last, zero, shifted(d + u2, -1)),
+            "qzm": jnp.where(first, zero, shifted(d - u2, 1)),
+        }
+        for name in NAMES:
+            self.at[name].write(row, values[name])
+
+    def edge(self):
+        for name in NAMES:
+            rows = self.at[name]
+            rows.write(-1, jnp.zeros((rows.wide, rows.ref.shape[-1]), jnp.float32))
+
+    def terms(self, fields, row, count, adjoint):
+        at = self.at
+        if adjoint:
+            up, low, ends = at["xm"].read(row + 1, count), at["xp"].read(row - 1, count), ("qyp", "qym", "qzp", "qzm")
+        else:
+            up, low, ends = at["xp"].read(row, count), at["xm"].read(row, count), ("yp", "ym", "zp", "zm")
+        yp, ym, zp, zm = (at[n].read(row, count) for n in ends)
+        same = at["c0"].read(row, count)
+        result = []
+        for v in fields:
+            c = v.read(row, count)
+            around = up * v.read(row + 1, count) + low * v.read(row - 1, count)
+            around = around + (yp * v.read(row, count, 1) + ym * v.read(row, count, -1))
+            around = around + (zp * shifted(c, -1) + zm * shifted(c, 1))
+            result.append((around, c, same * c))
+        return result
+
+    def fine(self, fields, row, count, adjoint):
+        return [own + around for around, c, own in self.terms(fields, row, count, adjoint)]
+
+    def coarse(self, v, row, count, adjoint):
+        ((around, c, own),) = self.terms([v], row, count, adjoint)
+        return c + float(STEPS) * (around + (own - c))
+
+
+def chunks(start, stop, size=CHUNK):
+    return [(row, min(size, stop - row)) for row in range(start, stop, size)]
+
+
+def joined(core, own, side):
+    return jnp.where(core == 1, jnp.concatenate([side, own], 0), jnp.concatenate([own, side], 0))
+
+
+def mid(core, cells):
+    return jnp.where(core == 1, cells[SIDE:], cells[:-SIDE])
+
+
+def zeros(rows):
+    return jnp.zeros((rows.wide, rows.ref.shape[-1]), jnp.float32)
+
+
+def pack_kernel(rows, own, where_ref, d_ref, u_ref, control_ref, sg_ref, ag_ref, initial_ref, target_ref,
+                x_out, side_out, d_out, u_out, control_out, sg_out, ag_out, initial_out, target_out, whole_sem, part_sem):
+    slab, space, core = where_ref[0], where_ref[1], where_ref[2]
+    ins = (d_ref, u_ref, control_ref, sg_ref, ag_ref, initial_ref, target_ref)
+    outs = (d_out, u_out, control_out, sg_out, ag_out, initial_out, target_out)
+    fields = (d_ref, u_ref.at[0], u_ref.at[1], u_ref.at[2], control_ref.at[0], sg_ref.at[0], None, target_ref.at[0])
+    beside = pl.multiple_of(jnp.where(core == 0, own - SIDE, 0), SIDE)
+    begin = [jnp.where(space == 0, rows - n, 0) for n in RIMS]
+    parts, wholes = [], []
+    for i, field in enumerate(fields):
+        if field is not None:
+            rim = x_out.at[pl.ds(STARTS[i], RIMS[i])]
+            parts.append(pltpu.make_async_copy(field.at[pl.ds(begin[i], RIMS[i])], rim, part_sem.at[2 * i]))
+            parts.append(pltpu.make_async_copy(field.at[:, pl.ds(beside, SIDE)], side_out.at[i], part_sem.at[2 * i + 1]))
+    for i, (source, target) in enumerate(zip(ins, outs)):
+        wholes.append(pltpu.make_async_copy(source, target, whole_sem.at[i]))
+    for copy in (wholes[4], wholes[5], *parts, *wholes[:4], wholes[6]):
+        copy.start()
+    wholes[4].wait()
+    wholes[5].wait()
+    first = slab == 0
+    for j in range(RIMS[6]):
+        at = begin[6] + j
+        x_out[STARTS[6] + j] = jnp.where(first, initial_out[at], ag_out[0, at])
+    for row in range(rows):
+        cells = jnp.where(first, initial_out[row], ag_out[0, row])
+        side_out[6, row] = jnp.where(core == 0, cells[own - SIDE :], cells[:SIDE])
+    for copy in (*parts, *wholes[:4], wholes[6]):
+        copy.wait()
+
+
+def inner_kernel(rows, wide, where_ref, d_ref, u_ref, control_ref, sg_ref, ag_ref, initial_ref, target_ref, side_ref,
+                 coef_out, hist_out, z_out, base_out, state_out, c_a, c_b, g_a, g_b, s_a, s_b, con_ref):
+    slab, space, core = where_ref[0], where_ref[1], where_ref[2]
+    first = slab == 0
+    c, g, s = ([Rows(r, wide) for r in pair] for pair in ((c_a, c_b), (g_a, g_b), (s_a, s_b)))
+    con = Rows(con_ref, wide, 0)
+    for field in (*c, *g, *s):
+        field.write(-1, zeros(field))
+    stencil = Stencil(coef_out, wide)
+    stencil.edge()
+
+    def natural(row):
+        return jnp.where(space == 1, rows - 1 - row, row)
+
+    def mine(i, own, row):
+        return joined(core, own, side_ref[i, natural(row)])
+
+    for row in range(rows):
+        at = natural(row)
+        stencil.fill(row, [mine(0, d_ref[at], row)] + [mine(1 + i, u_ref[i, at], row) for i in range(3)], space, core)
+        con.write(row, mine(4, control_ref[0, at], row))
+        g[0].write(row, mine(5, sg_ref[0, at], row))
+        start = mine(6, initial_ref[at], row)
+        c[0].write(row, jnp.where(first, start, jnp.zeros_like(start)))
+        s[0].write(row, mine(6, ag_ref[0, at], row))
+
+    def keep(level, fields):
+        for i, field in enumerate(fields):
+            hist_out[i, level] = field.read(rows - 2 - level, 2)
+
+    keep(0, (c[0], g[0], s[0]))
+    for step in range(STEPS):
+        now, later = step % 2, 1 - step % 2
+        for row, count in chunks(0, rows - 1 - step, 4):
+            to_c, to_g = stencil.fine((c[now], g[now]), row, count, False)
+            (to_s,) = stencil.fine((s[now],), row, count, True)
+            c[later].write(row, to_c + con.read(row, count))
+            g[later].write(row, to_g)
+            s[later].write(row, to_s)
+        if step < STEPS - 1:
+            keep(step + 1, (c[later], g[later], s[later]))
+    cc, dd = c[1], s[1]
+    ready = rows - STEPS
+    for row in range(ready):
+        sg = mine(5, sg_ref[0, natural(row)], row)
+        gap = c[0].read(row) - sg
+        ag = mine(6, ag_ref[0, natural(row)], row)
+        state = sg + gap
+        rest = state - mine(7, target_ref[0, natural(row)], row) - ag
+        cc.write(row, gap)
+        dd.write(row, rest)
+        state_out[row] = mid(core, state)
+        base_out[row] = mid(core, ag + rest)
+    keep(STEPS, (cc, g[0], s[0], dd))
+    for row, count in chunks(0, ready - 1):
+        x = g[0].read(row, count) + stencil.coarse(cc, row, count, False)
+        e = s[0].read(row, count) + stencil.coarse(dd, row, count, True)
+        for r in range(count):
+            z_out[row + r] = mid(core, x[r * wide : (r + 1) * wide])
+            z_out[ready - 1 + row + r] = mid(core, e[r * wide : (r + 1) * wide])
+
+
+def wedge_kernel(rows, wide, where_ref, coef_in, hist_ref, d_ref, u_ref, control_ref, sg_ref, ag_ref, target_ref, side_ref, z_ref, xr_ref, ys_ref,
+                 coef_out, z_out, x_out, far_out, base_out, state_out, c_a, c_b, g_a, g_b, s_a, s_b, con_ref, sg_s, tar_s, ag_s):
+    slab, space, core = where_ref[0], where_ref[1], where_ref[2]
+    first = slab == 0
+    flip = space == 1
+    c, g, s = (
+        [[Rows(r, wide, rows - 2 - level) for r in pair] for level in range(STEPS + 1)]
+        for pair in ((c_a, c_b), (g_a, g_b), (s_a, s_b))
+    )
+    at_level = lambda field, level: field[level][level % 2]
+    low = rows - STEPS
+    con, sgs, tars, ags = (Rows(r, wide, low) for r in (con_ref, sg_s, tar_s, ag_s))
+    stencil = Stencil(coef_out, wide)
+
+    def natural(row):
+        return jnp.where(flip, rows - 1 - row, row)
+
+    def rim(i, j):
+        at = STARTS[i] + jnp.where(flip, RIMS[i] - 1 - j, j)
+        return joined(core, xr_ref[at], ys_ref[at])
+
+    for j in range(NEAR):
+        stencil.fill(rows + j, [rim(i, j) for i in range(4)], space, core)
+    for row in range(low, rows):
+        at = natural(row)
+        con.write(row, joined(core, control_ref[0, at], side_ref[4, at]))
+        sgs.write(row, joined(core, sg_ref[0, at], side_ref[5, at]))
+        ags.write(row, joined(core, ag_ref[0, at], side_ref[6, at]))
+        tars.write(row, joined(core, target_ref[0, at], side_ref[7, at]))
+    for j in range(NEAR):
+        con.write(rows + j, rim(4, j))
+    sgs.write(rows, rim(5, 0))
+    ags.write(rows, rim(6, 0))
+    tars.write(rows, rim(7, 0))
+    for j in range(NEAR + 1):
+        start = rim(6, j)
+        c[0][0].write(rows + j, jnp.where(first, start, jnp.zeros_like(start)))
+        if j < NEAR:
+            s[0][0].write(rows + j, start)
+            g[0][0].write(rows + j, rim(5, j))
+
+    def restore(level, fields):
+        for i, field in enumerate(fields):
+            field.write(rows - 2 - level, hist_ref[i, level])
+
+    restore(0, (c[0][0], g[0][0], s[0][0]))
+    for level in range(STEPS):
+        row = rows - 1 - level
+        nc, ng, ns = (at_level(f, level) for f in (c, g, s))
+        lc, lg, ls = (at_level(f, level + 1) for f in (c, g, s))
+        to_c, to_g = stencil.fine((nc, ng), row, NEAR, False)
+        (to_s,) = stencil.fine((ns,), row, NEAR, True)
+        lc.write(row, to_c + con.read(row, NEAR))
+        lg.write(row, to_g)
+        ls.write(row, to_s)
+        (to_c,) = stencil.fine((nc,), row + NEAR, 1, False)
+        lc.write(row + NEAR, to_c + con.read(row + NEAR))
+        if level < STEPS - 1:
+            restore(level + 1, (lc, lg, ls))
+    fc, fg, fs = (at_level(f, STEPS) for f in (c, g, s))
+    cc, dd = c[STEPS][1], s[STEPS][1]
+    restore(STEPS, (cc, fg, fs, dd))
+    count = NEAR + 1
+    sg = sgs.read(low, count)
+    gap = fc.read(low, count) - sg
+    state = sg + gap
+    ag = ags.read(low, count)
+    rest = state - tars.read(low, count) - ag
+    cc.write(low, gap)
+    dd.write(low, rest)
+    base = ag + rest
+    x = fg.read(low - 1, count) + stencil.coarse(cc, low - 1, count, False)
+    e = fs.read(low - 1, count) + stencil.coarse(dd, low - 1, count, True)
+
+    def cells(value, r):
+        return mid(core, value[r * wide : (r + 1) * wide])
+
+    for r in range(NEAR):
+        state_out[r] = cells(state, r)
+        base_out[r] = cells(base, r)
+    for r in range(count):
+        x_row, e_row = cells(x, r), cells(e, r)
+        z_out[r] = x_row
+        z_out[count + r] = e_row
+        for out in (x_out, far_out):
+            out[count - 1 - r] = x_row
+            out[FAR_X + count - 1 - r] = e_row
+    for j in range(count, FAR_X):
+        x_row = z_ref[rows - 1 - j]
+        for out in (x_out, far_out):
+            out[j] = x_row
+    late = FAR_X + FAR_E
+    for j in range(LATE):
+        x_out[late + j] = cells(base, NEAR - 1 - j)
+    for j in range(COEF - NEAR):
+        at = natural(rows - 1 - NEAR - j)
+        for i, value in enumerate([d_ref[at]] + [u_ref[i, at] for i in range(3)]):
+            x_out[late + LATE + i * (COEF - NEAR) + j] = value
+
+
+def message_kernel(rows, wide, where_ref, coef_in, za, zb, ra, rb, xr, xzr, za_y, zb_y, ra_y, rb_y, xr_y, xzr_y,
+                   coef_out, msg_out, h_out, xa_out, eb_out, xb_s, ea_s):
+    slab, space, core = where_ref[0], where_ref[1], where_ref[2]
+    odd = slab % 2 == 1
+    upper = slab >= 2
+    stencil = Stencil(coef_out, wide)
+    late = FAR_X + FAR_E
+    for j in range(COEF - NEAR):
+        at = [late + LATE + i * (COEF - NEAR) + j for i in range(4)]
+        stencil.fill(rows + NEAR + j, [joined(core, xr[r], xr_y[late + r - late - LATE]) for r in at], space, core)
+    xa, xb, ea, eb, h = (Rows(r, wide) for r in (xa_out, xb_s, ea_s, eb_out, h_out))
+    for field in (xa, xb, ea, eb, h):
+        field.write(-1, zeros(field))
+
+    def both(lower, higher, row, mine, mine_y, other, other_y, at):
+        a, b = joined(core, mine[at], mine_y[at]), joined(core, other[at], other_y[at])
+        lower.write(row, jnp.where(odd, b, a))
+        higher.write(row, jnp.where(odd, a, b))
+
+    inner = rows - NEAR - 1
+    for row in range(rows):
+        if row < inner:
+            both(xa, xb, row, za, za_y, ra, ra_y, row)
+            both(ea, eb, row, za, za_y, ra, ra_y, inner + row)
+        else:
+            both(xa, xb, row, zb, zb_y, rb, rb_y, row - inner)
+            both(ea, eb, row, zb, zb_y, rb, rb_y, rows - inner + row - inner)
+    for j in range(FAR_X):
+        both(xa, xb, rows + j, xr, xr_y, xzr, xzr_y, j)
+    for j in range(FAR_E):
+        both(ea, eb, rows + j, xr, xr_y, xzr, xzr_y, FAR_X + j)
+
+    @pl.when(jnp.logical_not(upper))
+    def _():
+        for row, count in chunks(0, rows + FAR_X - 1):
+            h.write(row, xb.read(row, count) + stencil.coarse(xa, row, count, False))
+        for row in range(rows + MSG):
+            msg_out[row] = mid(core, h.read(row))
+
+    @pl.when(upper)
+    def _():
+        for row, count in chunks(0, rows + FAR_E):
+            h.write(row, eb.read(row, count) + stencil.coarse(xa, row, count, True))
+        for row, count in chunks(0, rows + FAR_E - 1):
+            value = ea.read(row, count) + stencil.coarse(h, row, count, True)
+            for r in range(count):
+                msg_out[row + r] = mid(core, value[r * wide : (r + 1) * wide])
+        msg_out[rows + FAR_E - 1] = mid(core, zeros(ea))
+
+
+def base_kernel(rows, wide, where_ref, coef_ref, h_ref, xa_ref, eb_ref, start_a, start_b, start_x, base_out, t1_s, t2_s):
+    slab, core = where_ref[0], where_ref[2]
+    odd = slab % 2 == 1
+    upper = slab >= 2
+    stencil = Stencil(coef_ref, wide)
+    h, xa, eb, t1, t2 = (Rows(r, wide) for r in (h_ref, xa_ref, eb_ref, t1_s, t2_s))
+    for field in (t1, t2):
+        field.write(-1, zeros(field))
+
+    def start(row):
+        if row >= rows:
+            return start_x[FAR_X + FAR_E + row - rows]
+        return start_a[row] if row < start_a.shape[0] else start_b[row - start_a.shape[0]]
+
+    def put(source):
+        for row in range(rows + LATE):
+            base_out[row] = start(row) + mid(core, source.read(row))
+
+    @pl.when(jnp.logical_not(upper))
+    def _():
+        for row, count in chunks(0, rows + FAR_X - 2):
+            t1.write(row, stencil.coarse(h, row, count, False))
+        for row, count in chunks(0, rows + FAR_X - 3):
+            t2.write(row, h.read(row, count) + stencil.coarse(t1, row, count, True))
+        for row, count in chunks(0, rows + FAR_X - 4):
+            t1.write(row, xa.read(row, count) + stencil.coarse(t2, row, count, True))
+
+        @pl.when(odd)
+        def _():
+            put(t1)
+
+        @pl.when(jnp.logical_not(odd))
+        def _():
+            for row, count in chunks(0, rows + LATE):
+                t2.write(row, eb.read(row, count) + stencil.coarse(t1, row, count, True))
+            put(t2)
+
+    @pl.when(upper & odd)
+    def _():
+        put(xa)
+
+    @pl.when(upper & jnp.logical_not(odd))
+    def _():
+        put(h)
+
+
+def last_kernel(rows, wide, where_ref, coef_ref, msg, msg_y, base, base_y, xa_ref, state_a, state_b, control_ref,
+                state_out, gradient_out, m_s, t0_s, t1_s, total_s):
+    slab, space, core = where_ref[0], where_ref[1], where_ref[2]
+    stencil = Stencil(coef_ref, wide)
+    m, t0, t1, total, xa = (Rows(r, wide) for r in (m_s, t0_s, t1_s, total_s, xa_ref))
+    for field in (m, t0, t1):
+        field.write(-1, zeros(field))
+
+    def natural(row):
+        return jnp.where(space == 1, rows - 1 - row, row)
+
+    def state(came):
+        for row in range(rows):
+            before = state_a[row] if row < state_a.shape[0] else state_b[row - state_a.shape[0]]
+            state_out[0, natural(row)] = before + mid(core, came(row)) if came else before
+
+    def begin(extra):
+        for row, count in chunks(0, rows + LATE):
+            ready = jnp.concatenate([joined(core, base[r], base_y[r]) for r in range(row, row + count)], 0)
+            t1.write(row, ready + extra(row, count))
+
+    for row in range(rows + MSG):
+        m.write(row, joined(core, msg[row], msg_y[row]))
+
+    @pl.when(slab == 0)
+    def _():
+        begin(lambda row, count: stencil.coarse(m, row, count, True))
+        state(None)
+
+    @pl.when(slab == 1)
+    def _():
+        begin(m.read)
+        state(xa.read)
+
+    @pl.when(slab >= 2)
+    def _():
+        for row, count in chunks(0, rows + MSG - 1):
+            t0.write(row, stencil.coarse(m, row, count, False))
+
+    @pl.when(slab == 2)
+    def _():
+        begin(lambda row, count: m.read(row, count) + stencil.coarse(t0, row, count, True))
+        state(m.read)
+
+    @pl.when(slab == 3)
+    def _():
+        begin(t0.read)
+        state(lambda row: xa.read(row) + t0.read(row))
+
+    pair = (t1, m)
+    for step in range(STEPS - 1):
+        now, later = pair[step % 2], pair[1 - step % 2]
+        for row, count in chunks(0, rows + LATE - 1 - step):
+            (value,) = stencil.fine((now,), row, count, True)
+            if step < STEPS - 2:
+                later.write(row, value)
+            count = min(count, rows - row)
+            if count > 0:
+                value = value[: count * wide] + (total if step else now).read(row, count)
+                if step < STEPS - 2:
+                    total.write(row, value)
+                else:
+                    for r in range(count):
+                        at = natural(row + r)
+                        own = mid(core, value[r * wide : (r + 1) * wide])
+                        gradient_out[0, at] = own / float(STEPS) + 0.5 * control_ref[0, at]
+
+
+def call(kernel, outs, scratch, flops, *args, alias=None, source=pltpu.VMEM, moved=4000000):
+    whole = pl.BlockSpec(memory_space=pltpu.VMEM)
+    return pl.pallas_call(
+        kernel,
+        out_shape=[jax.ShapeDtypeStruct(shape, jnp.float32) for shape in outs],
+        in_specs=[pl.BlockSpec(memory_space=pltpu.SMEM)] + [pl.BlockSpec(memory_space=source)] * (len(args) - 1),
+        out_specs=[whole] * len(outs),
+        scratch_shapes=[pltpu.VMEM(shape, jnp.float32) if isinstance(shape, tuple) else shape for shape in scratch],
+        input_output_aliases=alias or {},
+        compiler_params=pltpu.CompilerParams(vmem_limit_bytes=24 * 1024 * 1024),
+        cost_estimate=pl.CostEstimate(flops=flops, bytes_accessed=moved, transcendentals=0),
+    )(*args)
+
+
+def swapped(block, axis):
+    return lax.ppermute(block, axis, [(0, 1), (1, 0)])
+
+
+def across(block, distance):
+    return lax.ppermute(block, "tm", [(i, i ^ distance) for i in range(4)])
+
+
+def across_turned(block, distance):
+    route = [(2 * i + j, 2 * (i ^ distance) + 1 - j) for i in range(4) for j in range(2)]
+    return lax.ppermute(block, ("tm", "space"), route)
+
+
+def four_slabs(initial, diffusion, velocity, control, target, state_guess, adjoint_guess):
+    rows, own, depth = diffusion.shape
+    wide = own + SIDE
+    slab, space, core = lax.axis_index("tm"), lax.axis_index("space"), lax.axis_index("yz")
+    where = jnp.stack([slab, space, core]).astype(jnp.int32)
+    def edge(block):
+        return lax.dynamic_slice_in_dim(block, jnp.where(core == 0, own - SIDE, 0), SIDE, axis=block.ndim - 2)
+
+    def flat(count):
+        return (count * wide, depth)
+
+    def through(fields, axis):
+        got = swapped(jnp.concatenate([edge(f) for f in fields], 0), axis)
+        ends = [sum(f.shape[0] for f in fields[: i + 1]) for i in range(len(fields))]
+        return [got[e - f.shape[0] : e] for f, e in zip(fields, ends)]
+
+    inputs = (diffusion, velocity, control, state_guess, adjoint_guess, initial, target)
+    x_send, side_send, *inputs = call(
+        functools.partial(pack_kernel, rows, own),
+        [(sum(RIMS), own, depth), (len(RIMS), rows, SIDE, depth)] + [a.shape for a in inputs],
+        [pltpu.SemaphoreType.DMA((len(inputs),)), pltpu.SemaphoreType.DMA((2 * len(RIMS),))],
+        100000,
+        where, *(pltpu.with_memory_space_constraint(a, pltpu.HBM) for a in inputs),
+        source=pltpu.HBM,
+        moved=1000,
+    )
+    diffusion, velocity, control, state_guess, adjoint_guess, initial, target = inputs
+    x_here = swapped(x_send, "space")
+    side = swapped(side_send, "yz")
+    coefs = (len(NAMES), *flat(rows + COEF + 1))
+    inner = rows - NEAR - 1
+    tall = flat(rows + FAR_X + 2)
+    cells = lambda count: (count, own, depth)
+    coef, hist, z_a, base_a, state_a = call(
+        functools.partial(inner_kernel, rows, wide),
+        [coefs, (4, STEPS + 1, *flat(2)), cells(2 * inner), cells(inner + 1), cells(inner + 1)],
+        [flat(rows + 2)] * 6 + [flat(rows)],
+        16000000,
+        where, *inputs, side,
+    )
+    r_a = across(z_a, 1)
+    x_here, coef = lax.optimization_barrier((x_here, coef))
+    x_side = swapped(edge(x_here), "yz")
+    small = flat(NEAR + 5)
+    count = FAR_X + FAR_E
+    coef, z_b, x_out, far, base_b, state_b = call(
+        functools.partial(wedge_kernel, rows, wide),
+        [coefs, cells(2 * NEAR + 2), cells(count + LATE + 4 * (COEF - NEAR)), cells(count), cells(NEAR), cells(NEAR)],
+        [small] * 6 + [flat(2 * NEAR)] + [flat(NEAR + 1)] * 3,
+        6000000,
+        where, coef, hist, diffusion, velocity, control, state_guess, adjoint_guess, target, side, z_a, x_here, x_side,
+        alias={1: 0},
+    )
+    x_in = swapped(x_out, "space")
+    xz_in = across_turned(far, 1)
+    r_b = across(z_b, 1)
+    za_y, ra_y = through([z_a, r_a], "yz")
+    zb_y, rb_y, xr_y, xzr_y = through([z_b, r_b, jnp.concatenate([x_in[:count], x_in[count + LATE :]], 0), xz_in], "yz")
+    coef, msg, h, xa, eb = call(
+        functools.partial(message_kernel, rows, wide),
+        [coefs, cells(rows + MSG), tall, tall, tall],
+        [tall, tall],
+        6000000,
+        where, coef, z_a, z_b, r_a, r_b, x_in, xz_in, za_y, zb_y, ra_y, rb_y, xr_y, xzr_y,
+        alias={1: 0},
+    )
+    msg_in = across(msg, 2)
+    (base,) = call(
+        functools.partial(base_kernel, rows, wide),
+        [(rows + LATE, own, depth)],
+        [tall, tall],
+        8000000,
+        where, coef, h, xa, eb, base_a, base_b, x_in,
+    )
+    (base_y,) = through([base], "yz")
+    (msg_y,) = through([msg_in], "yz")
+    return call(
+        functools.partial(last_kernel, rows, wide),
+        [(1, rows, own, depth), (1, rows, own, depth)],
+        [tall] * 4,
+        8000000,
+        where, coef, msg_in, msg_y, base, base_y, xa, state_a, state_b, control,
+    )
+
+
 def solution(mesh):
+    sizes = mesh.shape
+
+    def local(*args):
+        rows, own, depth = args[1].shape
+        fits = (sizes["tm"], sizes["space"], sizes["yz"]) == (4, 2, 2)
+        fits = fits and rows >= 2 * FAR_X and own % 8 == 0 and own >= SIDE and depth % 128 == 0
+        return four_slabs(*args) if fits else any_mesh(*args)
+
+    field = P(("groups", "space"), "yz", None)
+    slabs = P("tm", ("groups", "space"), "yz", None)
     return jax.shard_map(
         local,
         mesh=mesh,
-        in_specs=(
-            P(("groups", "space"), "yz", None),
-            P(("groups", "space"), "yz", None),
-            P(None, ("groups", "space"), "yz", None),
-            P("tm", ("groups", "space"), "yz", None),
-            P("tm", ("groups", "space"), "yz", None),
-            P("tm", ("groups", "space"), "yz", None),
-            P("tm", ("groups", "space"), "yz", None),
-        ),
-        out_specs=(
-            P("tm", ("groups", "space"), "yz", None),
-            P("tm", ("groups", "space"), "yz", None),
-        ),
+        in_specs=(field, field, P(None, ("groups", "space"), "yz", None), slabs, slabs, slabs, slabs),
+        out_specs=(slabs, slabs),
         check_vma=False,
     )

time: 368 us -> 55.3 us (0.15)
  the two profiles are of different devices: /device:TPU:17 before, /device:TPU:0 now
where the time goes in v2:
time: 55.3 us; the launch traced here: 55.2 us
  waiting for transfers between devices  24.3 us (44%)
  Pallas kernels  17.5 us (32%)
  starting transfers between devices  12.3 us (22%)
  between operations  0.82 us (1%)
    pallas_call x6, Pallas kernels, call(): pl.pallas_call(kernel, out_shape=[jax.ShapeDtypeStruct(shape, jnp.float32...  17.5 us
    ppermute x3, waiting for transfers between devices, across(): return lax.ppermute(block, 'tm', [(i, i ^ distance) for i in range(4)])  16.4 us
    ppermute x8, waiting for transfers between devices, swapped(): return lax.ppermute(block, axis, [(0, 1), (1, 0)])  7.86 us
    ppermute x3, starting transfers between devices, across(): return lax.ppermute(block, 'tm', [(i, i ^ distance) for i in range(4)])  5.58 us
    ppermute x8, starting transfers between devices, swapped(): return lax.ppermute(block, axis, [(0, 1), (1, 0)])  5.46 us
    ppermute x1, starting transfers between devices, across_turned(): return lax.ppermute(block, ('tm', 'space'), route)  1.28 us
  transfers between devices with their start and end apart: 12, of which 7 were waited for; matrix products, arithmetic and copies ran while one was open for 0% of the time, Pallas kernels for 17%

profile of v2, /device:TPU:0, one launch (start us, length us, event | category | flops | bytes accessed | tf_op | source)
XLA Modules:
  0.0 55.2 jit_solution(5411619318543736052)
XLA Ops:
  0.6 0.1 pad_add_fusion.where_ref
  0.7 3.5 %shard_map.86 = (f32[44,16,128]{2,1,0:T(8,128)S(1)}, f32[8,24,8,128]{3,2,1,0:T(8,128)}, f32[24,16,128]{2,1,0:T(8,128)S(1)}, f32[3,24,16,128]{3,2,1,0:T(8,128)S(1...) custom-call(s32[3]{0:T(128)S(1)} %pad_add_fusion.where_ref, ...), custom_call_target="tpu_custom_call" | custom-call | flops 100000 | bytes 1000 | tf_op jit(solution)/shard_map/pallas_call | solution.py:586
  4.2 0.5 collective-permute-start.1
  4.7 2.6 %collective-permute-start = (f32[44,16,128]{2,1,0:T(8,128)S(1)}, f32[44,16,128]{2,1,0:T(8,128)S(1)}, u32[]{:S(2)}, u32[]{:S(2)}) collective-permute-start(f32[44,16,128]{2,1,0:T(8,128)S(1)} %get-tuple-element.29), channel_id=1, source_target_pairs={{0,2},{2,0},{1,3},{3,1},{4,6},{6,4},{5,7},{7,5},{8,10},{10,8},{9,1... | collective-permute-start | bytes 1081352 | tf_op jit(solution)/shard_map/ppermute | solution.py:599
  7.3 0.0 collective-permute-done.1.side_ref
  7.3 5.0 %shard_map.87 = (f32[11,816,128]{2,1,0:T(8,128)S(1)}, f32[4,7,48,128]{3,2,1,0:T(8,128)S(1)}, f32[34,16,128]{2,1,0:T(8,128)S(1)}, f32[18,16,128]{2,1,0:T(8,128)S(1)}, f32[18,16,128]{2,1,0:T(8,128)S(1)}) custom-call(s32[3]{0:T(128)S(1)} %pad_add_fusion.where_ref, f32[24,16,128]{2,1,0:T(8,128)S(1)} %get-tuple-element.30.d_ref, ...), custom_call_target="tpu_custom_call" | custom-call | flops 16000000 | bytes 4000000 | tf_op jit(solution)/shard_map/pallas_call | solution.py:586
  12.3 4.0 %collective-permute-done.xr_ref = f32[44,16,128]{2,1,0:T(8,128)S(1)} collective-permute-done((f32[44,16,128]{2,1,0:T(8,128)S(1)}, f32[44,16,128]{2,1,0:T(8,128)S(1)}, u32[]{:S(2)}, u32[]{:S(2)}) %collective-permute-start) | collective-permute-done | bytes 360480 | tf_op jit(solution)/shard_map/ppermute | solution.py:599
  16.3 0.1 collective-permute-start.2
  16.4 1.9 %collective-permute-start.3 = (f32[34,16,128]{2,1,0:T(8,128)S(1)}, f32[34,16,128]{2,1,0:T(8,128)S(1)}, u32[]{:S(2)}, u32[]{:S(2)}) collective-permute-start(f32[34,16,128]{2,1,0:T(8,128)S(1)} %get-tuple-element.41.z_ref.za), channel_id=1, source_target_pairs={{0,4},{4,0},{8,12},{12,8},{1,5},{5,1},{9,13},{13,9},{2,6},{6,2},{1... | collective-permute-start | bytes 835592 | tf_op jit(solution)/shard_map/ppermute | solution.py:603
  18.3 0.0 collective-permute-done.2.ys_ref
  18.3 2.3 %shard_map.88 = (f32[11,816,128]{2,1,0:T(8,128)S(1)}, f32[14,16,128]{2,1,0:T(8,128)S(1)}, f32[34,16,128]{2,1,0:T(8,128)S(1)}, f32[17,16,128]{2,1,0:T(8,128)S(1)}...) custom-call(s32[3]{0:T(128)S(1)} %pad_add_fusion.where_ref, ...), custom_call_target="tpu_custom_call", output_to_operand_aliasing={{0}: (1, {})} | custom-call | flops 6000000 | bytes 4000000 | tf_op jit(solution)/shard_map/pallas_call | solution.py:586
  20.6 1.5 %collective-permute-start.5 = (f32[34,16,128]{2,1,0:T(8,128)S(1)}, f32[34,16,128]{2,1,0:T(8,128)S(1)}, u32[]{:S(2)}, u32[]{:S(2)}) collective-permute-start(f32[34,16,128]{2,1,0:T(8,128)S(1)} %get-tuple-element.45), channel_id=1, source_target_pairs={{0,2},{2,0},{1,3},{3,1},{4,6},{6,4},{5,7},{7,5},{8,10},{10,8},{9,1... | collective-permute-start | bytes 835592 | tf_op jit(solution)/shard_map/ppermute | solution.py:599
  22.1 1.3 %collective-permute-start.6 = (f32[17,16,128]{2,1,0:T(8,128)S(1)}, f32[17,16,128]{2,1,0:T(8,128)S(1)}, u32[]{:S(2)}, u32[]{:S(2)}) collective-permute-start(f32[17,16,128]{2,1,0:T(8,128)S(1)} %get-tuple-element.46), channel_id=1, source_target_pairs={{0,6},{2,4},{4,2},{6,0},{8,14},{10,12},{12,10},{14,8},{1,7},{3,5},... | collective-permute-start | bytes 417800 | tf_op jit(solution)/shard_map/ppermute | solution.py:608
  23.4 0.7 %collective-permute-start.4 = (f32[14,16,128]{2,1,0:T(8,128)S(1)}, f32[14,16,128]{2,1,0:T(8,128)S(1)}, u32[]{:S(2)}, u32[]{:S(2)}) collective-permute-start(f32[14,16,128]{2,1,0:T(8,128)S(1)} %get-tuple-element.44.zb), channel_id=1, source_target_pairs={{0,4},{4,0},{8,12},{12,8},{1,5},{5,1},{9,13},{13,9},{2,6},{6,2},{1... | collective-permute-start | bytes 344072 | tf_op jit(solution)/shard_map/ppermute | solution.py:603
  24.2 1.7 %collective-permute-done.3.ra = f32[34,16,128]{2,1,0:T(8,128)S(1)} collective-permute-done((f32[34,16,128]{2,1,0:T(8,128)S(1)}, f32[34,16,128]{2,1,0:T(8,128)S(1)}, u32[]{:S(2)}, u32[]{:S(2)}) %collective-permute-start.3) | collective-permute-done | bytes 278560 | tf_op jit(solution)/shard_map/ppermute | solution.py:603
  25.9 0.1 collective-permute-start.7
  26.0 5.0 %collective-permute-done.4.rb = f32[14,16,128]{2,1,0:T(8,128)S(1)} collective-permute-done((f32[14,16,128]{2,1,0:T(8,128)S(1)}, f32[14,16,128]{2,1,0:T(8,128)S(1)}, u32[]{:S(2)}, u32[]{:S(2)}) %collective-permute-start.4) | collective-permute-done | bytes 114720 | tf_op jit(solution)/shard_map/ppermute | solution.py:603
  31.0 0.0 collective-permute-done.6.xzr
  31.1 1.3 %collective-permute-done.5.xr.start_x = f32[34,16,128]{2,1,0:T(8,128)S(1)} collective-permute-done((f32[34,16,128]{2,1,0:T(8,128)S(1)}, f32[34,16,128]{2,1,0:T(8,128)S(1)}, u32[]{:S(2)}, u32[]{:S(2)}) %collective-permute-start.5) | collective-permute-done | bytes 278560 | tf_op jit(solution)/shard_map/ppermute | solution.py:599
  32.5 0.1 collective-permute-start.8
  32.5 0.0 collective-permute-done.7
  32.6 1.5 %collective-permute-done.8 = f32[74,8,128]{2,1,0:T(8,128)S(1)} collective-permute-done((f32[74,8,128]{2,1,0:T(8,128)S(1)}, f32[74,8,128]{2,1,0:T(8,128)S(1)}, u32[]{:S(2)}, u32[]{:S(2)}) %collective-permute-start.8) | collective-permute-done | bytes 303136 | tf_op jit(solution)/shard_map/ppermute | solution.py:599
  34.2 1.1 %shard_map.89 = (f32[11,816,128]{2,1,0:T(8,128)S(1)}, f32[31,16,128]{2,1,0:T(8,128)S(1)}, f32[864,128]{1,0:T(8,128)S(1)}, f32[864,128]{1,0:T(8,128)S(1)}, f32[864,128]{1,0:T(8,128)S(1)}) custom-call(s32[3]{0:T(128)S(1)} %pad_add_fusion.where_ref, f32[11,816,128]{2,1,0:T(8,128)S(1)} %get-tuple-element.43.coef_in, ...), custom_call_target="tpu_custom_call", output_to_operand_aliasing={{0}: (1, {})} | custom-call | flops 6000000 | bytes 4000000 | tf_op jit(solution)/shard_map/pallas_call | solution.py:586
  35.3 2.9 %collective-permute-start.9 = (f32[31,16,128]{2,1,0:T(8,128)S(1)}, f32[31,16,128]{2,1,0:T(8,128)S(1)}, u32[]{:S(2)}, u32[]{:S(2)}) collective-permute-start(f32[31,16,128]{2,1,0:T(8,128)S(1)} %get-tuple-element.48), channel_id=1, source_target_pairs={{0,8},{4,12},{8,0},{12,4},{1,9},{5,13},{9,1},{13,5},{2,10},{6,14},... | collective-permute-start | bytes 761864 | tf_op jit(solution)/shard_map/ppermute | solution.py:603
  38.2 2.2 %shard_map.90.base = f32[29,16,128]{2,1,0:T(8,128)S(1)} custom-call(s32[3]{0:T(128)S(1)} %pad_add_fusion.where_ref, f32[11,816,128]{2,1,0:T(8,128)S(1)} %get-tuple-element.47.coef_ref, f32[864,128]{1,0:T(8,128)S(1)} %get-tuple-element.49.h_ref, f32[864,128]{1,0:T(8,128)S(1)} %get-tuple-element.50.xa_ref, f32[864,128]{1,0:T(8,128)S(1)} %get-tuple-element.51.eb_ref, ...), custom_call_target="tpu_custom_call" | custom-call | flops 8000000 | bytes 4000000 | tf_op jit(solution)/shard_map/pallas_call | solution.py:586
  40.4 9.7 %collective-permute-done.9.msg = f32[31,16,128]{2,1,0:T(8,128)S(1)} collective-permute-done((f32[31,16,128]{2,1,0:T(8,128)S(1)}, f32[31,16,128]{2,1,0:T(8,128)S(1)}, u32[]{:S(2)}, u32[]{:S(2)}) %collective-permute-start.9) | collective-permute-done | bytes 253984 | tf_op jit(solution)/shard_map/ppermute | solution.py:603
  50.1 0.1 collective-permute-start.10
  50.2 0.5 collective-permute-start.11
  50.8 1.0 %collective-permute-done.11.base_y = f32[29,8,128]{2,1,0:T(8,128)S(1)} collective-permute-done((f32[29,8,128]{2,1,0:T(8,128)S(1)}, f32[29,8,128]{2,1,0:T(8,128)S(1)}, u32[]{:S(2)}, u32[]{:S(2)}) %collective-permute-start.11) | collective-permute-done | bytes 118816 | tf_op jit(solution)/shard_map/ppermute | solution.py:599
  51.7 0.0 collective-permute-done.10.msg_y
  51.7 3.4 %shard_map.91 = (f32[1,24,16,128]{3,2,1,0:T(8,128)}, f32[1,24,16,128]{3,2,1,0:T(8,128)}) custom-call(s32[3]{0:T(128)S(1)} %pad_add_fusion.where_ref, f32[11,816,128]{2,1,0:T(8,128)S(1)} %get-tuple-element.47.coef_ref, f32[31,16,128]{2,1,0:T(8,128)S(1)} %collective-permute-done.9.msg, f32[31,8,128]{2,1,0:T(8,128)S(1)} %collective-permute-done.10.msg_y, ...), custom_call_target="tpu_custom_call" | custom-call | flops 8000000 | bytes 4000000 | tf_op jit(solution)/shard_map/pallas_call | solution.py:586
  (17 shorter events, 0.2 us)
Async XLA Ops:
  4.2 3.1 %collective-permute-start.1 = (f32[8,24,8,128]{3,2,1,0:T(8,128)}, f32[8,24,8,128]{3,2,1,0:T(8,128)S(1)}, u32[]{:S(2)}, u32[]{:S(2)}) collective-permute-start(f32[8,24,8,128]{3,2,1,0:T(8,128)} %get-tuple-element.37), channel_id=1, source_target_pairs={{0,1},{1,0},{2,3},{3,2},{4,5},{5,4},{6,7},{7,6},{8,9},{9,8},{10,11... | collective-permute-start | bytes 2359304 | tf_op jit(solution)/shard_map/ppermute | solution.py:599
  4.7 11.6 %collective-permute-start = (f32[44,16,128]{2,1,0:T(8,128)S(1)}, f32[44,16,128]{2,1,0:T(8,128)S(1)}, u32[]{:S(2)}, u32[]{:S(2)}) collective-permute-start(f32[44,16,128]{2,1,0:T(8,128)S(1)} %get-tuple-element.29), channel_id=1, source_target_pairs={{0,2},{2,0},{1,3},{3,1},{4,6},{6,4},{5,7},{7,5},{8,10},{10,8},{9,1... | collective-permute-start | bytes 1081352 | tf_op jit(solution)/shard_map/ppermute | solution.py:599
  16.3 2.0 %collective-permute-start.2 = (f32[44,8,128]{2,1,0:T(8,128)S(1)}, f32[44,8,128]{2,1,0:T(8,128)S(1)}, u32[]{:S(2)}, u32[]{:S(2)}) collective-permute-start(f32[44,8,128]{2,1,0:T(8,128)S(1)} %constant_dynamic-slice_fusion.7), channel_id=1, source_target_pairs={{0,1},{1,0},{2,3},{3,2},{4,5},{5,4},{6,7},{7,6},{8,9},{9,8},{10,11... | collective-permute-start | bytes 540680 | tf_op jit(solution)/shard_map/ppermute | solution.py:599
  16.4 9.5 %collective-permute-start.3 = (f32[34,16,128]{2,1,0:T(8,128)S(1)}, f32[34,16,128]{2,1,0:T(8,128)S(1)}, u32[]{:S(2)}, u32[]{:S(2)}) collective-permute-start(f32[34,16,128]{2,1,0:T(8,128)S(1)} %get-tuple-element.41.z_ref.za), channel_id=1, source_target_pairs={{0,4},{4,0},{8,12},{12,8},{1,5},{5,1},{9,13},{13,9},{2,6},{6,2},{1... | collective-permute-start | bytes 835592 | tf_op jit(solution)/shard_map/ppermute | solution.py:603
  20.6 11.8 %collective-permute-start.5 = (f32[34,16,128]{2,1,0:T(8,128)S(1)}, f32[34,16,128]{2,1,0:T(8,128)S(1)}, u32[]{:S(2)}, u32[]{:S(2)}) collective-permute-start(f32[34,16,128]{2,1,0:T(8,128)S(1)} %get-tuple-element.45), channel_id=1, source_target_pairs={{0,2},{2,0},{1,3},{3,1},{4,6},{6,4},{5,7},{7,5},{8,10},{10,8},{9,1... | collective-permute-start | bytes 835592 | tf_op jit(solution)/shard_map/ppermute | solution.py:599
  22.1 8.9 %collective-permute-start.6 = (f32[17,16,128]{2,1,0:T(8,128)S(1)}, f32[17,16,128]{2,1,0:T(8,128)S(1)}, u32[]{:S(2)}, u32[]{:S(2)}) collective-permute-start(f32[17,16,128]{2,1,0:T(8,128)S(1)} %get-tuple-element.46), channel_id=1, source_target_pairs={{0,6},{2,4},{4,2},{6,0},{8,14},{10,12},{12,10},{14,8},{1,7},{3,5},... | collective-permute-start | bytes 417800 | tf_op jit(solution)/shard_map/ppermute | solution.py:608
  23.4 7.6 %collective-permute-start.4 = (f32[14,16,128]{2,1,0:T(8,128)S(1)}, f32[14,16,128]{2,1,0:T(8,128)S(1)}, u32[]{:S(2)}, u32[]{:S(2)}) collective-permute-start(f32[14,16,128]{2,1,0:T(8,128)S(1)} %get-tuple-element.44.zb), channel_id=1, source_target_pairs={{0,4},{4,0},{8,12},{12,8},{1,5},{5,1},{9,13},{13,9},{2,6},{6,2},{1... | collective-permute-start | bytes 344072 | tf_op jit(solution)/shard_map/ppermute | solution.py:603
  25.9 6.6 %collective-permute-start.7 = (f32[68,8,128]{2,1,0:T(8,128)S(1)}, f32[68,8,128]{2,1,0:T(8,128)S(1)}, u32[]{:S(2)}, u32[]{:S(2)}) collective-permute-start(f32[68,8,128]{2,1,0:T(8,128)S(1)} %pad_maximum_fusion.1), channel_id=1, source_target_pairs={{0,1},{1,0},{2,3},{3,2},{4,5},{5,4},{6,7},{7,6},{8,9},{9,8},{10,11... | collective-permute-start | bytes 835592 | tf_op jit(solution)/shard_map/ppermute | solution.py:599
  32.5 1.7 %collective-permute-start.8 = (f32[74,8,128]{2,1,0:T(8,128)S(1)}, f32[74,8,128]{2,1,0:T(8,128)S(1)}, u32[]{:S(2)}, u32[]{:S(2)}) collective-permute-start(f32[74,8,128]{2,1,0:T(8,128)S(1)} %pad_maximum_fusion), channel_id=1, source_target_pairs={{0,1},{1,0},{2,3},{3,2},{4,5},{5,4},{6,7},{7,6},{8,9},{9,8},{10,11... | collective-permute-start | bytes 909320 | tf_op jit(solution)/shard_map/ppermute | solution.py:599
  35.3 14.8 %collective-permute-start.9 = (f32[31,16,128]{2,1,0:T(8,128)S(1)}, f32[31,16,128]{2,1,0:T(8,128)S(1)}, u32[]{:S(2)}, u32[]{:S(2)}) collective-permute-start(f32[31,16,128]{2,1,0:T(8,128)S(1)} %get-tuple-element.48), channel_id=1, source_target_pairs={{0,8},{4,12},{8,0},{12,4},{1,9},{5,13},{9,1},{13,5},{2,10},{6,14},... | collective-permute-start | bytes 761864 | tf_op jit(solution)/shard_map/ppermute | solution.py:603
  50.1 1.6 %collective-permute-start.10 = (f32[31,8,128]{2,1,0:T(8,128)S(1)}, f32[31,8,128]{2,1,0:T(8,128)S(1)}, u32[]{:S(2)}, u32[]{:S(2)}) collective-permute-start(f32[31,8,128]{2,1,0:T(8,128)S(1)} %constant_dynamic-slice_fusion.1), channel_id=1, source_target_pairs={{0,1},{1,0},{2,3},{3,2},{4,5},{5,4},{6,7},{7,6},{8,9},{9,8},{10,11... | collective-permute-start | bytes 380936 | tf_op jit(solution)/shard_map/ppermute | solution.py:599
  50.2 1.5 %collective-permute-start.11 = (f32[29,8,128]{2,1,0:T(8,128)S(1)}, f32[29,8,128]{2,1,0:T(8,128)S(1)}, u32[]{:S(2)}, u32[]{:S(2)}) collective-permute-start(f32[29,8,128]{2,1,0:T(8,128)S(1)} %constant_dynamic-slice_fusion), channel_id=1, source_target_pairs={{0,1},{1,0},{2,3},{3,2},{4,5},{5,4},{6,7},{7,6},{8,9},{9,8},{10,11... | collective-permute-start | bytes 356360 | tf_op jit(solution)/shard_map/ppermute | solution.py:599

commit v3 on v2

--- a/solution.py
+++ b/solution.py
@@ -127,15 +127,15 @@
 
 
 NAMES = ("c0", "xp", "xm", "yp", "ym", "zp", "zm", "qyp", "qym", "qzp", "qzm")
-CHUNK = 8
+CHUNK = 2
 
 
 class Rows:
     def __init__(self, ref, wide, first=-1):
         self.ref, self.wide, self.first = ref, wide, first
 
-    def read(self, row, count=1, shift=0):
-        return self.ref[pl.ds((row - self.first) * self.wide + shift, count * self.wide)]
+    def read(self, row, count=1):
+        return self.ref[pl.ds((row - self.first) * self.wide, count * self.wide)]
 
     def write(self, row, value):
         self.ref[pl.ds((row - self.first) * self.wide, value.shape[0])] = value
@@ -195,7 +195,7 @@
         for v in fields:
             c = v.read(row, count)
             around = up * v.read(row + 1, count) + low * v.read(row - 1, count)
-            around = around + (yp * v.read(row, count, 1) + ym * v.read(row, count, -1))
+            around = around + (yp * next_cells(c, -1) + ym * next_cells(c, 1))
             around = around + (zp * shifted(c, -1) + zm * shifted(c, 1))
             result.append((around, c, same * c))
         return result
@@ -225,38 +225,49 @@
 
 
 def pack_kernel(rows, own, where_ref, d_ref, u_ref, control_ref, sg_ref, ag_ref, initial_ref, target_ref,
-                x_out, side_out, d_out, u_out, control_out, sg_out, ag_out, initial_out, target_out, whole_sem, part_sem):
+                x_out, side_out, more_out, rims, sides, sem):
     slab, space, core = where_ref[0], where_ref[1], where_ref[2]
-    ins = (d_ref, u_ref, control_ref, sg_ref, ag_ref, initial_ref, target_ref)
-    outs = (d_out, u_out, control_out, sg_out, ag_out, initial_out, target_out)
     fields = (d_ref, u_ref.at[0], u_ref.at[1], u_ref.at[2], control_ref.at[0], sg_ref.at[0], None, target_ref.at[0])
+    starts = (ag_ref.at[0], initial_ref)
     beside = pl.multiple_of(jnp.where(core == 0, own - SIDE, 0), SIDE)
-    begin = [jnp.where(space == 0, rows - n, 0) for n in RIMS]
-    parts, wholes = [], []
+    copies = []
+
+    def bring(source, to):
+        copies.append(pltpu.make_async_copy(source, to, sem.at[len(copies)]))
+        copies[-1].start()
+
+    def rim(i):
+        return pl.ds(jnp.where(space == 0, rows - RIMS[i], 0), RIMS[i])
+
+    def edge(field):
+        return field.at[:, pl.ds(beside, SIDE)]
+
+    for i, field in enumerate(starts):
+        bring(field.at[rim(6)], rims.at[i])
+        bring(edge(field), sides.at[i])
     for i, field in enumerate(fields):
         if field is not None:
-            rim = x_out.at[pl.ds(STARTS[i], RIMS[i])]
-            parts.append(pltpu.make_async_copy(field.at[pl.ds(begin[i], RIMS[i])], rim, part_sem.at[2 * i]))
-            parts.append(pltpu.make_async_copy(field.at[:, pl.ds(beside, SIDE)], side_out.at[i], part_sem.at[2 * i + 1]))
-    for i, (source, target) in enumerate(zip(ins, outs)):
-        wholes.append(pltpu.make_async_copy(source, target, whole_sem.at[i]))
-    for copy in (wholes[4], wholes[5], *parts, *wholes[:4], wholes[6]):
+            bring(field.at[rim(i)], x_out.at[pl.ds(STARTS[i], RIMS[i])])
+            bring(edge(field), side_out.at[i])
+    kept = COEF - NEAR
+    for i, field in enumerate(fields[:4]):
+        bring(field.at[pl.ds(jnp.where(space == 0, rows - COEF, NEAR), kept)], more_out.at[pl.ds(i * kept, kept)])
+    for copy in copies:
+        copy.wait()
+    x_out[pl.ds(STARTS[6], RIMS[6])] = jnp.where(slab == 0, rims[1], rims[0])
+    side_out[6] = jnp.where(slab == 0, sides[1], sides[0])
+
+
+def inner_kernel(rows, wide, where_ref, d_hbm, u_hbm, control_hbm, sg_hbm, ag_hbm, initial_hbm, target_hbm, side_ref,
+                 coef_out, hist_out, kept_out, z_out, base_out, state_out, control_ref,
+                 c_a, c_b, g_a, g_b, s_a, s_b, con_ref, d_ref, u_ref, sg_ref, ag_ref, initial_ref, target_ref, sem):
+    ins = (d_hbm, u_hbm, control_hbm, sg_hbm, ag_hbm, initial_hbm, target_hbm)
+    outs = (d_ref, u_ref, control_ref, sg_ref, ag_ref, initial_ref, target_ref)
+    copies = [pltpu.make_async_copy(a, b, sem.at[i]) for i, (a, b) in enumerate(zip(ins, outs))]
+    for copy in copies:
         copy.start()
-    wholes[4].wait()
-    wholes[5].wait()
-    first = slab == 0
-    for j in range(RIMS[6]):
-        at = begin[6] + j
-        x_out[STARTS[6] + j] = jnp.where(first, initial_out[at], ag_out[0, at])
-    for row in range(rows):
-        cells = jnp.where(first, initial_out[row], ag_out[0, row])
-        side_out[6, row] = jnp.where(core == 0, cells[own - SIDE :], cells[:SIDE])
-    for copy in (*parts, *wholes[:4], wholes[6]):
+    for copy in copies:
         copy.wait()
-
-
-def inner_kernel(rows, wide, where_ref, d_ref, u_ref, control_ref, sg_ref, ag_ref, initial_ref, target_ref, side_ref,
-                 coef_out, hist_out, z_out, base_out, state_out, c_a, c_b, g_a, g_b, s_a, s_b, con_ref):
     slab, space, core = where_ref[0], where_ref[1], where_ref[2]
     first = slab == 0
     c, g, s = ([Rows(r, wide) for r in pair] for pair in ((c_a, c_b), (g_a, g_b), (s_a, s_b)))
@@ -281,6 +292,12 @@
         c[0].write(row, jnp.where(first, start, jnp.zeros_like(start)))
         s[0].write(row, mine(6, ag_ref[0, at], row))
 
+    low = rows - STEPS
+    for row in range(low, rows):
+        values = (con.read(row), g[0].read(row), s[0].read(row), mine(7, target_ref[0, natural(row)], row))
+        for i, value in enumerate(values):
+            kept_out[i, pl.ds((row - low) * wide, wide)] = value
+
     def keep(level, fields):
         for i, field in enumerate(fields):
             hist_out[i, level] = field.read(rows - 2 - level, 2)
@@ -288,7 +305,7 @@
     keep(0, (c[0], g[0], s[0]))
     for step in range(STEPS):
         now, later = step % 2, 1 - step % 2
-        for row, count in chunks(0, rows - 1 - step, 4):
+        for row, count in chunks(0, rows - 1 - step):
             to_c, to_g = stencil.fine((c[now], g[now]), row, count, False)
             (to_s,) = stencil.fine((s[now],), row, count, True)
             c[later].write(row, to_c + con.read(row, count))
@@ -317,8 +334,8 @@
             z_out[ready - 1 + row + r] = mid(core, e[r * wide : (r + 1) * wide])
 
 
-def wedge_kernel(rows, wide, where_ref, coef_in, hist_ref, d_ref, u_ref, control_ref, sg_ref, ag_ref, target_ref, side_ref, z_ref, xr_ref, ys_ref,
-                 coef_out, z_out, x_out, far_out, base_out, state_out, c_a, c_b, g_a, g_b, s_a, s_b, con_ref, sg_s, tar_s, ag_s):
+def wedge_kernel(rows, wide, where_ref, coef_in, hist_ref, kept_ref, more_ref, z_ref, xr_ref, ys_ref,
+                 coef_out, z_out, x_out, far_out, base_out, state_out, c_a, c_b, g_a, g_b, s_a, s_b, con_ref):
     slab, space, core = where_ref[0], where_ref[1], where_ref[2]
     first = slab == 0
     flip = space == 1
@@ -328,7 +345,8 @@
     )
     at_level = lambda field, level: field[level][level % 2]
     low = rows - STEPS
-    con, sgs, tars, ags = (Rows(r, wide, low) for r in (con_ref, sg_s, tar_s, ag_s))
+    con = Rows(con_ref, wide, low)
+    con.write(low, kept_ref[0])
     stencil = Stencil(coef_out, wide)
 
     def natural(row):
@@ -340,17 +358,8 @@
 
     for j in range(NEAR):
         stencil.fill(rows + j, [rim(i, j) for i in range(4)], space, core)
-    for row in range(low, rows):
-        at = natural(row)
-        con.write(row, joined(core, control_ref[0, at], side_ref[4, at]))
-        sgs.write(row, joined(core, sg_ref[0, at], side_ref[5, at]))
-        ags.write(row, joined(core, ag_ref[0, at], side_ref[6, at]))
-        tars.write(row, joined(core, target_ref[0, at], side_ref[7, at]))
     for j in range(NEAR):
         con.write(rows + j, rim(4, j))
-    sgs.write(rows, rim(5, 0))
-    ags.write(rows, rim(6, 0))
-    tars.write(rows, rim(7, 0))
     for j in range(NEAR + 1):
         start = rim(6, j)
         c[0][0].write(rows + j, jnp.where(first, start, jnp.zeros_like(start)))
@@ -367,11 +376,12 @@
         row = rows - 1 - level
         nc, ng, ns = (at_level(f, level) for f in (c, g, s))
         lc, lg, ls = (at_level(f, level + 1) for f in (c, g, s))
-        to_c, to_g = stencil.fine((nc, ng), row, NEAR, False)
-        (to_s,) = stencil.fine((ns,), row, NEAR, True)
-        lc.write(row, to_c + con.read(row, NEAR))
-        lg.write(row, to_g)
-        ls.write(row, to_s)
+        for r, count in chunks(row, row + NEAR):
+            to_c, to_g = stencil.fine((nc, ng), r, count, False)
+            (to_s,) = stencil.fine((ns,), r, count, True)
+            lc.write(r, to_c + con.read(r, count))
+            lg.write(r, to_g)
+            ls.write(r, to_s)
         (to_c,) = stencil.fine((nc,), row + NEAR, 1, False)
         lc.write(row + NEAR, to_c + con.read(row + NEAR))
         if level < STEPS - 1:
@@ -380,16 +390,14 @@
     cc, dd = c[STEPS][1], s[STEPS][1]
     restore(STEPS, (cc, fg, fs, dd))
     count = NEAR + 1
-    sg = sgs.read(low, count)
+    sg = jnp.concatenate([kept_ref[1], rim(5, 0)], 0)
     gap = fc.read(low, count) - sg
     state = sg + gap
-    ag = ags.read(low, count)
-    rest = state - tars.read(low, count) - ag
+    ag = jnp.concatenate([kept_ref[2], rim(6, 0)], 0)
+    rest = state - jnp.concatenate([kept_ref[3], rim(7, 0)], 0) - ag
     cc.write(low, gap)
     dd.write(low, rest)
     base = ag + rest
-    x = fg.read(low - 1, count) + stencil.coarse(cc, low - 1, count, False)
-    e = fs.read(low - 1, count) + stencil.coarse(dd, low - 1, count, True)
 
     def cells(value, r):
         return mid(core, value[r * wide : (r + 1) * wide])
@@ -398,7 +406,9 @@
         state_out[r] = cells(state, r)
         base_out[r] = cells(base, r)
     for r in range(count):
-        x_row, e_row = cells(x, r), cells(e, r)
+        row = low - 1 + r
+        x_row = mid(core, fg.read(row) + stencil.coarse(cc, row, 1, False))
+        e_row = mid(core, fs.read(row) + stencil.coarse(dd, row, 1, True))
         z_out[r] = x_row
         z_out[count + r] = e_row
         for out in (x_out, far_out):
@@ -411,10 +421,17 @@
     late = FAR_X + FAR_E
     for j in range(LATE):
         x_out[late + j] = cells(base, NEAR - 1 - j)
-    for j in range(COEF - NEAR):
-        at = natural(rows - 1 - NEAR - j)
-        for i, value in enumerate([d_ref[at]] + [u_ref[i, at] for i in range(3)]):
-            x_out[late + LATE + i * (COEF - NEAR) + j] = value
+    kept = COEF - NEAR
+    for j in range(kept):
+        at = jnp.where(flip, j, kept - 1 - j)
+        for i in range(4):
+            x_out[late + LATE + i * kept + j] = more_ref[i * kept + at]
+
+
+def sorted_pair(core, odd, lower, higher, row, mine, mine_y, other, other_y, at):
+    a, b = joined(core, mine[at], mine_y[at]), joined(core, other[at], other_y[at])
+    lower.write(row, jnp.where(odd, b, a))
+    higher.write(row, jnp.where(odd, a, b))
 
 
 def message_kernel(rows, wide, where_ref, coef_in, za, zb, ra, rb, xr, xzr, za_y, zb_y, ra_y, rb_y, xr_y, xzr_y,
@@ -425,46 +442,41 @@
     stencil = Stencil(coef_out, wide)
     late = FAR_X + FAR_E
     for j in range(COEF - NEAR):
-        at = [late + LATE + i * (COEF - NEAR) + j for i in range(4)]
-        stencil.fill(rows + NEAR + j, [joined(core, xr[r], xr_y[late + r - late - LATE]) for r in at], space, core)
-    xa, xb, ea, eb, h = (Rows(r, wide) for r in (xa_out, xb_s, ea_s, eb_out, h_out))
-    for field in (xa, xb, ea, eb, h):
+        at = [late + i * (COEF - NEAR) + j for i in range(4)]
+        stencil.fill(rows + NEAR + j, [joined(core, xr[r + LATE], xr_y[r]) for r in at], space, core)
+    xa, xb, ea, eb, h = fields = [Rows(r, wide) for r in (xa_out, xb_s, ea_s, eb_out, h_out)]
+    for field in fields:
         field.write(-1, zeros(field))
-
-    def both(lower, higher, row, mine, mine_y, other, other_y, at):
-        a, b = joined(core, mine[at], mine_y[at]), joined(core, other[at], other_y[at])
-        lower.write(row, jnp.where(odd, b, a))
-        higher.write(row, jnp.where(odd, a, b))
-
     inner = rows - NEAR - 1
-    for row in range(rows):
-        if row < inner:
-            both(xa, xb, row, za, za_y, ra, ra_y, row)
-            both(ea, eb, row, za, za_y, ra, ra_y, inner + row)
-        else:
-            both(xa, xb, row, zb, zb_y, rb, rb_y, row - inner)
-            both(ea, eb, row, zb, zb_y, rb, rb_y, rows - inner + row - inner)
+    for row in range(inner):
+        sorted_pair(core, odd, xa, xb, row, za, za_y, ra, ra_y, row)
+        sorted_pair(core, odd, ea, eb, row, za, za_y, ra, ra_y, inner + row)
+    for row in range(inner, rows):
+        sorted_pair(core, odd, xa, xb, row, zb, zb_y, rb, rb_y, row - inner)
+        sorted_pair(core, odd, ea, eb, row, zb, zb_y, rb, rb_y, rows - inner + row - inner)
     for j in range(FAR_X):
-        both(xa, xb, rows + j, xr, xr_y, xzr, xzr_y, j)
+        sorted_pair(core, odd, xa, xb, rows + j, xr, xr_y, xzr, xzr_y, j)
     for j in range(FAR_E):
-        both(ea, eb, rows + j, xr, xr_y, xzr, xzr_y, FAR_X + j)
+        sorted_pair(core, odd, ea, eb, rows + j, xr, xr_y, xzr, xzr_y, FAR_X + j)
+
+    def send(row, count, value):
+        for r in range(row, min(row + count, rows + MSG)):
+            msg_out[r] = mid(core, value[(r - row) * wide : (r - row + 1) * wide])
 
     @pl.when(jnp.logical_not(upper))
     def _():
         for row, count in chunks(0, rows + FAR_X - 1):
-            h.write(row, xb.read(row, count) + stencil.coarse(xa, row, count, False))
-        for row in range(rows + MSG):
-            msg_out[row] = mid(core, h.read(row))
+            value = xb.read(row, count) + stencil.coarse(xa, row, count, False)
+            h.write(row, value)
+            send(row, count, value)
 
     @pl.when(upper)
     def _():
         for row, count in chunks(0, rows + FAR_E):
             h.write(row, eb.read(row, count) + stencil.coarse(xa, row, count, True))
         for row, count in chunks(0, rows + FAR_E - 1):
-            value = ea.read(row, count) + stencil.coarse(h, row, count, True)
-            for r in range(count):
-                msg_out[row + r] = mid(core, value[r * wide : (r + 1) * wide])
-        msg_out[rows + FAR_E - 1] = mid(core, zeros(ea))
+            send(row, count, ea.read(row, count) + stencil.coarse(h, row, count, True))
+        send(rows + FAR_E - 1, 1, zeros(ea))
 
 
 def base_kernel(rows, wide, where_ref, coef_ref, h_ref, xa_ref, eb_ref, start_a, start_b, start_x, base_out, t1_s, t2_s):
@@ -514,7 +526,7 @@
 
 
 def last_kernel(rows, wide, where_ref, coef_ref, msg, msg_y, base, base_y, xa_ref, state_a, state_b, control_ref,
-                state_out, gradient_out, m_s, t0_s, t1_s, total_s):
+                state_hbm, gradient_hbm, m_s, t0_s, t1_s, total_s, state_out, gradient_out, sem):
     slab, space, core = where_ref[0], where_ref[1], where_ref[2]
     stencil = Stencil(coef_ref, wide)
     m, t0, t1, total, xa = (Rows(r, wide) for r in (m_s, t0_s, t1_s, total_s, xa_ref))
@@ -527,7 +539,7 @@
     def state(came):
         for row in range(rows):
             before = state_a[row] if row < state_a.shape[0] else state_b[row - state_a.shape[0]]
-            state_out[0, natural(row)] = before + mid(core, came(row)) if came else before
+            state_out[natural(row)] = before + mid(core, came(row)) if came else before
 
     def begin(extra):
         for row, count in chunks(0, rows + LATE):
@@ -562,6 +574,8 @@
         begin(t0.read)
         state(lambda row: xa.read(row) + t0.read(row))
 
+    copies = [pltpu.make_async_copy(state_out, state_hbm.at[0], sem.at[0])]
+    copies[0].start()
     pair = (t1, m)
     for step in range(STEPS - 1):
         now, later = pair[step % 2], pair[1 - step % 2]
@@ -578,20 +592,28 @@
                     for r in range(count):
                         at = natural(row + r)
                         own = mid(core, value[r * wide : (r + 1) * wide])
-                        gradient_out[0, at] = own / float(STEPS) + 0.5 * control_ref[0, at]
-
-
-def call(kernel, outs, scratch, flops, *args, alias=None, source=pltpu.VMEM, moved=4000000):
-    whole = pl.BlockSpec(memory_space=pltpu.VMEM)
+                        gradient_out[at] = own / float(STEPS) + 0.5 * control_ref[0, at]
+                    if (row + count) % 8 and row + count < rows:
+                        continue
+                    begin_at, size = row + count - 8, 8
+                    part = pl.ds(jnp.where(space == 1, rows - begin_at - size, begin_at), size)
+                    copies.append(pltpu.make_async_copy(gradient_out.at[part], gradient_hbm.at[0, part], sem.at[len(copies)]))
+                    copies[-1].start()
+    for copy in copies:
+        copy.wait()
+
+
+def call(kernel, outs, scratch, *args, alias=None, in_hbm=0, target=pltpu.VMEM):
     return pl.pallas_call(
         kernel,
         out_shape=[jax.ShapeDtypeStruct(shape, jnp.float32) for shape in outs],
-        in_specs=[pl.BlockSpec(memory_space=pltpu.SMEM)] + [pl.BlockSpec(memory_space=source)] * (len(args) - 1),
-        out_specs=[whole] * len(outs),
+        in_specs=[pl.BlockSpec(memory_space=pltpu.SMEM)]
+        + [pl.BlockSpec(memory_space=pltpu.HBM if i < in_hbm else pltpu.VMEM) for i in range(len(args) - 1)],
+        out_specs=[pl.BlockSpec(memory_space=target)] * len(outs),
         scratch_shapes=[pltpu.VMEM(shape, jnp.float32) if isinstance(shape, tuple) else shape for shape in scratch],
         input_output_aliases=alias or {},
         compiler_params=pltpu.CompilerParams(vmem_limit_bytes=24 * 1024 * 1024),
-        cost_estimate=pl.CostEstimate(flops=flops, bytes_accessed=moved, transcendentals=0),
+        cost_estimate=pl.CostEstimate(flops=1000, bytes_accessed=1000, transcendentals=0),
     )(*args)
 
 
@@ -625,40 +647,40 @@
         return [got[e - f.shape[0] : e] for f, e in zip(fields, ends)]
 
     inputs = (diffusion, velocity, control, state_guess, adjoint_guess, initial, target)
-    x_send, side_send, *inputs = call(
+    shapes = [a.shape for a in inputs]
+    inputs = [pltpu.with_memory_space_constraint(a, pltpu.HBM) for a in inputs]
+    cells = lambda count: (count, own, depth)
+    edges = (rows, SIDE, depth)
+    kept = COEF - NEAR
+    x_send, side_send, more = call(
         functools.partial(pack_kernel, rows, own),
-        [(sum(RIMS), own, depth), (len(RIMS), rows, SIDE, depth)] + [a.shape for a in inputs],
-        [pltpu.SemaphoreType.DMA((len(inputs),)), pltpu.SemaphoreType.DMA((2 * len(RIMS),))],
-        100000,
-        where, *(pltpu.with_memory_space_constraint(a, pltpu.HBM) for a in inputs),
-        source=pltpu.HBM,
-        moved=1000,
-    )
-    diffusion, velocity, control, state_guess, adjoint_guess, initial, target = inputs
+        [cells(sum(RIMS)), (len(RIMS), *edges), cells(4 * kept)],
+        [(2, *cells(RIMS[6])), (2, *edges), pltpu.SemaphoreType.DMA((2 * len(RIMS) + 6,))],
+        where, *inputs,
+        in_hbm=len(inputs),
+    )
     x_here = swapped(x_send, "space")
     side = swapped(side_send, "yz")
     coefs = (len(NAMES), *flat(rows + COEF + 1))
     inner = rows - NEAR - 1
     tall = flat(rows + FAR_X + 2)
-    cells = lambda count: (count, own, depth)
-    coef, hist, z_a, base_a, state_a = call(
+    loaded = [shape for i, shape in enumerate(shapes) if i != 2]
+    coef, hist, last, z_a, base_a, state_a, control = call(
         functools.partial(inner_kernel, rows, wide),
-        [coefs, (4, STEPS + 1, *flat(2)), cells(2 * inner), cells(inner + 1), cells(inner + 1)],
-        [flat(rows + 2)] * 6 + [flat(rows)],
-        16000000,
+        [coefs, (4, STEPS + 1, *flat(2)), (4, *flat(NEAR)), cells(2 * inner), cells(inner + 1), cells(inner + 1), shapes[2]],
+        [flat(rows + 2)] * 6 + [flat(rows)] + loaded + [pltpu.SemaphoreType.DMA((len(inputs),))],
         where, *inputs, side,
+        in_hbm=len(inputs),
     )
     r_a = across(z_a, 1)
     x_here, coef = lax.optimization_barrier((x_here, coef))
     x_side = swapped(edge(x_here), "yz")
-    small = flat(NEAR + 5)
     count = FAR_X + FAR_E
     coef, z_b, x_out, far, base_b, state_b = call(
         functools.partial(wedge_kernel, rows, wide),
-        [coefs, cells(2 * NEAR + 2), cells(count + LATE + 4 * (COEF - NEAR)), cells(count), cells(NEAR), cells(NEAR)],
-        [small] * 6 + [flat(2 * NEAR)] + [flat(NEAR + 1)] * 3,
-        6000000,
-        where, coef, hist, diffusion, velocity, control, state_guess, adjoint_guess, target, side, z_a, x_here, x_side,
+        [coefs, cells(2 * NEAR + 2), cells(count + LATE + 4 * kept), cells(count), cells(NEAR), cells(NEAR)],
+        [flat(NEAR + 5)] * 6 + [flat(2 * NEAR)],
+        where, coef, hist, last, more, z_a, x_here, x_side,
         alias={1: 0},
     )
     x_in = swapped(x_out, "space")
@@ -670,26 +692,24 @@
         functools.partial(message_kernel, rows, wide),
         [coefs, cells(rows + MSG), tall, tall, tall],
         [tall, tall],
-        6000000,
         where, coef, z_a, z_b, r_a, r_b, x_in, xz_in, za_y, zb_y, ra_y, rb_y, xr_y, xzr_y,
         alias={1: 0},
     )
-    msg_in = across(msg, 2)
+    msg_in = across(msg, 3)
     (base,) = call(
         functools.partial(base_kernel, rows, wide),
-        [(rows + LATE, own, depth)],
+        [cells(rows + LATE)],
         [tall, tall],
-        8000000,
         where, coef, h, xa, eb, base_a, base_b, x_in,
     )
     (base_y,) = through([base], "yz")
     (msg_y,) = through([msg_in], "yz")
     return call(
         functools.partial(last_kernel, rows, wide),
-        [(1, rows, own, depth), (1, rows, own, depth)],
-        [tall] * 4,
-        8000000,
+        [(1, *cells(rows)), (1, *cells(rows))],
+        [tall] * 4 + [cells(rows)] * 2 + [pltpu.SemaphoreType.DMA((1 + rows // 8,))],
         where, coef, msg_in, msg_y, base, base_y, xa, state_a, state_b, control,
+        target=pltpu.HBM,
     )
 
 
@@ -699,7 +719,7 @@
     def local(*args):
         rows, own, depth = args[1].shape
         fits = (sizes["tm"], sizes["space"], sizes["yz"]) == (4, 2, 2)
-        fits = fits and rows >= 2 * FAR_X and own % 8 == 0 and own >= SIDE and depth % 128 == 0
+        fits = fits and rows >= 2 * FAR_X and rows % 8 == 0 and own % 8 == 0 and own >= SIDE and depth % 128 == 0
         return four_slabs(*args) if fits else any_mesh(*args)
 
     field = P(("groups", "space"), "yz", None)

time: 55.3 us -> 54.1 us (0.978)
  the two profiles are of different devices: /device:TPU:0 before, /device:TPU:17 now
where the time goes in v3:
time: 54.1 us; the launch traced here: 53.9 us
  waiting for transfers between devices  25.9 us (48%)
  Pallas kernels  15.4 us (28%)
  starting transfers between devices  11.6 us (21%)
  between operations  0.76 us (1%)
    ppermute x3, waiting for transfers between devices, across(): return lax.ppermute(block, 'tm', [(i, i ^ distance) for i in range(4)])  15.6 us
    pallas_call x6, Pallas kernels, call(): pl.pallas_call(kernel, out_shape=[jax.ShapeDtypeStruct(shape, jnp.float32...  15.4 us
    ppermute x8, starting transfers between devices, swapped(): return lax.ppermute(block, axis, [(0, 1), (1, 0)])  7.74 us
    ppermute x8, waiting for transfers between devices, swapped(): return lax.ppermute(block, axis, [(0, 1), (1, 0)])  6.36 us
    ppermute x1, waiting for transfers between devices, across_turned(): return lax.ppermute(block, ('tm', 'space'), route)  3.95 us
    ppermute x3, starting transfers between devices, across(): return lax.ppermute(block, 'tm', [(i, i ^ distance) for i in range(4)])  2.45 us
    ppermute x1, starting transfers between devices, across_turned(): return lax.ppermute(block, ('tm', 'space'), route)  1.39 us
  transfers between devices with their start and end apart: 12, of which 9 were waited for; matrix products, arithmetic and copies ran while one was open for 0% of the time, Pallas kernels for 16%

profile of v3, /device:TPU:17, one launch (start us, length us, event | category | flops | bytes accessed | tf_op | source)
XLA Modules:
  0.0 53.9 jit_solution(5885487070356620607)
XLA Ops:
  0.6 0.1 pad_add_fusion.where_ref
  0.7 2.1 %shard_map.86 = (f32[44,16,128]{2,1,0:T(8,128)S(1)}, f32[8,24,8,128]{3,2,1,0:T(8,128)S(1)}, f32[12,16,128]{2,1,0:T(8,128)S(1)}) custom-call(s32[3]{0:T(128)S(1)} %pad_add_fusion.where_ref, f32[24,16,128]{2,1,0:T(8,128)} %d_hbm.1, f32[3,24,16,128]{3,2,1,0:T(8,128)} %u_hbm.1, f32[1,24,16,128]{3,2,1,0:T(8,128)} %control_hbm.1, f32[1,24,16,128]{3,2,1,0:T(8,128)} %sg_hbm.1, ...), custom_call_target="tpu_custom_call" | custom-call | flops 1000 | bytes 1000 | tf_op jit(solution)/shard_map/pallas_call | solution.py:607
  2.9 0.7 %collective-permute-start.1 = (f32[8,24,8,128]{3,2,1,0:T(8,128)S(1)}, f32[8,24,8,128]{3,2,1,0:T(8,128)S(1)}, u32[]{:S(2)}, u32[]{:S(2)}) collective-permute-start(f32[8,24,8,128]{3,2,1,0:T(8,128)S(1)} %get-tuple-element.26), channel_id=1, source_target_pairs={{0,1},{1,0},{2,3},{3,2},{4,5},{5,4},{6,7},{7,6},{8,9},{9,8},{10,11... | collective-permute-start | bytes 2359304 | tf_op jit(solution)/shard_map/ppermute | solution.py:621
  3.6 1.2 %collective-permute-start = (f32[44,16,128]{2,1,0:T(8,128)S(1)}, f32[44,16,128]{2,1,0:T(8,128)S(1)}, u32[]{:S(2)}, u32[]{:S(2)}) collective-permute-start(f32[44,16,128]{2,1,0:T(8,128)S(1)} %get-tuple-element.25), channel_id=1, source_target_pairs={{0,2},{2,0},{1,3},{3,1},{4,6},{6,4},{5,7},{7,5},{8,10},{10,8},{9,1... | collective-permute-start | bytes 1081352 | tf_op jit(solution)/shard_map/ppermute | solution.py:621
  4.8 0.7 %collective-permute-done.1.side_ref = f32[8,24,8,128]{3,2,1,0:T(8,128)S(1)} collective-permute-done((f32[8,24,8,128]{3,2,1,0:T(8,128)S(1)}, f32[8,24,8,128]{3,2,1,0:T(8,128)S(1)}, u32[]{:S(2)}, u32[]{:S(2)}) %collective-permute-start.1) | collective-permute-done | bytes 786464 | tf_op jit(solution)/shard_map/ppermute | solution.py:621
  5.5 6.1 %shard_map.87 = (f32[11,816,128]{2,1,0:T(8,128)S(1)}, f32[4,7,48,128]{3,2,1,0:T(8,128)S(1)}, f32[4,144,128]{2,1,0:T(8,128)S(1)}, f32[34,16,128]{2,1,0:T(8,128)S(...) custom-call(s32[3]{0:T(128)S(1)} %pad_add_fusion.where_ref, ...), custom_call_target="tpu_custom_call" | custom-call | flops 1000 | bytes 1000 | tf_op jit(solution)/shard_map/pallas_call | solution.py:607
  11.6 2.0 %collective-permute-done.xr_ref = f32[44,16,128]{2,1,0:T(8,128)S(1)} collective-permute-done((f32[44,16,128]{2,1,0:T(8,128)S(1)}, f32[44,16,128]{2,1,0:T(8,128)S(1)}, u32[]{:S(2)}, u32[]{:S(2)}) %collective-permute-start) | collective-permute-done | bytes 360480 | tf_op jit(solution)/shard_map/ppermute | solution.py:621
  13.6 0.9 %collective-permute-start.2 = (f32[44,8,128]{2,1,0:T(8,128)S(1)}, f32[44,8,128]{2,1,0:T(8,128)S(1)}, u32[]{:S(2)}, u32[]{:S(2)}) collective-permute-start(f32[44,8,128]{2,1,0:T(8,128)S(1)} %constant_dynamic-slice_fusion.7), channel_id=1, source_target_pairs={{0,1},{1,0},{2,3},{3,2},{4,5},{5,4},{6,7},{7,6},{8,9},{9,8},{10,11... | collective-permute-start | bytes 540680 | tf_op jit(solution)/shard_map/ppermute | solution.py:621
  14.5 1.3 %collective-permute-start.3 = (f32[34,16,128]{2,1,0:T(8,128)S(1)}, f32[34,16,128]{2,1,0:T(8,128)S(1)}, u32[]{:S(2)}, u32[]{:S(2)}) collective-permute-start(f32[34,16,128]{2,1,0:T(8,128)S(1)} %get-tuple-element.32.z_ref.za), channel_id=1, source_target_pairs={{0,4},{4,0},{8,12},{12,8},{1,5},{5,1},{9,13},{13,9},{2,6},{6,2},{1... | collective-permute-start | bytes 835592 | tf_op jit(solution)/shard_map/ppermute | solution.py:625
  15.8 0.0 collective-permute-done.2.ys_ref
  15.9 1.8 %shard_map.88 = (f32[11,816,128]{2,1,0:T(8,128)S(1)}, f32[14,16,128]{2,1,0:T(8,128)S(1)}, f32[34,16,128]{2,1,0:T(8,128)S(1)}, f32[17,16,128]{2,1,0:T(8,128)S(1)}...) custom-call(s32[3]{0:T(128)S(1)} %pad_add_fusion.where_ref, ...), custom_call_target="tpu_custom_call", output_to_operand_aliasing={{0}: (1, {})} | custom-call | flops 1000 | bytes 1000 | tf_op jit(solution)/shard_map/pallas_call | solution.py:607
  17.6 1.1 %collective-permute-start.4 = (f32[14,16,128]{2,1,0:T(8,128)S(1)}, f32[14,16,128]{2,1,0:T(8,128)S(1)}, u32[]{:S(2)}, u32[]{:S(2)}) collective-permute-start(f32[14,16,128]{2,1,0:T(8,128)S(1)} %get-tuple-element.35.zb), channel_id=1, source_target_pairs={{0,4},{4,0},{8,12},{12,8},{1,5},{5,1},{9,13},{13,9},{2,6},{6,2},{1... | collective-permute-start | bytes 344072 | tf_op jit(solution)/shard_map/ppermute | solution.py:625
  18.7 1.4 %collective-permute-start.6 = (f32[17,16,128]{2,1,0:T(8,128)S(1)}, f32[17,16,128]{2,1,0:T(8,128)S(1)}, u32[]{:S(2)}, u32[]{:S(2)}) collective-permute-start(f32[17,16,128]{2,1,0:T(8,128)S(1)} %get-tuple-element.37), channel_id=1, source_target_pairs={{0,6},{2,4},{4,2},{6,0},{8,14},{10,12},{12,10},{14,8},{1,7},{3,5},... | collective-permute-start | bytes 417800 | tf_op jit(solution)/shard_map/ppermute | solution.py:630
  20.1 0.3 collective-permute-start.5
  20.4 2.4 %collective-permute-done.3.ra = f32[34,16,128]{2,1,0:T(8,128)S(1)} collective-permute-done((f32[34,16,128]{2,1,0:T(8,128)S(1)}, f32[34,16,128]{2,1,0:T(8,128)S(1)}, u32[]{:S(2)}, u32[]{:S(2)}) %collective-permute-start.3) | collective-permute-done | bytes 278560 | tf_op jit(solution)/shard_map/ppermute | solution.py:625
  22.8 1.4 %collective-permute-start.7 = (f32[68,8,128]{2,1,0:T(8,128)S(1)}, f32[68,8,128]{2,1,0:T(8,128)S(1)}, u32[]{:S(2)}, u32[]{:S(2)}) collective-permute-start(f32[68,8,128]{2,1,0:T(8,128)S(1)} %pad_maximum_fusion.1), channel_id=1, source_target_pairs={{0,1},{1,0},{2,3},{3,2},{4,5},{5,4},{6,7},{7,6},{8,9},{9,8},{10,11... | collective-permute-start | bytes 835592 | tf_op jit(solution)/shard_map/ppermute | solution.py:621
  24.2 1.0 %collective-permute-done.4.rb = f32[14,16,128]{2,1,0:T(8,128)S(1)} collective-permute-done((f32[14,16,128]{2,1,0:T(8,128)S(1)}, f32[14,16,128]{2,1,0:T(8,128)S(1)}, u32[]{:S(2)}, u32[]{:S(2)}) %collective-permute-start.4) | collective-permute-done | bytes 114720 | tf_op jit(solution)/shard_map/ppermute | solution.py:625
  25.2 3.9 %collective-permute-done.6.xzr = f32[17,16,128]{2,1,0:T(8,128)S(1)} collective-permute-done((f32[17,16,128]{2,1,0:T(8,128)S(1)}, f32[17,16,128]{2,1,0:T(8,128)S(1)}, u32[]{:S(2)}, u32[]{:S(2)}) %collective-permute-start.6) | collective-permute-done | bytes 139296 | tf_op jit(solution)/shard_map/ppermute | solution.py:630
  29.2 1.2 %collective-permute-done.5.xr.start_x = f32[34,16,128]{2,1,0:T(8,128)S(1)} collective-permute-done((f32[34,16,128]{2,1,0:T(8,128)S(1)}, f32[34,16,128]{2,1,0:T(8,128)S(1)}, u32[]{:S(2)}, u32[]{:S(2)}) %collective-permute-start.5) | collective-permute-done | bytes 278560 | tf_op jit(solution)/shard_map/ppermute | solution.py:621
  30.4 1.9 %collective-permute-start.8 = (f32[74,8,128]{2,1,0:T(8,128)S(1)}, f32[74,8,128]{2,1,0:T(8,128)S(1)}, u32[]{:S(2)}, u32[]{:S(2)}) collective-permute-start(f32[74,8,128]{2,1,0:T(8,128)S(1)} %pad_maximum_fusion), channel_id=1, source_target_pairs={{0,1},{1,0},{2,3},{3,2},{4,5},{5,4},{6,7},{7,6},{8,9},{9,8},{10,11... | collective-permute-start | bytes 909320 | tf_op jit(solution)/shard_map/ppermute | solution.py:621
  32.3 0.0 collective-permute-done.7
  32.3 1.2 %collective-permute-done.8 = f32[74,8,128]{2,1,0:T(8,128)S(1)} collective-permute-done((f32[74,8,128]{2,1,0:T(8,128)S(1)}, f32[74,8,128]{2,1,0:T(8,128)S(1)}, u32[]{:S(2)}, u32[]{:S(2)}) %collective-permute-start.8) | collective-permute-done | bytes 303136 | tf_op jit(solution)/shard_map/ppermute | solution.py:621
  33.6 1.3 %shard_map.89 = (f32[11,816,128]{2,1,0:T(8,128)S(1)}, f32[31,16,128]{2,1,0:T(8,128)S(1)}, f32[864,128]{1,0:T(8,128)S(1)}, f32[864,128]{1,0:T(8,128)S(1)}, f32[864,128]{1,0:T(8,128)S(1)}) custom-call(s32[3]{0:T(128)S(1)} %pad_add_fusion.where_ref, f32[11,816,128]{2,1,0:T(8,128)S(1)} %get-tuple-element.34.coef_in, ...), custom_call_target="tpu_custom_call", output_to_operand_aliasing={{0}: (1, {})} | custom-call | flops 1000 | bytes 1000 | tf_op jit(solution)/shard_map/pallas_call | solution.py:607
  34.9 0.1 collective-permute-start.9
  35.0 0.6 %shard_map.90.base = f32[29,16,128]{2,1,0:T(8,128)S(1)} custom-call(s32[3]{0:T(128)S(1)} %pad_add_fusion.where_ref, f32[11,816,128]{2,1,0:T(8,128)S(1)} %get-tuple-element.38.coef_ref, f32[864,128]{1,0:T(8,128)S(1)} %get-tuple-element.40.h_ref, f32[864,128]{1,0:T(8,128)S(1)} %get-tuple-element.41.xa_ref, f32[864,128]{1,0:T(8,128)S(1)} %get-tuple-element.42.eb_ref, ...), custom_call_target="tpu_custom_call" | custom-call | flops 1000 | bytes 1000 | tf_op jit(solution)/shard_map/pallas_call | solution.py:607
  35.6 12.2 %collective-permute-done.9.msg = f32[31,16,128]{2,1,0:T(8,128)S(1)} collective-permute-done((f32[31,16,128]{2,1,0:T(8,128)S(1)}, f32[31,16,128]{2,1,0:T(8,128)S(1)}, u32[]{:S(2)}, u32[]{:S(2)}) %collective-permute-start.9) | collective-permute-done | bytes 253984 | tf_op jit(solution)/shard_map/ppermute | solution.py:625
  47.8 1.3 %collective-permute-start.10 = (f32[31,8,128]{2,1,0:T(8,128)S(1)}, f32[31,8,128]{2,1,0:T(8,128)S(1)}, u32[]{:S(2)}, u32[]{:S(2)}) collective-permute-start(f32[31,8,128]{2,1,0:T(8,128)S(1)} %constant_dynamic-slice_fusion.1), channel_id=1, source_target_pairs={{0,1},{1,0},{2,3},{3,2},{4,5},{5,4},{6,7},{7,6},{8,9},{9,8},{10,11... | collective-permute-start | bytes 380936 | tf_op jit(solution)/shard_map/ppermute | solution.py:621
  49.0 0.1 collective-permute-start.11
  49.1 1.3 %collective-permute-done.11.base_y = f32[29,8,128]{2,1,0:T(8,128)S(1)} collective-permute-done((f32[29,8,128]{2,1,0:T(8,128)S(1)}, f32[29,8,128]{2,1,0:T(8,128)S(1)}, u32[]{:S(2)}, u32[]{:S(2)}) %collective-permute-start.11) | collective-permute-done | bytes 118816 | tf_op jit(solution)/shard_map/ppermute | solution.py:621
  50.4 0.0 collective-permute-done.10.msg_y
  50.4 3.4 %shard_map.91 = (f32[1,24,16,128]{3,2,1,0:T(8,128)}, f32[1,24,16,128]{3,2,1,0:T(8,128)}) custom-call(s32[3]{0:T(128)S(1)} %pad_add_fusion.where_ref, f32[11,816,128]{2,1,0:T(8,128)S(1)} %get-tuple-element.38.coef_ref, f32[31,16,128]{2,1,0:T(8,128)S(1)} %collective-permute-done.9.msg, f32[31,8,128]{2,1,0:T(8,128)S(1)} %collective-permute-done.10.msg_y, ...), custom_call_target="tpu_custom_call" | custom-call | flops 1000 | bytes 1000 | tf_op jit(solution)/shard_map/pallas_call | solution.py:607
  (17 shorter events, 0.2 us)
Async XLA Ops:
  2.9 2.7 %collective-permute-start.1 = (f32[8,24,8,128]{3,2,1,0:T(8,128)S(1)}, f32[8,24,8,128]{3,2,1,0:T(8,128)S(1)}, u32[]{:S(2)}, u32[]{:S(2)}) collective-permute-start(f32[8,24,8,128]{3,2,1,0:T(8,128)S(1)} %get-tuple-element.26), channel_id=1, source_target_pairs={{0,1},{1,0},{2,3},{3,2},{4,5},{5,4},{6,7},{7,6},{8,9},{9,8},{10,11... | collective-permute-start | bytes 2359304 | tf_op jit(solution)/shard_map/ppermute | solution.py:621
  3.6 10.0 %collective-permute-start = (f32[44,16,128]{2,1,0:T(8,128)S(1)}, f32[44,16,128]{2,1,0:T(8,128)S(1)}, u32[]{:S(2)}, u32[]{:S(2)}) collective-permute-start(f32[44,16,128]{2,1,0:T(8,128)S(1)} %get-tuple-element.25), channel_id=1, source_target_pairs={{0,2},{2,0},{1,3},{3,1},{4,6},{6,4},{5,7},{7,5},{8,10},{10,8},{9,1... | collective-permute-start | bytes 1081352 | tf_op jit(solution)/shard_map/ppermute | solution.py:621
  13.6 2.2 %collective-permute-start.2 = (f32[44,8,128]{2,1,0:T(8,128)S(1)}, f32[44,8,128]{2,1,0:T(8,128)S(1)}, u32[]{:S(2)}, u32[]{:S(2)}) collective-permute-start(f32[44,8,128]{2,1,0:T(8,128)S(1)} %constant_dynamic-slice_fusion.7), channel_id=1, source_target_pairs={{0,1},{1,0},{2,3},{3,2},{4,5},{5,4},{6,7},{7,6},{8,9},{9,8},{10,11... | collective-permute-start | bytes 540680 | tf_op jit(solution)/shard_map/ppermute | solution.py:621
  14.5 8.2 %collective-permute-start.3 = (f32[34,16,128]{2,1,0:T(8,128)S(1)}, f32[34,16,128]{2,1,0:T(8,128)S(1)}, u32[]{:S(2)}, u32[]{:S(2)}) collective-permute-start(f32[34,16,128]{2,1,0:T(8,128)S(1)} %get-tuple-element.32.z_ref.za), channel_id=1, source_target_pairs={{0,4},{4,0},{8,12},{12,8},{1,5},{5,1},{9,13},{13,9},{2,6},{6,2},{1... | collective-permute-start | bytes 835592 | tf_op jit(solution)/shard_map/ppermute | solution.py:625
  17.6 7.6 %collective-permute-start.4 = (f32[14,16,128]{2,1,0:T(8,128)S(1)}, f32[14,16,128]{2,1,0:T(8,128)S(1)}, u32[]{:S(2)}, u32[]{:S(2)}) collective-permute-start(f32[14,16,128]{2,1,0:T(8,128)S(1)} %get-tuple-element.35.zb), channel_id=1, source_target_pairs={{0,4},{4,0},{8,12},{12,8},{1,5},{5,1},{9,13},{13,9},{2,6},{6,2},{1... | collective-permute-start | bytes 344072 | tf_op jit(solution)/shard_map/ppermute | solution.py:625
  18.7 10.5 %collective-permute-start.6 = (f32[17,16,128]{2,1,0:T(8,128)S(1)}, f32[17,16,128]{2,1,0:T(8,128)S(1)}, u32[]{:S(2)}, u32[]{:S(2)}) collective-permute-start(f32[17,16,128]{2,1,0:T(8,128)S(1)} %get-tuple-element.37), channel_id=1, source_target_pairs={{0,6},{2,4},{4,2},{6,0},{8,14},{10,12},{12,10},{14,8},{1,7},{3,5},... | collective-permute-start | bytes 417800 | tf_op jit(solution)/shard_map/ppermute | solution.py:630
  20.1 10.2 %collective-permute-start.5 = (f32[34,16,128]{2,1,0:T(8,128)S(1)}, f32[34,16,128]{2,1,0:T(8,128)S(1)}, u32[]{:S(2)}, u32[]{:S(2)}) collective-permute-start(f32[34,16,128]{2,1,0:T(8,128)S(1)} %get-tuple-element.36), channel_id=1, source_target_pairs={{0,2},{2,0},{1,3},{3,1},{4,6},{6,4},{5,7},{7,5},{8,10},{10,8},{9,1... | collective-permute-start | bytes 835592 | tf_op jit(solution)/shard_map/ppermute | solution.py:621
  22.8 9.5 %collective-permute-start.7 = (f32[68,8,128]{2,1,0:T(8,128)S(1)}, f32[68,8,128]{2,1,0:T(8,128)S(1)}, u32[]{:S(2)}, u32[]{:S(2)}) collective-permute-start(f32[68,8,128]{2,1,0:T(8,128)S(1)} %pad_maximum_fusion.1), channel_id=1, source_target_pairs={{0,1},{1,0},{2,3},{3,2},{4,5},{5,4},{6,7},{7,6},{8,9},{9,8},{10,11... | collective-permute-start | bytes 835592 | tf_op jit(solution)/shard_map/ppermute | solution.py:621
  30.4 3.1 %collective-permute-start.8 = (f32[74,8,128]{2,1,0:T(8,128)S(1)}, f32[74,8,128]{2,1,0:T(8,128)S(1)}, u32[]{:S(2)}, u32[]{:S(2)}) collective-permute-start(f32[74,8,128]{2,1,0:T(8,128)S(1)} %pad_maximum_fusion), channel_id=1, source_target_pairs={{0,1},{1,0},{2,3},{3,2},{4,5},{5,4},{6,7},{7,6},{8,9},{9,8},{10,11... | collective-permute-start | bytes 909320 | tf_op jit(solution)/shard_map/ppermute | solution.py:621
  34.9 12.9 %collective-permute-start.9 = (f32[31,16,128]{2,1,0:T(8,128)S(1)}, f32[31,16,128]{2,1,0:T(8,128)S(1)}, u32[]{:S(2)}, u32[]{:S(2)}) collective-permute-start(f32[31,16,128]{2,1,0:T(8,128)S(1)} %get-tuple-element.39), channel_id=1, source_target_pairs={{0,12},{4,8},{8,4},{12,0},{1,13},{5,9},{9,5},{13,1},{2,14},{6,10},... | collective-permute-start | bytes 761864 | tf_op jit(solution)/shard_map/ppermute | solution.py:625
  47.8 2.7 %collective-permute-start.10 = (f32[31,8,128]{2,1,0:T(8,128)S(1)}, f32[31,8,128]{2,1,0:T(8,128)S(1)}, u32[]{:S(2)}, u32[]{:S(2)}) collective-permute-start(f32[31,8,128]{2,1,0:T(8,128)S(1)} %constant_dynamic-slice_fusion.1), channel_id=1, source_target_pairs={{0,1},{1,0},{2,3},{3,2},{4,5},{5,4},{6,7},{7,6},{8,9},{9,8},{10,11... | collective-permute-start | bytes 380936 | tf_op jit(solution)/shard_map/ppermute | solution.py:621
  49.0 1.4 %collective-permute-start.11 = (f32[29,8,128]{2,1,0:T(8,128)S(1)}, f32[29,8,128]{2,1,0:T(8,128)S(1)}, u32[]{:S(2)}, u32[]{:S(2)}) collective-permute-start(f32[29,8,128]{2,1,0:T(8,128)S(1)} %constant_dynamic-slice_fusion), channel_id=1, source_target_pairs={{0,1},{1,0},{2,3},{3,2},{4,5},{5,4},{6,7},{7,6},{8,9},{9,8},{10,11... | collective-permute-start | bytes 356360 | tf_op jit(solution)/shard_map/ppermute | solution.py:621

commit v4 on v3

--- a/solution.py
+++ b/solution.py
@@ -641,10 +641,10 @@
     def flat(count):
         return (count * wide, depth)
 
-    def through(fields, axis):
-        got = swapped(jnp.concatenate([edge(f) for f in fields], 0), axis)
-        ends = [sum(f.shape[0] for f in fields[: i + 1]) for i in range(len(fields))]
-        return [got[e - f.shape[0] : e] for f, e in zip(fields, ends)]
+    def sent(*groups):
+        sizes = [sum(e.shape[0] for e in group) for group in groups]
+        got = swapped(jnp.concatenate([e for group in groups for e in group], 0), "yz")
+        return [got[sum(sizes[:i]) : sum(sizes[: i + 1])] for i in range(len(sizes))]
 
     inputs = (diffusion, velocity, control, state_guess, adjoint_guess, initial, target)
     shapes = [a.shape for a in inputs]
@@ -686,8 +686,10 @@
     x_in = swapped(x_out, "space")
     xz_in = across_turned(far, 1)
     r_b = across(z_b, 1)
-    za_y, ra_y = through([z_a, r_a], "yz")
-    zb_y, rb_y, xr_y, xzr_y = through([z_b, r_b, jnp.concatenate([x_in[:count], x_in[count + LATE :]], 0), xz_in], "yz")
+    za_y, ra_y = sent([edge(z_a)], [edge(r_a)])
+    x_edge, xz_in, r_b = lax.optimization_barrier((edge(x_in), xz_in, r_b))
+    xz_edge, r_b = lax.optimization_barrier((edge(xz_in), r_b))
+    xr_y, xzr_y, zb_y, rb_y = sent([x_edge[:count], x_edge[count + LATE :]], [xz_edge], [edge(z_b)], [edge(r_b)])
     coef, msg, h, xa, eb = call(
         functools.partial(message_kernel, rows, wide),
         [coefs, cells(rows + MSG), tall, tall, tall],
@@ -702,8 +704,9 @@
         [tall, tall],
         where, coef, h, xa, eb, base_a, base_b, x_in,
     )
-    (base_y,) = through([base], "yz")
-    (msg_y,) = through([msg_in], "yz")
+    base_y = swapped(edge(base), "yz")
+    msg_in, base_y = lax.optimization_barrier((msg_in, base_y))
+    msg_y = swapped(edge(msg_in), "yz")
     return call(
         functools.partial(last_kernel, rows, wide),
         [(1, *cells(rows)), (1, *cells(rows))],

time: 54.1 us -> 51.5 us (0.952)
  waiting for transfers between devices: 25.9 us -> 23.7 us
    ppermute x3, waiting for transfers between devices: 15.6 us -> 12.9 us  [across(): return lax.ppermute(block, 'tm', [(i, i ^ distance) for i in range(4)])]
    ppermute x1, starting transfers between devices: 1.39 us -> 0.41 us  [across_turned(): return lax.ppermute(block, ('tm', 'space'), route)]
    ppermute x8, waiting for transfers between devices: 6.36 us -> 7.25 us  [swapped(): return lax.ppermute(block, axis, [(0, 1), (1, 0)])]
    ppermute x8, starting transfers between devices: 7.74 us -> 8.32 us  [swapped(): return lax.ppermute(block, axis, [(0, 1), (1, 0)])]
where the time goes in v4:
time: 51.5 us; the launch traced here: 51.3 us
  waiting for transfers between devices  23.7 us (46%)
  Pallas kernels  15.3 us (30%)
  starting transfers between devices  11.2 us (22%)
  between operations  0.78 us (2%)
    pallas_call x6, Pallas kernels, call(): pl.pallas_call(kernel, out_shape=[jax.ShapeDtypeStruct(shape, jnp.float32...  15.3 us
    ppermute x3, waiting for transfers between devices, across(): return lax.ppermute(block, 'tm', [(i, i ^ distance) for i in range(4)])  12.9 us
    ppermute x8, starting transfers between devices, swapped(): return lax.ppermute(block, axis, [(0, 1), (1, 0)])  8.32 us
    ppermute x8, waiting for transfers between devices, swapped(): return lax.ppermute(block, axis, [(0, 1), (1, 0)])  7.25 us
    ppermute x1, waiting for transfers between devices, across_turned(): return lax.ppermute(block, ('tm', 'space'), route)  3.53 us
    ppermute x3, starting transfers between devices, across(): return lax.ppermute(block, 'tm', [(i, i ^ distance) for i in range(4)])  2.48 us
  transfers between devices with their start and end apart: 12, of which 9 were waited for; matrix products, arithmetic and copies ran while one was open for 0% of the time, Pallas kernels for 16%

profile of v4, /device:TPU:17, one launch (start us, length us, event | category | flops | bytes accessed | tf_op | source)
XLA Modules:
  0.0 51.3 jit_solution(1707898747912120277)
XLA Ops:
  0.6 0.1 pad_add_fusion.where_ref
  0.7 2.1 %shard_map.86 = (f32[44,16,128]{2,1,0:T(8,128)S(1)}, f32[8,24,8,128]{3,2,1,0:T(8,128)S(1)}, f32[12,16,128]{2,1,0:T(8,128)S(1)}) custom-call(s32[3]{0:T(128)S(1)} %pad_add_fusion.where_ref, f32[24,16,128]{2,1,0:T(8,128)} %d_hbm.1, f32[3,24,16,128]{3,2,1,0:T(8,128)} %u_hbm.1, f32[1,24,16,128]{3,2,1,0:T(8,128)} %control_hbm.1, f32[1,24,16,128]{3,2,1,0:T(8,128)} %sg_hbm.1, ...), custom_call_target="tpu_custom_call" | custom-call | flops 1000 | bytes 1000 | tf_op jit(solution)/shard_map/pallas_call | solution.py:607
  2.9 0.7 %collective-permute-start.1 = (f32[8,24,8,128]{3,2,1,0:T(8,128)S(1)}, f32[8,24,8,128]{3,2,1,0:T(8,128)S(1)}, u32[]{:S(2)}, u32[]{:S(2)}) collective-permute-start(f32[8,24,8,128]{3,2,1,0:T(8,128)S(1)} %get-tuple-element.33), channel_id=1, source_target_pairs={{0,1},{1,0},{2,3},{3,2},{4,5},{5,4},{6,7},{7,6},{8,9},{9,8},{10,11... | collective-permute-start | bytes 2359304 | tf_op jit(solution)/shard_map/ppermute | solution.py:621
  3.6 1.2 %collective-permute-start = (f32[44,16,128]{2,1,0:T(8,128)S(1)}, f32[44,16,128]{2,1,0:T(8,128)S(1)}, u32[]{:S(2)}, u32[]{:S(2)}) collective-permute-start(f32[44,16,128]{2,1,0:T(8,128)S(1)} %get-tuple-element.32), channel_id=1, source_target_pairs={{0,2},{2,0},{1,3},{3,1},{4,6},{6,4},{5,7},{7,5},{8,10},{10,8},{9,1... | collective-permute-start | bytes 1081352 | tf_op jit(solution)/shard_map/ppermute | solution.py:621
  4.8 0.7 %collective-permute-done.1.side_ref = f32[8,24,8,128]{3,2,1,0:T(8,128)S(1)} collective-permute-done((f32[8,24,8,128]{3,2,1,0:T(8,128)S(1)}, f32[8,24,8,128]{3,2,1,0:T(8,128)S(1)}, u32[]{:S(2)}, u32[]{:S(2)}) %collective-permute-start.1) | collective-permute-done | bytes 786464 | tf_op jit(solution)/shard_map/ppermute | solution.py:621
  5.5 6.1 %shard_map.87 = (f32[11,816,128]{2,1,0:T(8,128)S(1)}, f32[4,7,48,128]{3,2,1,0:T(8,128)S(1)}, f32[4,144,128]{2,1,0:T(8,128)S(1)}, f32[34,16,128]{2,1,0:T(8,128)S(...) custom-call(s32[3]{0:T(128)S(1)} %pad_add_fusion.where_ref, ...), custom_call_target="tpu_custom_call" | custom-call | flops 1000 | bytes 1000 | tf_op jit(solution)/shard_map/pallas_call | solution.py:607
  11.6 2.0 %collective-permute-done.xr_ref = f32[44,16,128]{2,1,0:T(8,128)S(1)} collective-permute-done((f32[44,16,128]{2,1,0:T(8,128)S(1)}, f32[44,16,128]{2,1,0:T(8,128)S(1)}, u32[]{:S(2)}, u32[]{:S(2)}) %collective-permute-start) | collective-permute-done | bytes 360480 | tf_op jit(solution)/shard_map/ppermute | solution.py:621
  13.6 0.9 %collective-permute-start.2 = (f32[44,8,128]{2,1,0:T(8,128)S(1)}, f32[44,8,128]{2,1,0:T(8,128)S(1)}, u32[]{:S(2)}, u32[]{:S(2)}) collective-permute-start(f32[44,8,128]{2,1,0:T(8,128)S(1)} %constant_dynamic-slice_fusion.6), channel_id=1, source_target_pairs={{0,1},{1,0},{2,3},{3,2},{4,5},{5,4},{6,7},{7,6},{8,9},{9,8},{10,11... | collective-permute-start | bytes 540680 | tf_op jit(solution)/shard_map/ppermute | solution.py:621
  14.5 1.3 %collective-permute-start.3 = (f32[34,16,128]{2,1,0:T(8,128)S(1)}, f32[34,16,128]{2,1,0:T(8,128)S(1)}, u32[]{:S(2)}, u32[]{:S(2)}) collective-permute-start(f32[34,16,128]{2,1,0:T(8,128)S(1)} %get-tuple-element.39.z_ref.za), channel_id=1, source_target_pairs={{0,4},{4,0},{8,12},{12,8},{1,5},{5,1},{9,13},{13,9},{2,6},{6,2},{1... | collective-permute-start | bytes 835592 | tf_op jit(solution)/shard_map/ppermute | solution.py:625
  15.8 0.0 collective-permute-done.2.ys_ref
  15.8 1.8 %shard_map.88 = (f32[11,816,128]{2,1,0:T(8,128)S(1)}, f32[14,16,128]{2,1,0:T(8,128)S(1)}, f32[34,16,128]{2,1,0:T(8,128)S(1)}, f32[17,16,128]{2,1,0:T(8,128)S(1)}...) custom-call(s32[3]{0:T(128)S(1)} %pad_add_fusion.where_ref, ...), custom_call_target="tpu_custom_call", output_to_operand_aliasing={{0}: (1, {})} | custom-call | flops 1000 | bytes 1000 | tf_op jit(solution)/shard_map/pallas_call | solution.py:607
  17.6 1.3 %collective-permute-start.4 = (f32[34,16,128]{2,1,0:T(8,128)S(1)}, f32[34,16,128]{2,1,0:T(8,128)S(1)}, u32[]{:S(2)}, u32[]{:S(2)}) collective-permute-start(f32[34,16,128]{2,1,0:T(8,128)S(1)} %get-tuple-element.43), channel_id=1, source_target_pairs={{0,2},{2,0},{1,3},{3,1},{4,6},{6,4},{5,7},{7,5},{8,10},{10,8},{9,1... | collective-permute-start | bytes 835592 | tf_op jit(solution)/shard_map/ppermute | solution.py:621
  18.9 1.1 %collective-permute-start.6 = (f32[14,16,128]{2,1,0:T(8,128)S(1)}, f32[14,16,128]{2,1,0:T(8,128)S(1)}, u32[]{:S(2)}, u32[]{:S(2)}) collective-permute-start(f32[14,16,128]{2,1,0:T(8,128)S(1)} %get-tuple-element.42.zb), channel_id=1, source_target_pairs={{0,4},{4,0},{8,12},{12,8},{1,5},{5,1},{9,13},{13,9},{2,6},{6,2},{1... | collective-permute-start | bytes 344072 | tf_op jit(solution)/shard_map/ppermute | solution.py:625
  20.0 0.4 collective-permute-start.5
  20.4 2.4 %collective-permute-done.3.ra = f32[34,16,128]{2,1,0:T(8,128)S(1)} collective-permute-done((f32[34,16,128]{2,1,0:T(8,128)S(1)}, f32[34,16,128]{2,1,0:T(8,128)S(1)}, u32[]{:S(2)}, u32[]{:S(2)}) %collective-permute-start.3) | collective-permute-done | bytes 278560 | tf_op jit(solution)/shard_map/ppermute | solution.py:625
  22.8 1.4 %collective-permute-start.7 = (f32[68,8,128]{2,1,0:T(8,128)S(1)}, f32[68,8,128]{2,1,0:T(8,128)S(1)}, u32[]{:S(2)}, u32[]{:S(2)}) collective-permute-start(f32[68,8,128]{2,1,0:T(8,128)S(1)} %pad_maximum_fusion), channel_id=1, source_target_pairs={{0,1},{1,0},{2,3},{3,2},{4,5},{5,4},{6,7},{7,6},{8,9},{9,8},{10,11... | collective-permute-start | bytes 835592 | tf_op jit(solution)/shard_map/ppermute | solution.py:621
  24.2 1.4 %collective-permute-done.4.xr.start_x = f32[34,16,128]{2,1,0:T(8,128)S(1)} collective-permute-done((f32[34,16,128]{2,1,0:T(8,128)S(1)}, f32[34,16,128]{2,1,0:T(8,128)S(1)}, u32[]{:S(2)}, u32[]{:S(2)}) %collective-permute-start.4) | collective-permute-done | bytes 278560 | tf_op jit(solution)/shard_map/ppermute | solution.py:621
  25.6 0.0 collective-permute-done.6.rb
  25.6 3.5 %collective-permute-done.5.xzr = f32[17,16,128]{2,1,0:T(8,128)S(1)} collective-permute-done((f32[17,16,128]{2,1,0:T(8,128)S(1)}, f32[17,16,128]{2,1,0:T(8,128)S(1)}, u32[]{:S(2)}, u32[]{:S(2)}) %collective-permute-start.5) | collective-permute-done | bytes 139296 | tf_op jit(solution)/shard_map/ppermute | solution.py:630
  29.2 0.9 %collective-permute-start.8 = (f32[74,8,128]{2,1,0:T(8,128)S(1)}, f32[74,8,128]{2,1,0:T(8,128)S(1)}, u32[]{:S(2)}, u32[]{:S(2)}) collective-permute-start(f32[74,8,128]{2,1,0:T(8,128)S(1)} %dynamic-slice_dynamic-update-slice_fusion), channel_id=1, source_target_pairs={{0,1},{1,0},{2,3},{3,2},{4,5},{5,4},{6,7},{7,6},{8,9},{9,8},{10,11... | collective-permute-start | bytes 909320 | tf_op jit(solution)/shard_map/ppermute | solution.py:621
  30.1 0.0 collective-permute-done.7
  30.2 1.2 %collective-permute-done.8 = f32[74,8,128]{2,1,0:T(8,128)S(1)} collective-permute-done((f32[74,8,128]{2,1,0:T(8,128)S(1)}, f32[74,8,128]{2,1,0:T(8,128)S(1)}, u32[]{:S(2)}, u32[]{:S(2)}) %collective-permute-start.8) | collective-permute-done | bytes 303136 | tf_op jit(solution)/shard_map/ppermute | solution.py:621
  31.4 1.3 %shard_map.89 = (f32[11,816,128]{2,1,0:T(8,128)S(1)}, f32[31,16,128]{2,1,0:T(8,128)S(1)}, f32[864,128]{1,0:T(8,128)S(1)}, f32[864,128]{1,0:T(8,128)S(1)}, f32[864,128]{1,0:T(8,128)S(1)}) custom-call(s32[3]{0:T(128)S(1)} %pad_add_fusion.where_ref, f32[11,816,128]{2,1,0:T(8,128)S(1)} %get-tuple-element.41.coef_in, ...), custom_call_target="tpu_custom_call", output_to_operand_aliasing={{0}: (1, {})} | custom-call | flops 1000 | bytes 1000 | tf_op jit(solution)/shard_map/pallas_call | solution.py:607
  32.7 0.1 collective-permute-start.9
  32.8 0.6 %shard_map.90.base = f32[29,16,128]{2,1,0:T(8,128)S(1)} custom-call(s32[3]{0:T(128)S(1)} %pad_add_fusion.where_ref, f32[11,816,128]{2,1,0:T(8,128)S(1)} %get-tuple-element.50.coef_ref, f32[864,128]{1,0:T(8,128)S(1)} %get-tuple-element.52.h_ref, f32[864,128]{1,0:T(8,128)S(1)} %get-tuple-element.53.xa_ref, f32[864,128]{1,0:T(8,128)S(1)} %get-tuple-element.54.eb_ref, ...), custom_call_target="tpu_custom_call" | custom-call | flops 1000 | bytes 1000 | tf_op jit(solution)/shard_map/pallas_call | solution.py:607
  33.4 0.6 %collective-permute-start.10 = (f32[29,8,128]{2,1,0:T(8,128)S(1)}, f32[29,8,128]{2,1,0:T(8,128)S(1)}, u32[]{:S(2)}, u32[]{:S(2)}) collective-permute-start(f32[29,8,128]{2,1,0:T(8,128)S(1)} %constant_dynamic-slice_fusion.1), channel_id=1, source_target_pairs={{0,1},{1,0},{2,3},{3,2},{4,5},{5,4},{6,7},{7,6},{8,9},{9,8},{10,11... | collective-permute-start | bytes 356360 | tf_op jit(solution)/shard_map/ppermute | solution.py:621
  34.0 1.0 %collective-permute-done.10.base_y = f32[29,8,128]{2,1,0:T(8,128)S(1)} collective-permute-done((f32[29,8,128]{2,1,0:T(8,128)S(1)}, f32[29,8,128]{2,1,0:T(8,128)S(1)}, u32[]{:S(2)}, u32[]{:S(2)}) %collective-permute-start.10) | collective-permute-done | bytes 118816 | tf_op jit(solution)/shard_map/ppermute | solution.py:621
  35.0 10.6 %collective-permute-done.9.msg = f32[31,16,128]{2,1,0:T(8,128)S(1)} collective-permute-done((f32[31,16,128]{2,1,0:T(8,128)S(1)}, f32[31,16,128]{2,1,0:T(8,128)S(1)}, u32[]{:S(2)}, u32[]{:S(2)}) %collective-permute-start.9) | collective-permute-done | bytes 253984 | tf_op jit(solution)/shard_map/ppermute | solution.py:625
  45.6 1.3 %collective-permute-start.11 = (f32[31,8,128]{2,1,0:T(8,128)S(1)}, f32[31,8,128]{2,1,0:T(8,128)S(1)}, u32[]{:S(2)}, u32[]{:S(2)}) collective-permute-start(f32[31,8,128]{2,1,0:T(8,128)S(1)} %constant_dynamic-slice_fusion), channel_id=1, source_target_pairs={{0,1},{1,0},{2,3},{3,2},{4,5},{5,4},{6,7},{7,6},{8,9},{9,8},{10,11... | collective-permute-start | bytes 380936 | tf_op jit(solution)/shard_map/ppermute | solution.py:621
  46.9 1.0 %collective-permute-done.11.msg_y = f32[31,8,128]{2,1,0:T(8,128)S(1)} collective-permute-done((f32[31,8,128]{2,1,0:T(8,128)S(1)}, f32[31,8,128]{2,1,0:T(8,128)S(1)}, u32[]{:S(2)}, u32[]{:S(2)}) %collective-permute-start.11) | collective-permute-done | bytes 127008 | tf_op jit(solution)/shard_map/ppermute | solution.py:621
  47.8 3.4 %shard_map.91 = (f32[1,24,16,128]{3,2,1,0:T(8,128)}, f32[1,24,16,128]{3,2,1,0:T(8,128)}) custom-call(s32[3]{0:T(128)S(1)} %pad_add_fusion.where_ref, f32[11,816,128]{2,1,0:T(8,128)S(1)} %get-tuple-element.50.coef_ref, f32[31,16,128]{2,1,0:T(8,128)S(1)} %collective-permute-done.9.msg, f32[31,8,128]{2,1,0:T(8,128)S(1)} %collective-permute-done.11.msg_y, ...), custom_call_target="tpu_custom_call" | custom-call | flops 1000 | bytes 1000 | tf_op jit(solution)/shard_map/pallas_call | solution.py:607
  (17 shorter events, 0.2 us)
Async XLA Ops:
  2.9 2.7 %collective-permute-start.1 = (f32[8,24,8,128]{3,2,1,0:T(8,128)S(1)}, f32[8,24,8,128]{3,2,1,0:T(8,128)S(1)}, u32[]{:S(2)}, u32[]{:S(2)}) collective-permute-start(f32[8,24,8,128]{3,2,1,0:T(8,128)S(1)} %get-tuple-element.33), channel_id=1, source_target_pairs={{0,1},{1,0},{2,3},{3,2},{4,5},{5,4},{6,7},{7,6},{8,9},{9,8},{10,11... | collective-permute-start | bytes 2359304 | tf_op jit(solution)/shard_map/ppermute | solution.py:621
  3.6 10.0 %collective-permute-start = (f32[44,16,128]{2,1,0:T(8,128)S(1)}, f32[44,16,128]{2,1,0:T(8,128)S(1)}, u32[]{:S(2)}, u32[]{:S(2)}) collective-permute-start(f32[44,16,128]{2,1,0:T(8,128)S(1)} %get-tuple-element.32), channel_id=1, source_target_pairs={{0,2},{2,0},{1,3},{3,1},{4,6},{6,4},{5,7},{7,5},{8,10},{10,8},{9,1... | collective-permute-start | bytes 1081352 | tf_op jit(solution)/shard_map/ppermute | solution.py:621
  13.6 2.2 %collective-permute-start.2 = (f32[44,8,128]{2,1,0:T(8,128)S(1)}, f32[44,8,128]{2,1,0:T(8,128)S(1)}, u32[]{:S(2)}, u32[]{:S(2)}) collective-permute-start(f32[44,8,128]{2,1,0:T(8,128)S(1)} %constant_dynamic-slice_fusion.6), channel_id=1, source_target_pairs={{0,1},{1,0},{2,3},{3,2},{4,5},{5,4},{6,7},{7,6},{8,9},{9,8},{10,11... | collective-permute-start | bytes 540680 | tf_op jit(solution)/shard_map/ppermute | solution.py:621
  14.5 8.2 %collective-permute-start.3 = (f32[34,16,128]{2,1,0:T(8,128)S(1)}, f32[34,16,128]{2,1,0:T(8,128)S(1)}, u32[]{:S(2)}, u32[]{:S(2)}) collective-permute-start(f32[34,16,128]{2,1,0:T(8,128)S(1)} %get-tuple-element.39.z_ref.za), channel_id=1, source_target_pairs={{0,4},{4,0},{8,12},{12,8},{1,5},{5,1},{9,13},{13,9},{2,6},{6,2},{1... | collective-permute-start | bytes 835592 | tf_op jit(solution)/shard_map/ppermute | solution.py:625
  17.6 8.0 %collective-permute-start.4 = (f32[34,16,128]{2,1,0:T(8,128)S(1)}, f32[34,16,128]{2,1,0:T(8,128)S(1)}, u32[]{:S(2)}, u32[]{:S(2)}) collective-permute-start(f32[34,16,128]{2,1,0:T(8,128)S(1)} %get-tuple-element.43), channel_id=1, source_target_pairs={{0,2},{2,0},{1,3},{3,1},{4,6},{6,4},{5,7},{7,5},{8,10},{10,8},{9,1... | collective-permute-start | bytes 835592 | tf_op jit(solution)/shard_map/ppermute | solution.py:621
  18.9 6.7 %collective-permute-start.6 = (f32[14,16,128]{2,1,0:T(8,128)S(1)}, f32[14,16,128]{2,1,0:T(8,128)S(1)}, u32[]{:S(2)}, u32[]{:S(2)}) collective-permute-start(f32[14,16,128]{2,1,0:T(8,128)S(1)} %get-tuple-element.42.zb), channel_id=1, source_target_pairs={{0,4},{4,0},{8,12},{12,8},{1,5},{5,1},{9,13},{13,9},{2,6},{6,2},{1... | collective-permute-start | bytes 344072 | tf_op jit(solution)/shard_map/ppermute | solution.py:625
  20.0 9.1 %collective-permute-start.5 = (f32[17,16,128]{2,1,0:T(8,128)S(1)}, f32[17,16,128]{2,1,0:T(8,128)S(1)}, u32[]{:S(2)}, u32[]{:S(2)}) collective-permute-start(f32[17,16,128]{2,1,0:T(8,128)S(1)} %get-tuple-element.44), channel_id=1, source_target_pairs={{0,6},{2,4},{4,2},{6,0},{8,14},{10,12},{12,10},{14,8},{1,7},{3,5},... | collective-permute-start | bytes 417800 | tf_op jit(solution)/shard_map/ppermute | solution.py:630
  22.8 7.3 %collective-permute-start.7 = (f32[68,8,128]{2,1,0:T(8,128)S(1)}, f32[68,8,128]{2,1,0:T(8,128)S(1)}, u32[]{:S(2)}, u32[]{:S(2)}) collective-permute-start(f32[68,8,128]{2,1,0:T(8,128)S(1)} %pad_maximum_fusion), channel_id=1, source_target_pairs={{0,1},{1,0},{2,3},{3,2},{4,5},{5,4},{6,7},{7,6},{8,9},{9,8},{10,11... | collective-permute-start | bytes 835592 | tf_op jit(solution)/shard_map/ppermute | solution.py:621
  29.2 2.1 %collective-permute-start.8 = (f32[74,8,128]{2,1,0:T(8,128)S(1)}, f32[74,8,128]{2,1,0:T(8,128)S(1)}, u32[]{:S(2)}, u32[]{:S(2)}) collective-permute-start(f32[74,8,128]{2,1,0:T(8,128)S(1)} %dynamic-slice_dynamic-update-slice_fusion), channel_id=1, source_target_pairs={{0,1},{1,0},{2,3},{3,2},{4,5},{5,4},{6,7},{7,6},{8,9},{9,8},{10,11... | collective-permute-start | bytes 909320 | tf_op jit(solution)/shard_map/ppermute | solution.py:621
  32.7 12.9 %collective-permute-start.9 = (f32[31,16,128]{2,1,0:T(8,128)S(1)}, f32[31,16,128]{2,1,0:T(8,128)S(1)}, u32[]{:S(2)}, u32[]{:S(2)}) collective-permute-start(f32[31,16,128]{2,1,0:T(8,128)S(1)} %get-tuple-element.51), channel_id=1, source_target_pairs={{0,12},{4,8},{8,4},{12,0},{1,13},{5,9},{9,5},{13,1},{2,14},{6,10},... | collective-permute-start | bytes 761864 | tf_op jit(solution)/shard_map/ppermute | solution.py:625
  33.4 1.6 %collective-permute-start.10 = (f32[29,8,128]{2,1,0:T(8,128)S(1)}, f32[29,8,128]{2,1,0:T(8,128)S(1)}, u32[]{:S(2)}, u32[]{:S(2)}) collective-permute-start(f32[29,8,128]{2,1,0:T(8,128)S(1)} %constant_dynamic-slice_fusion.1), channel_id=1, source_target_pairs={{0,1},{1,0},{2,3},{3,2},{4,5},{5,4},{6,7},{7,6},{8,9},{9,8},{10,11... | collective-permute-start | bytes 356360 | tf_op jit(solution)/shard_map/ppermute | solution.py:621
  45.6 2.2 %collective-permute-start.11 = (f32[31,8,128]{2,1,0:T(8,128)S(1)}, f32[31,8,128]{2,1,0:T(8,128)S(1)}, u32[]{:S(2)}, u32[]{:S(2)}) collective-permute-start(f32[31,8,128]{2,1,0:T(8,128)S(1)} %constant_dynamic-slice_fusion), channel_id=1, source_target_pairs={{0,1},{1,0},{2,3},{3,2},{4,5},{5,4},{6,7},{7,6},{8,9},{9,8},{10,11... | collective-permute-start | bytes 380936 | tf_op jit(solution)/shard_map/ppermute | solution.py:621

commit v5 on v4

--- a/solution.py
+++ b/solution.py
@@ -12,9 +12,8 @@
 NEAR = 6
 LATE = 5
 MSG = 7
-FAR_X = 10
-FAR_E = 7
-COEF = FAR_X - 1
+FAR_X = 5
+FAR_E = 1
 RIMS = (NEAR, NEAR, NEAR, NEAR, NEAR, NEAR, NEAR + 1, 1)
 STARTS = tuple(sum(RIMS[:i]) for i in range(len(RIMS)))
 
@@ -225,7 +224,7 @@
 
 
 def pack_kernel(rows, own, where_ref, d_ref, u_ref, control_ref, sg_ref, ag_ref, initial_ref, target_ref,
-                x_out, side_out, more_out, rims, sides, sem):
+                x_out, side_out, rims, sides, sem):
     slab, space, core = where_ref[0], where_ref[1], where_ref[2]
     fields = (d_ref, u_ref.at[0], u_ref.at[1], u_ref.at[2], control_ref.at[0], sg_ref.at[0], None, target_ref.at[0])
     starts = (ag_ref.at[0], initial_ref)
@@ -249,9 +248,6 @@
         if field is not None:
             bring(field.at[rim(i)], x_out.at[pl.ds(STARTS[i], RIMS[i])])
             bring(edge(field), side_out.at[i])
-    kept = COEF - NEAR
-    for i, field in enumerate(fields[:4]):
-        bring(field.at[pl.ds(jnp.where(space == 0, rows - COEF, NEAR), kept)], more_out.at[pl.ds(i * kept, kept)])
     for copy in copies:
         copy.wait()
     x_out[pl.ds(STARTS[6], RIMS[6])] = jnp.where(slab == 0, rims[1], rims[0])
@@ -334,8 +330,8 @@
             z_out[ready - 1 + row + r] = mid(core, e[r * wide : (r + 1) * wide])
 
 
-def wedge_kernel(rows, wide, where_ref, coef_in, hist_ref, kept_ref, more_ref, z_ref, xr_ref, ys_ref,
-                 coef_out, z_out, x_out, far_out, base_out, state_out, c_a, c_b, g_a, g_b, s_a, s_b, con_ref):
+def wedge_kernel(rows, wide, where_ref, coef_in, hist_ref, kept_ref, xr_ref, ys_ref,
+                 coef_out, z_out, x_out, base_out, state_out, c_a, c_b, g_a, g_b, s_a, s_b, con_ref):
     slab, space, core = where_ref[0], where_ref[1], where_ref[2]
     first = slab == 0
     flip = space == 1
@@ -411,21 +407,10 @@
         e_row = mid(core, fs.read(row) + stencil.coarse(dd, row, 1, True))
         z_out[r] = x_row
         z_out[count + r] = e_row
-        for out in (x_out, far_out):
-            out[count - 1 - r] = x_row
-            out[FAR_X + count - 1 - r] = e_row
-    for j in range(count, FAR_X):
-        x_row = z_ref[rows - 1 - j]
-        for out in (x_out, far_out):
-            out[j] = x_row
-    late = FAR_X + FAR_E
-    for j in range(LATE):
-        x_out[late + j] = cells(base, NEAR - 1 - j)
-    kept = COEF - NEAR
-    for j in range(kept):
-        at = jnp.where(flip, j, kept - 1 - j)
-        for i in range(4):
-            x_out[late + LATE + i * kept + j] = more_ref[i * kept + at]
+        if count - 1 - r < FAR_X:
+            x_out[count - 1 - r] = x_row
+        if count - 1 - r < FAR_E:
+            x_out[FAR_X + count - 1 - r] = e_row
 
 
 def sorted_pair(core, odd, lower, higher, row, mine, mine_y, other, other_y, at):
@@ -434,16 +419,12 @@
     higher.write(row, jnp.where(odd, a, b))
 
 
-def message_kernel(rows, wide, where_ref, coef_in, za, zb, ra, rb, xr, xzr, za_y, zb_y, ra_y, rb_y, xr_y, xzr_y,
-                   coef_out, msg_out, h_out, xa_out, eb_out, xb_s, ea_s):
+def message_kernel(rows, wide, where_ref, coef_ref, za, zb, ra, rb, xr, xzr, za_y, zb_y, ra_y, rb_y, xr_y, xzr_y,
+                   msg_out, turn_out, h_out, xa_out, eb_out, xb_s, ea_s):
     slab, space, core = where_ref[0], where_ref[1], where_ref[2]
     odd = slab % 2 == 1
     upper = slab >= 2
-    stencil = Stencil(coef_out, wide)
-    late = FAR_X + FAR_E
-    for j in range(COEF - NEAR):
-        at = [late + i * (COEF - NEAR) + j for i in range(4)]
-        stencil.fill(rows + NEAR + j, [joined(core, xr[r + LATE], xr_y[r]) for r in at], space, core)
+    stencil = Stencil(coef_ref, wide)
     xa, xb, ea, eb, h = fields = [Rows(r, wide) for r in (xa_out, xb_s, ea_s, eb_out, h_out)]
     for field in fields:
         field.write(-1, zeros(field))
@@ -460,8 +441,11 @@
         sorted_pair(core, odd, ea, eb, rows + j, xr, xr_y, xzr, xzr_y, FAR_X + j)
 
     def send(row, count, value):
-        for r in range(row, min(row + count, rows + MSG)):
-            msg_out[r] = mid(core, value[(r - row) * wide : (r - row + 1) * wide])
+        for r in range(row, min(row + count, rows)):
+            cells = mid(core, value[(r - row) * wide : (r - row + 1) * wide])
+            msg_out[r] = cells
+            if r >= rows - MSG:
+                turn_out[rows - 1 - r] = cells
 
     @pl.when(jnp.logical_not(upper))
     def _():
@@ -472,14 +456,13 @@
 
     @pl.when(upper)
     def _():
-        for row, count in chunks(0, rows + FAR_E):
+        for row, count in chunks(0, rows + 1):
             h.write(row, eb.read(row, count) + stencil.coarse(xa, row, count, True))
-        for row, count in chunks(0, rows + FAR_E - 1):
+        for row, count in chunks(0, rows):
             send(row, count, ea.read(row, count) + stencil.coarse(h, row, count, True))
-        send(rows + FAR_E - 1, 1, zeros(ea))
-
-
-def base_kernel(rows, wide, where_ref, coef_ref, h_ref, xa_ref, eb_ref, start_a, start_b, start_x, base_out, t1_s, t2_s):
+
+
+def base_kernel(rows, wide, where_ref, coef_ref, h_ref, xa_ref, eb_ref, start_a, start_b, base_out, edge_out, t1_s, t2_s):
     slab, core = where_ref[0], where_ref[2]
     odd = slab % 2 == 1
     upper = slab >= 2
@@ -488,14 +471,13 @@
     for field in (t1, t2):
         field.write(-1, zeros(field))
 
-    def start(row):
-        if row >= rows:
-            return start_x[FAR_X + FAR_E + row - rows]
-        return start_a[row] if row < start_a.shape[0] else start_b[row - start_a.shape[0]]
-
     def put(source):
-        for row in range(rows + LATE):
-            base_out[row] = start(row) + mid(core, source.read(row))
+        for row in range(rows):
+            start = start_a[row] if row < start_a.shape[0] else start_b[row - start_a.shape[0]]
+            value = start + mid(core, source.read(row))
+            base_out[row] = value
+            if row >= rows - LATE:
+                edge_out[rows - 1 - row] = value
 
     @pl.when(jnp.logical_not(upper))
     def _():
@@ -512,7 +494,7 @@
 
         @pl.when(jnp.logical_not(odd))
         def _():
-            for row, count in chunks(0, rows + LATE):
+            for row, count in chunks(0, rows):
                 t2.write(row, eb.read(row, count) + stencil.coarse(t1, row, count, True))
             put(t2)
 
@@ -651,19 +633,18 @@
     inputs = [pltpu.with_memory_space_constraint(a, pltpu.HBM) for a in inputs]
     cells = lambda count: (count, own, depth)
     edges = (rows, SIDE, depth)
-    kept = COEF - NEAR
-    x_send, side_send, more = call(
+    x_send, side_send = call(
         functools.partial(pack_kernel, rows, own),
-        [cells(sum(RIMS)), (len(RIMS), *edges), cells(4 * kept)],
-        [(2, *cells(RIMS[6])), (2, *edges), pltpu.SemaphoreType.DMA((2 * len(RIMS) + 6,))],
+        [cells(sum(RIMS)), (len(RIMS), *edges)],
+        [(2, *cells(RIMS[6])), (2, *edges), pltpu.SemaphoreType.DMA((2 * len(RIMS) + 2,))],
         where, *inputs,
         in_hbm=len(inputs),
     )
     x_here = swapped(x_send, "space")
     side = swapped(side_send, "yz")
-    coefs = (len(NAMES), *flat(rows + COEF + 1))
+    coefs = (len(NAMES), *flat(rows + NEAR + 1))
     inner = rows - NEAR - 1
-    tall = flat(rows + FAR_X + 2)
+    tall = flat(rows + MSG + 2)
     loaded = [shape for i, shape in enumerate(shapes) if i != 2]
     coef, hist, last, z_a, base_a, state_a, control = call(
         functools.partial(inner_kernel, rows, wide),
@@ -675,38 +656,36 @@
     r_a = across(z_a, 1)
     x_here, coef = lax.optimization_barrier((x_here, coef))
     x_side = swapped(edge(x_here), "yz")
-    count = FAR_X + FAR_E
-    coef, z_b, x_out, far, base_b, state_b = call(
+    coef, z_b, x_out, base_b, state_b = call(
         functools.partial(wedge_kernel, rows, wide),
-        [coefs, cells(2 * NEAR + 2), cells(count + LATE + 4 * kept), cells(count), cells(NEAR), cells(NEAR)],
+        [coefs, cells(2 * NEAR + 2), cells(FAR_X + FAR_E), cells(NEAR), cells(NEAR)],
         [flat(NEAR + 5)] * 6 + [flat(2 * NEAR)],
-        where, coef, hist, last, more, z_a, x_here, x_side,
+        where, coef, hist, last, x_here, x_side,
         alias={1: 0},
     )
     x_in = swapped(x_out, "space")
-    xz_in = across_turned(far, 1)
+    xz_in = across_turned(x_out, 1)
     r_b = across(z_b, 1)
     za_y, ra_y = sent([edge(z_a)], [edge(r_a)])
-    x_edge, xz_in, r_b = lax.optimization_barrier((edge(x_in), xz_in, r_b))
-    xz_edge, r_b = lax.optimization_barrier((edge(xz_in), r_b))
-    xr_y, xzr_y, zb_y, rb_y = sent([x_edge[:count], x_edge[count + LATE :]], [xz_edge], [edge(z_b)], [edge(r_b)])
-    coef, msg, h, xa, eb = call(
+    xr_y, xzr_y, zb_y, rb_y = sent([edge(x_in)], [edge(xz_in)], [edge(z_b)], [edge(r_b)])
+    msg, turn, h, xa, eb = call(
         functools.partial(message_kernel, rows, wide),
-        [coefs, cells(rows + MSG), tall, tall, tall],
+        [cells(rows), cells(MSG), tall, tall, tall],
         [tall, tall],
         where, coef, z_a, z_b, r_a, r_b, x_in, xz_in, za_y, zb_y, ra_y, rb_y, xr_y, xzr_y,
-        alias={1: 0},
     )
     msg_in = across(msg, 3)
-    (base,) = call(
+    turn_in = across_turned(turn, 3)
+    base, base_edge = call(
         functools.partial(base_kernel, rows, wide),
-        [cells(rows + LATE)],
+        [cells(rows), cells(LATE)],
         [tall, tall],
-        where, coef, h, xa, eb, base_a, base_b, x_in,
-    )
-    base_y = swapped(edge(base), "yz")
-    msg_in, base_y = lax.optimization_barrier((msg_in, base_y))
-    msg_y = swapped(edge(msg_in), "yz")
+        where, coef, h, xa, eb, base_a, base_b,
+    )
+    base_x = swapped(base_edge, "space")
+    msg_in, base_x = lax.optimization_barrier((jnp.concatenate([msg_in, turn_in], 0), base_x))
+    base = jnp.concatenate([base, base_x], 0)
+    msg_y, base_y = sent([edge(msg_in)], [edge(base)])
     return call(
         functools.partial(last_kernel, rows, wide),
         [(1, *cells(rows)), (1, *cells(rows))],
@@ -722,7 +701,7 @@
     def local(*args):
         rows, own, depth = args[1].shape
         fits = (sizes["tm"], sizes["space"], sizes["yz"]) == (4, 2, 2)
-        fits = fits and rows >= 2 * FAR_X and rows % 8 == 0 and own % 8 == 0 and own >= SIDE and depth % 128 == 0
+        fits = fits and rows >= 2 * (NEAR + 1) and rows % 8 == 0 and own % 8 == 0 and own >= SIDE and depth % 128 == 0
         return four_slabs(*args) if fits else any_mesh(*args)
 
     field = P(("groups", "space"), "yz", None)

time: 51.5 us -> 50.1 us (0.973)
  waiting for transfers between devices: 23.7 us -> 21.9 us
    ppermute x1 -> x2, waiting for transfers between devices: 3.53 us -> 15 us  [across_turned(): return lax.ppermute(block, ('tm', 'space'), route)]
    ppermute x3, waiting for transfers between devices: 12.9 us -> 1.52 us  [across(): return lax.ppermute(block, 'tm', [(i, i ^ distance) for i in range(4)])]
    ppermute x1 -> x2, starting transfers between devices: 0.41 us -> 4.38 us  [across_turned(): return lax.ppermute(block, ('tm', 'space'), route)]
    ppermute x8, starting transfers between devices: 8.32 us -> 5.49 us  [swapped(): return lax.ppermute(block, axis, [(0, 1), (1, 0)])]
    ppermute x8, waiting for transfers between devices: 7.25 us -> 5.35 us  [swapped(): return lax.ppermute(block, axis, [(0, 1), (1, 0)])]
    ppermute x3, starting transfers between devices: 2.48 us -> 1.84 us  [across(): return lax.ppermute(block, 'tm', [(i, i ^ distance) for i in range(4)])]
  transfers between devices with their start and end apart: 12 -> 13, of which waited for: 9 -> 8; matrix products, arithmetic and copies ran while one was open for 0% -> 0% of each run, Pallas kernels for 16% -> 17%
where the time goes in v5:
time: 50.1 us; the launch traced here: 49.9 us
  waiting for transfers between devices  21.9 us (44%)
  Pallas kernels  15.2 us (30%)
  starting transfers between devices  11.7 us (23%)
  between operations  0.79 us (2%)
    pallas_call x6, Pallas kernels, call(): pl.pallas_call(kernel, out_shape=[jax.ShapeDtypeStruct(shape, jnp.float32...  15.2 us
    ppermute x2, waiting for transfers between devices, across_turned(): return lax.ppermute(block, ('tm', 'space'), route)  15 us
    ppermute x8, starting transfers between devices, swapped(): return lax.ppermute(block, axis, [(0, 1), (1, 0)])  5.49 us
    ppermute x8, waiting for transfers between devices, swapped(): return lax.ppermute(block, axis, [(0, 1), (1, 0)])  5.35 us
    ppermute x2, starting transfers between devices, across_turned(): return lax.ppermute(block, ('tm', 'space'), route)  4.38 us
    ppermute x3, starting transfers between devices, across(): return lax.ppermute(block, 'tm', [(i, i ^ distance) for i in range(4)])  1.84 us
    ppermute x3, waiting for transfers between devices, across(): return lax.ppermute(block, 'tm', [(i, i ^ distance) for i in range(4)])  1.52 us
  transfers between devices with their start and end apart: 13, of which 8 were waited for; matrix products, arithmetic and copies ran while one was open for 0% of the time, Pallas kernels for 17%

profile of v5, /device:TPU:17, one launch (start us, length us, event | category | flops | bytes accessed | tf_op | source)
XLA Modules:
  0.0 49.9 jit_solution(12557863543240206224)
XLA Ops:
  0.6 0.1 pad_add_fusion.where_ref
  0.7 2.1 %shard_map.86 = (f32[44,16,128]{2,1,0:T(8,128)S(1)}, f32[8,24,8,128]{3,2,1,0:T(8,128)S(1)}) custom-call(s32[3]{0:T(128)S(1)} %pad_add_fusion.where_ref, f32[24,16,128]{2,1,0:T(8,128)} %d_hbm.1, f32[3,24,16,128]{3,2,1,0:T(8,128)} %u_hbm.1, f32[1,24,16,128]{3,2,1,0:T(8,128)} %control_hbm.1, f32[1,24,16,128]{3,2,1,0:T(8,128)} %sg_hbm.1, ...), custom_call_target="tpu_custom_call" | custom-call | flops 1000 | bytes 1000 | tf_op jit(solution)/shard_map/pallas_call | solution.py:589
  2.8 0.7 %collective-permute-start.1 = (f32[8,24,8,128]{3,2,1,0:T(8,128)S(1)}, f32[8,24,8,128]{3,2,1,0:T(8,128)S(1)}, u32[]{:S(2)}, u32[]{:S(2)}) collective-permute-start(f32[8,24,8,128]{3,2,1,0:T(8,128)S(1)} %get-tuple-element.28), channel_id=1, source_target_pairs={{0,1},{1,0},{2,3},{3,2},{4,5},{5,4},{6,7},{7,6},{8,9},{9,8},{10,11... | collective-permute-start | bytes 2359304 | tf_op jit(solution)/shard_map/ppermute | solution.py:603
  3.6 1.2 %collective-permute-start = (f32[44,16,128]{2,1,0:T(8,128)S(1)}, f32[44,16,128]{2,1,0:T(8,128)S(1)}, u32[]{:S(2)}, u32[]{:S(2)}) collective-permute-start(f32[44,16,128]{2,1,0:T(8,128)S(1)} %get-tuple-element.27), channel_id=1, source_target_pairs={{0,2},{2,0},{1,3},{3,1},{4,6},{6,4},{5,7},{7,5},{8,10},{10,8},{9,1... | collective-permute-start | bytes 1081352 | tf_op jit(solution)/shard_map/ppermute | solution.py:603
  4.8 0.7 %collective-permute-done.1.side_ref = f32[8,24,8,128]{3,2,1,0:T(8,128)S(1)} collective-permute-done((f32[8,24,8,128]{3,2,1,0:T(8,128)S(1)}, f32[8,24,8,128]{3,2,1,0:T(8,128)S(1)}, u32[]{:S(2)}, u32[]{:S(2)}) %collective-permute-start.1) | collective-permute-done | bytes 786464 | tf_op jit(solution)/shard_map/ppermute | solution.py:603
  5.5 6.1 %shard_map.87 = (f32[11,744,128]{2,1,0:T(8,128)S(1)}, f32[4,7,48,128]{3,2,1,0:T(8,128)S(1)}, f32[4,144,128]{2,1,0:T(8,128)S(1)}, f32[34,16,128]{2,1,0:T(8,128)S(...) custom-call(s32[3]{0:T(128)S(1)} %pad_add_fusion.where_ref, ...), custom_call_target="tpu_custom_call" | custom-call | flops 1000 | bytes 1000 | tf_op jit(solution)/shard_map/pallas_call | solution.py:589
  11.5 2.0 %collective-permute-done.xr_ref = f32[44,16,128]{2,1,0:T(8,128)S(1)} collective-permute-done((f32[44,16,128]{2,1,0:T(8,128)S(1)}, f32[44,16,128]{2,1,0:T(8,128)S(1)}, u32[]{:S(2)}, u32[]{:S(2)}) %collective-permute-start) | collective-permute-done | bytes 360480 | tf_op jit(solution)/shard_map/ppermute | solution.py:603
  13.6 0.9 %collective-permute-start.2 = (f32[44,8,128]{2,1,0:T(8,128)S(1)}, f32[44,8,128]{2,1,0:T(8,128)S(1)}, u32[]{:S(2)}, u32[]{:S(2)}) collective-permute-start(f32[44,8,128]{2,1,0:T(8,128)S(1)} %constant_dynamic-slice_fusion.8), channel_id=1, source_target_pairs={{0,1},{1,0},{2,3},{3,2},{4,5},{5,4},{6,7},{7,6},{8,9},{9,8},{10,11... | collective-permute-start | bytes 540680 | tf_op jit(solution)/shard_map/ppermute | solution.py:603
  14.5 1.3 %collective-permute-start.3 = (f32[34,16,128]{2,1,0:T(8,128)S(1)}, f32[34,16,128]{2,1,0:T(8,128)S(1)}, u32[]{:S(2)}, u32[]{:S(2)}) collective-permute-start(f32[34,16,128]{2,1,0:T(8,128)S(1)} %get-tuple-element.35.za), channel_id=1, source_target_pairs={{0,4},{4,0},{8,12},{12,8},{1,5},{5,1},{9,13},{13,9},{2,6},{6,2},{1... | collective-permute-start | bytes 835592 | tf_op jit(solution)/shard_map/ppermute | solution.py:607
  15.8 0.0 collective-permute-done.2.ys_ref
  15.8 1.8 %shard_map.88 = (f32[11,744,128]{2,1,0:T(8,128)S(1)}, f32[14,16,128]{2,1,0:T(8,128)S(1)}, f32[6,16,128]{2,1,0:T(8,128)S(1)}, f32[6,16,128]{2,1,0:T(8,128)S(1)}, f32[6,16,128]{2,1,0:T(8,128)S(1)}) custom-call(s32[3]{0:T(128)S(1)} %pad_add_fusion.where_ref, f32[11,744,128]{2,1,0:T(8,128)S(1)} %get-tuple-element.30.coef_in, ...), custom_call_target="tpu_custom_call", output_to_operand_aliasing={{0}: (1, {})} | custom-call | flops 1000 | bytes 1000 | tf_op jit(solution)/shard_map/pallas_call | solution.py:589
  17.6 2.0 %collective-permute-start.6 = (f32[6,16,128]{2,1,0:T(8,128)S(1)}, f32[6,16,128]{2,1,0:T(8,128)S(1)}, u32[]{:S(2)}, u32[]{:S(2)}) collective-permute-start(f32[6,16,128]{2,1,0:T(8,128)S(1)} %get-tuple-element.37), channel_id=1, source_target_pairs={{0,6},{2,4},{4,2},{6,0},{8,14},{10,12},{12,10},{14,8},{1,7},{3,5},... | collective-permute-start | bytes 147464 | tf_op jit(solution)/shard_map/ppermute | solution.py:612
  19.6 0.3 collective-permute-start.5
  19.9 0.5 collective-permute-start.4
  20.3 4.4 %collective-permute-done.6.xzr = f32[6,16,128]{2,1,0:T(8,128)S(1)} collective-permute-done((f32[6,16,128]{2,1,0:T(8,128)S(1)}, f32[6,16,128]{2,1,0:T(8,128)S(1)}, u32[]{:S(2)}, u32[]{:S(2)}) %collective-permute-start.6) | collective-permute-done | bytes 49184 | tf_op jit(solution)/shard_map/ppermute | solution.py:612
  24.7 0.0 collective-permute-done.5.xr
  24.7 1.5 %collective-permute-done.4.rb = f32[14,16,128]{2,1,0:T(8,128)S(1)} collective-permute-done((f32[14,16,128]{2,1,0:T(8,128)S(1)}, f32[14,16,128]{2,1,0:T(8,128)S(1)}, u32[]{:S(2)}, u32[]{:S(2)}) %collective-permute-start.4) | collective-permute-done | bytes 114720 | tf_op jit(solution)/shard_map/ppermute | solution.py:607
  26.3 0.9 %collective-permute-start.8 = (f32[40,8,128]{2,1,0:T(8,128)S(1)}, f32[40,8,128]{2,1,0:T(8,128)S(1)}, u32[]{:S(2)}, u32[]{:S(2)}) collective-permute-start(f32[40,8,128]{2,1,0:T(8,128)S(1)} %pad_maximum_fusion.3), channel_id=1, source_target_pairs={{0,1},{1,0},{2,3},{3,2},{4,5},{5,4},{6,7},{7,6},{8,9},{9,8},{10,11... | collective-permute-start | bytes 491528 | tf_op jit(solution)/shard_map/ppermute | solution.py:603
  27.2 0.0 collective-permute-done.3.ra
  27.2 0.1 collective-permute-start.7
  27.3 0.9 %collective-permute-done.8 = f32[40,8,128]{2,1,0:T(8,128)S(1)} collective-permute-done((f32[40,8,128]{2,1,0:T(8,128)S(1)}, f32[40,8,128]{2,1,0:T(8,128)S(1)}, u32[]{:S(2)}, u32[]{:S(2)}) %collective-permute-start.8) | collective-permute-done | bytes 163872 | tf_op jit(solution)/shard_map/ppermute | solution.py:603
  28.2 0.6 %collective-permute-done.7 = f32[68,8,128]{2,1,0:T(8,128)S(1)} collective-permute-done((f32[68,8,128]{2,1,0:T(8,128)S(1)}, f32[68,8,128]{2,1,0:T(8,128)S(1)}, u32[]{:S(2)}, u32[]{:S(2)}) %collective-permute-start.7) | collective-permute-done | bytes 278560 | tf_op jit(solution)/shard_map/ppermute | solution.py:603
  28.9 1.2 %shard_map.89 = (f32[24,16,128]{2,1,0:T(8,128)S(1)}, f32[7,16,128]{2,1,0:T(8,128)S(1)}, f32[792,128]{1,0:T(8,128)S(1)}, f32[792,128]{1,0:T(8,128)S(1)}, f32[792,128]{1,0:T(8,128)S(1)}) custom-call(s32[3]{0:T(128)S(1)} %pad_add_fusion.where_ref, f32[11,744,128]{2,1,0:T(8,128)S(1)} %get-tuple-element.34.coef_ref, f32[34,16,128]{2,1,0:T(8,128)S(1)} %get-tuple-element.35.za, ...), custom_call_target="tpu_custom_call" | custom-call | flops 1000 | bytes 1000 | tf_op jit(solution)/shard_map/pallas_call | solution.py:589
  30.1 0.1 collective-permute-start.9
  30.2 2.4 %collective-permute-start.10 = (f32[7,16,128]{2,1,0:T(8,128)S(1)}, f32[7,16,128]{2,1,0:T(8,128)S(1)}, u32[]{:S(2)}, u32[]{:S(2)}) collective-permute-start(f32[7,16,128]{2,1,0:T(8,128)S(1)} %get-tuple-element.39), channel_id=1, source_target_pairs={{0,14},{2,12},{4,10},{6,8},{8,6},{10,4},{12,2},{14,0},{1,15},{3,13... | collective-permute-start | bytes 172040 | tf_op jit(solution)/shard_map/ppermute | solution.py:612
  32.6 0.6 %shard_map.90 = (f32[24,16,128]{2,1,0:T(8,128)S(1)}, f32[5,16,128]{2,1,0:T(8,128)S(1)}) custom-call(s32[3]{0:T(128)S(1)} %pad_add_fusion.where_ref, f32[11,744,128]{2,1,0:T(8,128)S(1)} %get-tuple-element.34.coef_ref, f32[792,128]{1,0:T(8,128)S(1)} %get-tuple-element.40.h_ref, f32[792,128]{1,0:T(8,128)S(1)} %get-tuple-element.41.xa_ref, ...), custom_call_target="tpu_custom_call" | custom-call | flops 1000 | bytes 1000 | tf_op jit(solution)/shard_map/pallas_call | solution.py:589
  33.2 0.3 collective-permute-start.11
  33.5 10.6 %collective-permute-done.10 = f32[7,16,128]{2,1,0:T(8,128)S(1)} collective-permute-done((f32[7,16,128]{2,1,0:T(8,128)S(1)}, f32[7,16,128]{2,1,0:T(8,128)S(1)}, u32[]{:S(2)}, u32[]{:S(2)}) %collective-permute-start.10) | collective-permute-done | bytes 57376 | tf_op jit(solution)/shard_map/ppermute | solution.py:612
  44.1 0.0 collective-permute-done.9
  44.2 0.0 collective-permute-done.11
  44.3 1.0 %collective-permute-start.12 = (f32[60,8,128]{2,1,0:T(8,128)S(1)}, f32[60,8,128]{2,1,0:T(8,128)S(1)}, u32[]{:S(2)}, u32[]{:S(2)}) collective-permute-start(f32[60,8,128]{2,1,0:T(8,128)S(1)} %pad_maximum_fusion.2), channel_id=1, source_target_pairs={{0,1},{1,0},{2,3},{3,2},{4,5},{5,4},{6,7},{7,6},{8,9},{9,8},{10,11... | collective-permute-start | bytes 737288 | tf_op jit(solution)/shard_map/ppermute | solution.py:603
  45.3 1.1 %collective-permute-done.12 = f32[60,8,128]{2,1,0:T(8,128)S(1)} collective-permute-done((f32[60,8,128]{2,1,0:T(8,128)S(1)}, f32[60,8,128]{2,1,0:T(8,128)S(1)}, u32[]{:S(2)}, u32[]{:S(2)}) %collective-permute-start.12) | collective-permute-done | bytes 245792 | tf_op jit(solution)/shard_map/ppermute | solution.py:603
  46.5 3.4 %shard_map.91 = (f32[1,24,16,128]{3,2,1,0:T(8,128)}, f32[1,24,16,128]{3,2,1,0:T(8,128)}) custom-call(s32[3]{0:T(128)S(1)} %pad_add_fusion.where_ref, f32[11,744,128]{2,1,0:T(8,128)S(1)} %get-tuple-element.34.coef_ref, f32[31,16,128]{2,1,0:T(8,128)S(1)} %pad_maximum_fusion.1.msg, f32[31,8,128]{2,1,0:T(8,128)S(1)} %slice.38.msg_y, ...), custom_call_target="tpu_custom_call" | custom-call | flops 1000 | bytes 1000 | tf_op jit(solution)/shard_map/pallas_call | solution.py:589
  (20 shorter events, 0.2 us)
Async XLA Ops:
  2.8 2.7 %collective-permute-start.1 = (f32[8,24,8,128]{3,2,1,0:T(8,128)S(1)}, f32[8,24,8,128]{3,2,1,0:T(8,128)S(1)}, u32[]{:S(2)}, u32[]{:S(2)}) collective-permute-start(f32[8,24,8,128]{3,2,1,0:T(8,128)S(1)} %get-tuple-element.28), channel_id=1, source_target_pairs={{0,1},{1,0},{2,3},{3,2},{4,5},{5,4},{6,7},{7,6},{8,9},{9,8},{10,11... | collective-permute-start | bytes 2359304 | tf_op jit(solution)/shard_map/ppermute | solution.py:603
  3.6 10.0 %collective-permute-start = (f32[44,16,128]{2,1,0:T(8,128)S(1)}, f32[44,16,128]{2,1,0:T(8,128)S(1)}, u32[]{:S(2)}, u32[]{:S(2)}) collective-permute-start(f32[44,16,128]{2,1,0:T(8,128)S(1)} %get-tuple-element.27), channel_id=1, source_target_pairs={{0,2},{2,0},{1,3},{3,1},{4,6},{6,4},{5,7},{7,5},{8,10},{10,8},{9,1... | collective-permute-start | bytes 1081352 | tf_op jit(solution)/shard_map/ppermute | solution.py:603
  13.6 2.2 %collective-permute-start.2 = (f32[44,8,128]{2,1,0:T(8,128)S(1)}, f32[44,8,128]{2,1,0:T(8,128)S(1)}, u32[]{:S(2)}, u32[]{:S(2)}) collective-permute-start(f32[44,8,128]{2,1,0:T(8,128)S(1)} %constant_dynamic-slice_fusion.8), channel_id=1, source_target_pairs={{0,1},{1,0},{2,3},{3,2},{4,5},{5,4},{6,7},{7,6},{8,9},{9,8},{10,11... | collective-permute-start | bytes 540680 | tf_op jit(solution)/shard_map/ppermute | solution.py:603
  14.5 12.7 %collective-permute-start.3 = (f32[34,16,128]{2,1,0:T(8,128)S(1)}, f32[34,16,128]{2,1,0:T(8,128)S(1)}, u32[]{:S(2)}, u32[]{:S(2)}) collective-permute-start(f32[34,16,128]{2,1,0:T(8,128)S(1)} %get-tuple-element.35.za), channel_id=1, source_target_pairs={{0,4},{4,0},{8,12},{12,8},{1,5},{5,1},{9,13},{13,9},{2,6},{6,2},{1... | collective-permute-start | bytes 835592 | tf_op jit(solution)/shard_map/ppermute | solution.py:607
  17.6 7.1 %collective-permute-start.6 = (f32[6,16,128]{2,1,0:T(8,128)S(1)}, f32[6,16,128]{2,1,0:T(8,128)S(1)}, u32[]{:S(2)}, u32[]{:S(2)}) collective-permute-start(f32[6,16,128]{2,1,0:T(8,128)S(1)} %get-tuple-element.37), channel_id=1, source_target_pairs={{0,6},{2,4},{4,2},{6,0},{8,14},{10,12},{12,10},{14,8},{1,7},{3,5},... | collective-permute-start | bytes 147464 | tf_op jit(solution)/shard_map/ppermute | solution.py:612
  19.6 5.1 %collective-permute-start.5 = (f32[6,16,128]{2,1,0:T(8,128)S(1)}, f32[6,16,128]{2,1,0:T(8,128)S(1)}, u32[]{:S(2)}, u32[]{:S(2)}) collective-permute-start(f32[6,16,128]{2,1,0:T(8,128)S(1)} %get-tuple-element.37), channel_id=1, source_target_pairs={{0,2},{2,0},{1,3},{3,1},{4,6},{6,4},{5,7},{7,5},{8,10},{10,8},{9,1... | collective-permute-start | bytes 147464 | tf_op jit(solution)/shard_map/ppermute | solution.py:603
  19.9 6.4 %collective-permute-start.4 = (f32[14,16,128]{2,1,0:T(8,128)S(1)}, f32[14,16,128]{2,1,0:T(8,128)S(1)}, u32[]{:S(2)}, u32[]{:S(2)}) collective-permute-start(f32[14,16,128]{2,1,0:T(8,128)S(1)} %get-tuple-element.36.zb), channel_id=1, source_target_pairs={{0,4},{4,0},{8,12},{12,8},{1,5},{5,1},{9,13},{13,9},{2,6},{6,2},{1... | collective-permute-start | bytes 344072 | tf_op jit(solution)/shard_map/ppermute | solution.py:607
  26.3 1.9 %collective-permute-start.8 = (f32[40,8,128]{2,1,0:T(8,128)S(1)}, f32[40,8,128]{2,1,0:T(8,128)S(1)}, u32[]{:S(2)}, u32[]{:S(2)}) collective-permute-start(f32[40,8,128]{2,1,0:T(8,128)S(1)} %pad_maximum_fusion.3), channel_id=1, source_target_pairs={{0,1},{1,0},{2,3},{3,2},{4,5},{5,4},{6,7},{7,6},{8,9},{9,8},{10,11... | collective-permute-start | bytes 491528 | tf_op jit(solution)/shard_map/ppermute | solution.py:603
  27.2 1.6 %collective-permute-start.7 = (f32[68,8,128]{2,1,0:T(8,128)S(1)}, f32[68,8,128]{2,1,0:T(8,128)S(1)}, u32[]{:S(2)}, u32[]{:S(2)}) collective-permute-start(f32[68,8,128]{2,1,0:T(8,128)S(1)} %pad_maximum_fusion), channel_id=1, source_target_pairs={{0,1},{1,0},{2,3},{3,2},{4,5},{5,4},{6,7},{7,6},{8,9},{9,8},{10,11... | collective-permute-start | bytes 835592 | tf_op jit(solution)/shard_map/ppermute | solution.py:603
  30.1 14.0 %collective-permute-start.9 = (f32[24,16,128]{2,1,0:T(8,128)S(1)}, f32[24,16,128]{2,1,0:T(8,128)S(1)}, u32[]{:S(2)}, u32[]{:S(2)}) collective-permute-start(f32[24,16,128]{2,1,0:T(8,128)S(1)} %get-tuple-element.38), channel_id=1, source_target_pairs={{0,12},{4,8},{8,4},{12,0},{1,13},{5,9},{9,5},{13,1},{2,14},{6,10},... | collective-permute-start | bytes 589832 | tf_op jit(solution)/shard_map/ppermute | solution.py:607
  30.2 13.9 %collective-permute-start.10 = (f32[7,16,128]{2,1,0:T(8,128)S(1)}, f32[7,16,128]{2,1,0:T(8,128)S(1)}, u32[]{:S(2)}, u32[]{:S(2)}) collective-permute-start(f32[7,16,128]{2,1,0:T(8,128)S(1)} %get-tuple-element.39), channel_id=1, source_target_pairs={{0,14},{2,12},{4,10},{6,8},{8,6},{10,4},{12,2},{14,0},{1,15},{3,13... | collective-permute-start | bytes 172040 | tf_op jit(solution)/shard_map/ppermute | solution.py:612
  33.2 11.0 %collective-permute-start.11 = (f32[5,16,128]{2,1,0:T(8,128)S(1)}, f32[5,16,128]{2,1,0:T(8,128)S(1)}, u32[]{:S(2)}, u32[]{:S(2)}) collective-permute-start(f32[5,16,128]{2,1,0:T(8,128)S(1)} %get-tuple-element.45), channel_id=1, source_target_pairs={{0,2},{2,0},{1,3},{3,1},{4,6},{6,4},{5,7},{7,5},{8,10},{10,8},{9,1... | collective-permute-start | bytes 122888 | tf_op jit(solution)/shard_map/ppermute | solution.py:603
  44.3 2.2 %collective-permute-start.12 = (f32[60,8,128]{2,1,0:T(8,128)S(1)}, f32[60,8,128]{2,1,0:T(8,128)S(1)}, u32[]{:S(2)}, u32[]{:S(2)}) collective-permute-start(f32[60,8,128]{2,1,0:T(8,128)S(1)} %pad_maximum_fusion.2), channel_id=1, source_target_pairs={{0,1},{1,0},{2,3},{3,2},{4,5},{5,4},{6,7},{7,6},{8,9},{9,8},{10,11... | collective-permute-start | bytes 737288 | tf_op jit(solution)/shard_map/ppermute | solution.py:603

commit v6 on v5

--- a/solution.py
+++ b/solution.py
@@ -667,6 +667,7 @@
     xz_in = across_turned(x_out, 1)
     r_b = across(z_b, 1)
     za_y, ra_y = sent([edge(z_a)], [edge(r_a)])
+    r_b, za_y, ra_y = lax.optimization_barrier((r_b, za_y, ra_y))
     xr_y, xzr_y, zb_y, rb_y = sent([edge(x_in)], [edge(xz_in)], [edge(z_b)], [edge(r_b)])
     msg, turn, h, xa, eb = call(
         functools.partial(message_kernel, rows, wide),

time: 50.1 us -> 48.5 us (0.968)
  waiting for transfers between devices: 21.9 us -> 18 us
  starting transfers between devices: 11.7 us -> 14 us
    ppermute x2, waiting for transfers between devices: 15 us -> 10.2 us  [across_turned(): return lax.ppermute(block, ('tm', 'space'), route)]
    ppermute x8, starting transfers between devices: 5.49 us -> 8.19 us  [swapped(): return lax.ppermute(block, axis, [(0, 1), (1, 0)])]
    ppermute x8, waiting for transfers between devices: 5.35 us -> 6.61 us  [swapped(): return lax.ppermute(block, axis, [(0, 1), (1, 0)])]
    ppermute x2, starting transfers between devices: 4.38 us -> 3.18 us  [across_turned(): return lax.ppermute(block, ('tm', 'space'), route)]
    ppermute x3, starting transfers between devices: 1.84 us -> 2.66 us  [across(): return lax.ppermute(block, 'tm', [(i, i ^ distance) for i in range(4)])]
  transfers between devices with their start and end apart: 13 -> 13, of which waited for: 8 -> 10; matrix products, arithmetic and copies ran while one was open for 0% -> 0% of each run, Pallas kernels for 17% -> 17%
where the time goes in v6:
time: 48.5 us; the launch traced here: 48.3 us
  waiting for transfers between devices  18 us (37%)
  Pallas kernels  15.2 us (31%)
  starting transfers between devices  14 us (29%)
  between operations  0.79 us (2%)
    pallas_call x6, Pallas kernels, call(): pl.pallas_call(kernel, out_shape=[jax.ShapeDtypeStruct(shape, jnp.float32...  15.2 us
    ppermute x2, waiting for transfers between devices, across_turned(): return lax.ppermute(block, ('tm', 'space'), route)  10.2 us
    ppermute x8, starting transfers between devices, swapped(): return lax.ppermute(block, axis, [(0, 1), (1, 0)])  8.19 us
    ppermute x8, waiting for transfers between devices, swapped(): return lax.ppermute(block, axis, [(0, 1), (1, 0)])  6.61 us
    ppermute x2, starting transfers between devices, across_turned(): return lax.ppermute(block, ('tm', 'space'), route)  3.18 us
    ppermute x3, starting transfers between devices, across(): return lax.ppermute(block, 'tm', [(i, i ^ distance) for i in range(4)])  2.66 us
    ppermute x3, waiting for transfers between devices, across(): return lax.ppermute(block, 'tm', [(i, i ^ distance) for i in range(4)])  1.17 us
  transfers between devices with their start and end apart: 13, of which 10 were waited for; matrix products, arithmetic and copies ran while one was open for 0% of the time, Pallas kernels for 17%

profile of v6, /device:TPU:17, one launch (start us, length us, event | category | flops | bytes accessed | tf_op | source)
XLA Modules:
  0.0 48.3 jit_solution(9881882711259628600)
XLA Ops:
  0.6 0.1 pad_add_fusion.where_ref
  0.7 2.1 %shard_map.86 = (f32[44,16,128]{2,1,0:T(8,128)S(1)}, f32[8,24,8,128]{3,2,1,0:T(8,128)S(1)}) custom-call(s32[3]{0:T(128)S(1)} %pad_add_fusion.where_ref, f32[24,16,128]{2,1,0:T(8,128)} %d_hbm.1, f32[3,24,16,128]{3,2,1,0:T(8,128)} %u_hbm.1, f32[1,24,16,128]{3,2,1,0:T(8,128)} %control_hbm.1, f32[1,24,16,128]{3,2,1,0:T(8,128)} %sg_hbm.1, ...), custom_call_target="tpu_custom_call" | custom-call | flops 1000 | bytes 1000 | tf_op jit(solution)/shard_map/pallas_call | solution.py:589
  2.8 0.7 %collective-permute-start.1 = (f32[8,24,8,128]{3,2,1,0:T(8,128)S(1)}, f32[8,24,8,128]{3,2,1,0:T(8,128)S(1)}, u32[]{:S(2)}, u32[]{:S(2)}) collective-permute-start(f32[8,24,8,128]{3,2,1,0:T(8,128)S(1)} %get-tuple-element.31), channel_id=1, source_target_pairs={{0,1},{1,0},{2,3},{3,2},{4,5},{5,4},{6,7},{7,6},{8,9},{9,8},{10,11... | collective-permute-start | bytes 2359304 | tf_op jit(solution)/shard_map/ppermute | solution.py:603
  3.6 1.2 %collective-permute-start = (f32[44,16,128]{2,1,0:T(8,128)S(1)}, f32[44,16,128]{2,1,0:T(8,128)S(1)}, u32[]{:S(2)}, u32[]{:S(2)}) collective-permute-start(f32[44,16,128]{2,1,0:T(8,128)S(1)} %get-tuple-element.30), channel_id=1, source_target_pairs={{0,2},{2,0},{1,3},{3,1},{4,6},{6,4},{5,7},{7,5},{8,10},{10,8},{9,1... | collective-permute-start | bytes 1081352 | tf_op jit(solution)/shard_map/ppermute | solution.py:603
  4.8 0.7 %collective-permute-done.1.side_ref = f32[8,24,8,128]{3,2,1,0:T(8,128)S(1)} collective-permute-done((f32[8,24,8,128]{3,2,1,0:T(8,128)S(1)}, f32[8,24,8,128]{3,2,1,0:T(8,128)S(1)}, u32[]{:S(2)}, u32[]{:S(2)}) %collective-permute-start.1) | collective-permute-done | bytes 786464 | tf_op jit(solution)/shard_map/ppermute | solution.py:603
  5.5 6.1 %shard_map.87 = (f32[11,744,128]{2,1,0:T(8,128)S(1)}, f32[4,7,48,128]{3,2,1,0:T(8,128)S(1)}, f32[4,144,128]{2,1,0:T(8,128)S(1)}, f32[34,16,128]{2,1,0:T(8,128)S(...) custom-call(s32[3]{0:T(128)S(1)} %pad_add_fusion.where_ref, ...), custom_call_target="tpu_custom_call" | custom-call | flops 1000 | bytes 1000 | tf_op jit(solution)/shard_map/pallas_call | solution.py:589
  11.5 2.0 %collective-permute-done.xr_ref = f32[44,16,128]{2,1,0:T(8,128)S(1)} collective-permute-done((f32[44,16,128]{2,1,0:T(8,128)S(1)}, f32[44,16,128]{2,1,0:T(8,128)S(1)}, u32[]{:S(2)}, u32[]{:S(2)}) %collective-permute-start) | collective-permute-done | bytes 360480 | tf_op jit(solution)/shard_map/ppermute | solution.py:603
  13.6 1.3 %collective-permute-start.3 = (f32[34,16,128]{2,1,0:T(8,128)S(1)}, f32[34,16,128]{2,1,0:T(8,128)S(1)}, u32[]{:S(2)}, u32[]{:S(2)}) collective-permute-start(f32[34,16,128]{2,1,0:T(8,128)S(1)} %get-tuple-element.38.za), channel_id=1, source_target_pairs={{0,4},{4,0},{8,12},{12,8},{1,5},{5,1},{9,13},{13,9},{2,6},{6,2},{1... | collective-permute-start | bytes 835592 | tf_op jit(solution)/shard_map/ppermute | solution.py:607
  14.9 1.2 %collective-permute-start.2 = (f32[44,8,128]{2,1,0:T(8,128)S(1)}, f32[44,8,128]{2,1,0:T(8,128)S(1)}, u32[]{:S(2)}, u32[]{:S(2)}) collective-permute-start(f32[44,8,128]{2,1,0:T(8,128)S(1)} %constant_dynamic-slice_fusion.8), channel_id=1, source_target_pairs={{0,1},{1,0},{2,3},{3,2},{4,5},{5,4},{6,7},{7,6},{8,9},{9,8},{10,11... | collective-permute-start | bytes 540680 | tf_op jit(solution)/shard_map/ppermute | solution.py:603
  16.1 1.0 %collective-permute-done.2.ys_ref = f32[44,8,128]{2,1,0:T(8,128)S(1)} collective-permute-done((f32[44,8,128]{2,1,0:T(8,128)S(1)}, f32[44,8,128]{2,1,0:T(8,128)S(1)}, u32[]{:S(2)}, u32[]{:S(2)}) %collective-permute-start.2) | collective-permute-done | bytes 180256 | tf_op jit(solution)/shard_map/ppermute | solution.py:603
  17.1 1.8 %shard_map.88 = (f32[11,744,128]{2,1,0:T(8,128)S(1)}, f32[14,16,128]{2,1,0:T(8,128)S(1)}, f32[6,16,128]{2,1,0:T(8,128)S(1)}, f32[6,16,128]{2,1,0:T(8,128)S(1)}, f32[6,16,128]{2,1,0:T(8,128)S(1)}) custom-call(s32[3]{0:T(128)S(1)} %pad_add_fusion.where_ref, f32[11,744,128]{2,1,0:T(8,128)S(1)} %get-tuple-element.33.coef_in, ...), custom_call_target="tpu_custom_call", output_to_operand_aliasing={{0}: (1, {})} | custom-call | flops 1000 | bytes 1000 | tf_op jit(solution)/shard_map/pallas_call | solution.py:589
  18.9 1.2 %collective-permute-start.7 = (f32[6,16,128]{2,1,0:T(8,128)S(1)}, f32[6,16,128]{2,1,0:T(8,128)S(1)}, u32[]{:S(2)}, u32[]{:S(2)}) collective-permute-start(f32[6,16,128]{2,1,0:T(8,128)S(1)} %get-tuple-element.41), channel_id=1, source_target_pairs={{0,6},{2,4},{4,2},{6,0},{8,14},{10,12},{12,10},{14,8},{1,7},{3,5},... | collective-permute-start | bytes 147464 | tf_op jit(solution)/shard_map/ppermute | solution.py:612
  20.1 0.3 collective-permute-start.6
  20.3 1.3 %collective-permute-start.4 = (f32[14,16,128]{2,1,0:T(8,128)S(1)}, f32[14,16,128]{2,1,0:T(8,128)S(1)}, u32[]{:S(2)}, u32[]{:S(2)}) collective-permute-start(f32[14,16,128]{2,1,0:T(8,128)S(1)} %get-tuple-element.39.zb), channel_id=1, source_target_pairs={{0,4},{4,0},{8,12},{12,8},{1,5},{5,1},{9,13},{13,9},{2,6},{6,2},{1... | collective-permute-start | bytes 344072 | tf_op jit(solution)/shard_map/ppermute | solution.py:607
  21.6 0.0 collective-permute-done.3.ra
  21.6 1.3 %collective-permute-start.5 = (f32[68,8,128]{2,1,0:T(8,128)S(1)}, f32[68,8,128]{2,1,0:T(8,128)S(1)}, u32[]{:S(2)}, u32[]{:S(2)}) collective-permute-start(f32[68,8,128]{2,1,0:T(8,128)S(1)} %pad_maximum_fusion), channel_id=1, source_target_pairs={{0,1},{1,0},{2,3},{3,2},{4,5},{5,4},{6,7},{7,6},{8,9},{9,8},{10,11... | collective-permute-start | bytes 835592 | tf_op jit(solution)/shard_map/ppermute | solution.py:603
  22.9 0.5 collective-permute-done.7.xzr
  23.4 0.4 collective-permute-done.6.xr
  23.8 0.3 collective-permute-done.5
  24.1 1.2 %collective-permute-done.4.rb = f32[14,16,128]{2,1,0:T(8,128)S(1)} collective-permute-done((f32[14,16,128]{2,1,0:T(8,128)S(1)}, f32[14,16,128]{2,1,0:T(8,128)S(1)}, u32[]{:S(2)}, u32[]{:S(2)}) %collective-permute-start.4) | collective-permute-done | bytes 114720 | tf_op jit(solution)/shard_map/ppermute | solution.py:607
  25.3 1.3 %collective-permute-start.8 = (f32[40,8,128]{2,1,0:T(8,128)S(1)}, f32[40,8,128]{2,1,0:T(8,128)S(1)}, u32[]{:S(2)}, u32[]{:S(2)}) collective-permute-start(f32[40,8,128]{2,1,0:T(8,128)S(1)} %pad_maximum_fusion.3), channel_id=1, source_target_pairs={{0,1},{1,0},{2,3},{3,2},{4,5},{5,4},{6,7},{7,6},{8,9},{9,8},{10,11... | collective-permute-start | bytes 491528 | tf_op jit(solution)/shard_map/ppermute | solution.py:603
  26.6 1.0 %collective-permute-done.8 = f32[40,8,128]{2,1,0:T(8,128)S(1)} collective-permute-done((f32[40,8,128]{2,1,0:T(8,128)S(1)}, f32[40,8,128]{2,1,0:T(8,128)S(1)}, u32[]{:S(2)}, u32[]{:S(2)}) %collective-permute-start.8) | collective-permute-done | bytes 163872 | tf_op jit(solution)/shard_map/ppermute | solution.py:603
  27.6 1.2 %shard_map.89 = (f32[24,16,128]{2,1,0:T(8,128)S(1)}, f32[7,16,128]{2,1,0:T(8,128)S(1)}, f32[792,128]{1,0:T(8,128)S(1)}, f32[792,128]{1,0:T(8,128)S(1)}, f32[792,128]{1,0:T(8,128)S(1)}) custom-call(s32[3]{0:T(128)S(1)} %pad_add_fusion.where_ref, f32[11,744,128]{2,1,0:T(8,128)S(1)} %get-tuple-element.37.coef_ref, f32[34,16,128]{2,1,0:T(8,128)S(1)} %get-tuple-element.38.za, ...), custom_call_target="tpu_custom_call" | custom-call | flops 1000 | bytes 1000 | tf_op jit(solution)/shard_map/pallas_call | solution.py:589
  28.9 0.1 collective-permute-start.9
  29.0 2.0 %collective-permute-start.10 = (f32[7,16,128]{2,1,0:T(8,128)S(1)}, f32[7,16,128]{2,1,0:T(8,128)S(1)}, u32[]{:S(2)}, u32[]{:S(2)}) collective-permute-start(f32[7,16,128]{2,1,0:T(8,128)S(1)} %get-tuple-element.45), channel_id=1, source_target_pairs={{0,14},{2,12},{4,10},{6,8},{8,6},{10,4},{12,2},{14,0},{1,15},{3,13... | collective-permute-start | bytes 172040 | tf_op jit(solution)/shard_map/ppermute | solution.py:612
  31.0 0.6 %shard_map.90 = (f32[24,16,128]{2,1,0:T(8,128)S(1)}, f32[5,16,128]{2,1,0:T(8,128)S(1)}) custom-call(s32[3]{0:T(128)S(1)} %pad_add_fusion.where_ref, f32[11,744,128]{2,1,0:T(8,128)S(1)} %get-tuple-element.37.coef_ref, f32[792,128]{1,0:T(8,128)S(1)} %get-tuple-element.46.h_ref, f32[792,128]{1,0:T(8,128)S(1)} %get-tuple-element.47.xa_ref, ...), custom_call_target="tpu_custom_call" | custom-call | flops 1000 | bytes 1000 | tf_op jit(solution)/shard_map/pallas_call | solution.py:589
  31.6 0.7 %collective-permute-start.11 = (f32[5,16,128]{2,1,0:T(8,128)S(1)}, f32[5,16,128]{2,1,0:T(8,128)S(1)}, u32[]{:S(2)}, u32[]{:S(2)}) collective-permute-start(f32[5,16,128]{2,1,0:T(8,128)S(1)} %get-tuple-element.51), channel_id=1, source_target_pairs={{0,2},{2,0},{1,3},{3,1},{4,6},{6,4},{5,7},{7,5},{8,10},{10,8},{9,1... | collective-permute-start | bytes 122888 | tf_op jit(solution)/shard_map/ppermute | solution.py:603
  32.3 9.7 %collective-permute-done.10 = f32[7,16,128]{2,1,0:T(8,128)S(1)} collective-permute-done((f32[7,16,128]{2,1,0:T(8,128)S(1)}, f32[7,16,128]{2,1,0:T(8,128)S(1)}, u32[]{:S(2)}, u32[]{:S(2)}) %collective-permute-start.10) | collective-permute-done | bytes 57376 | tf_op jit(solution)/shard_map/ppermute | solution.py:612
  42.0 0.0 collective-permute-done.9
  42.0 0.0 collective-permute-done.11
  42.1 1.6 %collective-permute-start.12 = (f32[60,8,128]{2,1,0:T(8,128)S(1)}, f32[60,8,128]{2,1,0:T(8,128)S(1)}, u32[]{:S(2)}, u32[]{:S(2)}) collective-permute-start(f32[60,8,128]{2,1,0:T(8,128)S(1)} %pad_maximum_fusion.2), channel_id=1, source_target_pairs={{0,1},{1,0},{2,3},{3,2},{4,5},{5,4},{6,7},{7,6},{8,9},{9,8},{10,11... | collective-permute-start | bytes 737288 | tf_op jit(solution)/shard_map/ppermute | solution.py:603
  43.7 1.1 %collective-permute-done.12 = f32[60,8,128]{2,1,0:T(8,128)S(1)} collective-permute-done((f32[60,8,128]{2,1,0:T(8,128)S(1)}, f32[60,8,128]{2,1,0:T(8,128)S(1)}, u32[]{:S(2)}, u32[]{:S(2)}) %collective-permute-start.12) | collective-permute-done | bytes 245792 | tf_op jit(solution)/shard_map/ppermute | solution.py:603
  44.9 3.4 %shard_map.91 = (f32[1,24,16,128]{3,2,1,0:T(8,128)}, f32[1,24,16,128]{3,2,1,0:T(8,128)}) custom-call(s32[3]{0:T(128)S(1)} %pad_add_fusion.where_ref, f32[11,744,128]{2,1,0:T(8,128)S(1)} %get-tuple-element.37.coef_ref, f32[31,16,128]{2,1,0:T(8,128)S(1)} %pad_maximum_fusion.1.msg, f32[31,8,128]{2,1,0:T(8,128)S(1)} %slice.38.msg_y, ...), custom_call_target="tpu_custom_call" | custom-call | flops 1000 | bytes 1000 | tf_op jit(solution)/shard_map/pallas_call | solution.py:589
  (20 shorter events, 0.2 us)
Async XLA Ops:
  2.8 2.7 %collective-permute-start.1 = (f32[8,24,8,128]{3,2,1,0:T(8,128)S(1)}, f32[8,24,8,128]{3,2,1,0:T(8,128)S(1)}, u32[]{:S(2)}, u32[]{:S(2)}) collective-permute-start(f32[8,24,8,128]{3,2,1,0:T(8,128)S(1)} %get-tuple-element.31), channel_id=1, source_target_pairs={{0,1},{1,0},{2,3},{3,2},{4,5},{5,4},{6,7},{7,6},{8,9},{9,8},{10,11... | collective-permute-start | bytes 2359304 | tf_op jit(solution)/shard_map/ppermute | solution.py:603
  3.6 10.0 %collective-permute-start = (f32[44,16,128]{2,1,0:T(8,128)S(1)}, f32[44,16,128]{2,1,0:T(8,128)S(1)}, u32[]{:S(2)}, u32[]{:S(2)}) collective-permute-start(f32[44,16,128]{2,1,0:T(8,128)S(1)} %get-tuple-element.30), channel_id=1, source_target_pairs={{0,2},{2,0},{1,3},{3,1},{4,6},{6,4},{5,7},{7,5},{8,10},{10,8},{9,1... | collective-permute-start | bytes 1081352 | tf_op jit(solution)/shard_map/ppermute | solution.py:603
  13.6 8.1 %collective-permute-start.3 = (f32[34,16,128]{2,1,0:T(8,128)S(1)}, f32[34,16,128]{2,1,0:T(8,128)S(1)}, u32[]{:S(2)}, u32[]{:S(2)}) collective-permute-start(f32[34,16,128]{2,1,0:T(8,128)S(1)} %get-tuple-element.38.za), channel_id=1, source_target_pairs={{0,4},{4,0},{8,12},{12,8},{1,5},{5,1},{9,13},{13,9},{2,6},{6,2},{1... | collective-permute-start | bytes 835592 | tf_op jit(solution)/shard_map/ppermute | solution.py:607
  14.9 2.2 %collective-permute-start.2 = (f32[44,8,128]{2,1,0:T(8,128)S(1)}, f32[44,8,128]{2,1,0:T(8,128)S(1)}, u32[]{:S(2)}, u32[]{:S(2)}) collective-permute-start(f32[44,8,128]{2,1,0:T(8,128)S(1)} %constant_dynamic-slice_fusion.8), channel_id=1, source_target_pairs={{0,1},{1,0},{2,3},{3,2},{4,5},{5,4},{6,7},{7,6},{8,9},{9,8},{10,11... | collective-permute-start | bytes 540680 | tf_op jit(solution)/shard_map/ppermute | solution.py:603
  18.9 4.5 %collective-permute-start.7 = (f32[6,16,128]{2,1,0:T(8,128)S(1)}, f32[6,16,128]{2,1,0:T(8,128)S(1)}, u32[]{:S(2)}, u32[]{:S(2)}) collective-permute-start(f32[6,16,128]{2,1,0:T(8,128)S(1)} %get-tuple-element.41), channel_id=1, source_target_pairs={{0,6},{2,4},{4,2},{6,0},{8,14},{10,12},{12,10},{14,8},{1,7},{3,5},... | collective-permute-start | bytes 147464 | tf_op jit(solution)/shard_map/ppermute | solution.py:612
  20.1 3.7 %collective-permute-start.6 = (f32[6,16,128]{2,1,0:T(8,128)S(1)}, f32[6,16,128]{2,1,0:T(8,128)S(1)}, u32[]{:S(2)}, u32[]{:S(2)}) collective-permute-start(f32[6,16,128]{2,1,0:T(8,128)S(1)} %get-tuple-element.41), channel_id=1, source_target_pairs={{0,2},{2,0},{1,3},{3,1},{4,6},{6,4},{5,7},{7,5},{8,10},{10,8},{9,1... | collective-permute-start | bytes 147464 | tf_op jit(solution)/shard_map/ppermute | solution.py:603
  20.3 5.0 %collective-permute-start.4 = (f32[14,16,128]{2,1,0:T(8,128)S(1)}, f32[14,16,128]{2,1,0:T(8,128)S(1)}, u32[]{:S(2)}, u32[]{:S(2)}) collective-permute-start(f32[14,16,128]{2,1,0:T(8,128)S(1)} %get-tuple-element.39.zb), channel_id=1, source_target_pairs={{0,4},{4,0},{8,12},{12,8},{1,5},{5,1},{9,13},{13,9},{2,6},{6,2},{1... | collective-permute-start | bytes 344072 | tf_op jit(solution)/shard_map/ppermute | solution.py:607
  21.6 2.5 %collective-permute-start.5 = (f32[68,8,128]{2,1,0:T(8,128)S(1)}, f32[68,8,128]{2,1,0:T(8,128)S(1)}, u32[]{:S(2)}, u32[]{:S(2)}) collective-permute-start(f32[68,8,128]{2,1,0:T(8,128)S(1)} %pad_maximum_fusion), channel_id=1, source_target_pairs={{0,1},{1,0},{2,3},{3,2},{4,5},{5,4},{6,7},{7,6},{8,9},{9,8},{10,11... | collective-permute-start | bytes 835592 | tf_op jit(solution)/shard_map/ppermute | solution.py:603
  25.3 2.3 %collective-permute-start.8 = (f32[40,8,128]{2,1,0:T(8,128)S(1)}, f32[40,8,128]{2,1,0:T(8,128)S(1)}, u32[]{:S(2)}, u32[]{:S(2)}) collective-permute-start(f32[40,8,128]{2,1,0:T(8,128)S(1)} %pad_maximum_fusion.3), channel_id=1, source_target_pairs={{0,1},{1,0},{2,3},{3,2},{4,5},{5,4},{6,7},{7,6},{8,9},{9,8},{10,11... | collective-permute-start | bytes 491528 | tf_op jit(solution)/shard_map/ppermute | solution.py:603
  28.9 13.1 %collective-permute-start.9 = (f32[24,16,128]{2,1,0:T(8,128)S(1)}, f32[24,16,128]{2,1,0:T(8,128)S(1)}, u32[]{:S(2)}, u32[]{:S(2)}) collective-permute-start(f32[24,16,128]{2,1,0:T(8,128)S(1)} %get-tuple-element.44), channel_id=1, source_target_pairs={{0,12},{4,8},{8,4},{12,0},{1,13},{5,9},{9,5},{13,1},{2,14},{6,10},... | collective-permute-start | bytes 589832 | tf_op jit(solution)/shard_map/ppermute | solution.py:607
  29.0 13.0 %collective-permute-start.10 = (f32[7,16,128]{2,1,0:T(8,128)S(1)}, f32[7,16,128]{2,1,0:T(8,128)S(1)}, u32[]{:S(2)}, u32[]{:S(2)}) collective-permute-start(f32[7,16,128]{2,1,0:T(8,128)S(1)} %get-tuple-element.45), channel_id=1, source_target_pairs={{0,14},{2,12},{4,10},{6,8},{8,6},{10,4},{12,2},{14,0},{1,15},{3,13... | collective-permute-start | bytes 172040 | tf_op jit(solution)/shard_map/ppermute | solution.py:612
  31.6 10.4 %collective-permute-start.11 = (f32[5,16,128]{2,1,0:T(8,128)S(1)}, f32[5,16,128]{2,1,0:T(8,128)S(1)}, u32[]{:S(2)}, u32[]{:S(2)}) collective-permute-start(f32[5,16,128]{2,1,0:T(8,128)S(1)} %get-tuple-element.51), channel_id=1, source_target_pairs={{0,2},{2,0},{1,3},{3,1},{4,6},{6,4},{5,7},{7,5},{8,10},{10,8},{9,1... | collective-permute-start | bytes 122888 | tf_op jit(solution)/shard_map/ppermute | solution.py:603
  42.1 2.7 %collective-permute-start.12 = (f32[60,8,128]{2,1,0:T(8,128)S(1)}, f32[60,8,128]{2,1,0:T(8,128)S(1)}, u32[]{:S(2)}, u32[]{:S(2)}) collective-permute-start(f32[60,8,128]{2,1,0:T(8,128)S(1)} %pad_maximum_fusion.2), channel_id=1, source_target_pairs={{0,1},{1,0},{2,3},{3,2},{4,5},{5,4},{6,7},{7,6},{8,9},{9,8},{10,11... | collective-permute-start | bytes 737288 | tf_op jit(solution)/shard_map/ppermute | solution.py:603

commit v7 on v6

--- a/solution.py
+++ b/solution.py
@@ -224,7 +224,7 @@
 
 
 def pack_kernel(rows, own, where_ref, d_ref, u_ref, control_ref, sg_ref, ag_ref, initial_ref, target_ref,
-                x_out, side_out, rims, sides, sem):
+                x_out, side_out, sem):
     slab, space, core = where_ref[0], where_ref[1], where_ref[2]
     fields = (d_ref, u_ref.at[0], u_ref.at[1], u_ref.at[2], control_ref.at[0], sg_ref.at[0], None, target_ref.at[0])
     starts = (ag_ref.at[0], initial_ref)
@@ -241,17 +241,32 @@
     def edge(field):
         return field.at[:, pl.ds(beside, SIDE)]
 
-    for i, field in enumerate(starts):
-        bring(field.at[rim(6)], rims.at[i])
-        bring(edge(field), sides.at[i])
+    def begin(field):
+        at = pl.ds(STARTS[6], RIMS[6])
+        return [
+            pltpu.make_async_copy(field.at[rim(6)], x_out.at[at], sem.at[2 * len(RIMS)]),
+            pltpu.make_async_copy(edge(field), side_out.at[6], sem.at[2 * len(RIMS) + 1]),
+        ]
+
+    for wanted, field in zip((slab != 0, slab == 0), starts):
+
+        @pl.when(wanted)
+        def _(field=field):
+            for copy in begin(field):
+                copy.start()
+
     for i, field in enumerate(fields):
         if field is not None:
             bring(field.at[rim(i)], x_out.at[pl.ds(STARTS[i], RIMS[i])])
             bring(edge(field), side_out.at[i])
     for copy in copies:
         copy.wait()
-    x_out[pl.ds(STARTS[6], RIMS[6])] = jnp.where(slab == 0, rims[1], rims[0])
-    side_out[6] = jnp.where(slab == 0, sides[1], sides[0])
+    for wanted, field in zip((slab != 0, slab == 0), starts):
+
+        @pl.when(wanted)
+        def _(field=field):
+            for copy in begin(field):
+                copy.wait()
 
 
 def inner_kernel(rows, wide, where_ref, d_hbm, u_hbm, control_hbm, sg_hbm, ag_hbm, initial_hbm, target_hbm, side_ref,
@@ -636,7 +651,7 @@
     x_send, side_send = call(
         functools.partial(pack_kernel, rows, own),
         [cells(sum(RIMS)), (len(RIMS), *edges)],
-        [(2, *cells(RIMS[6])), (2, *edges), pltpu.SemaphoreType.DMA((2 * len(RIMS) + 2,))],
+        [pltpu.SemaphoreType.DMA((2 * len(RIMS) + 2,))],
         where, *inputs,
         in_hbm=len(inputs),
     )

time: 48.5 us -> 48.4 us (level)
  no operation moved by 1% of the time
where the time goes in v7:
time: 48.4 us; the launch traced here: 48.2 us
  waiting for transfers between devices  18 us (37%)
  Pallas kernels  15.1 us (31%)
  starting transfers between devices  14 us (29%)
  between operations  0.79 us (2%)
    pallas_call x6, Pallas kernels, call(): pl.pallas_call(kernel, out_shape=[jax.ShapeDtypeStruct(shape, jnp.float32...  15.1 us
    ppermute x2, waiting for transfers between devices, across_turned(): return lax.ppermute(block, ('tm', 'space'), route)  10.2 us
    ppermute x8, starting transfers between devices, swapped(): return lax.ppermute(block, axis, [(0, 1), (1, 0)])  8.19 us
    ppermute x8, waiting for transfers between devices, swapped(): return lax.ppermute(block, axis, [(0, 1), (1, 0)])  6.61 us
    ppermute x2, starting transfers between devices, across_turned(): return lax.ppermute(block, ('tm', 'space'), route)  3.18 us
    ppermute x3, starting transfers between devices, across(): return lax.ppermute(block, 'tm', [(i, i ^ distance) for i in range(4)])  2.66 us
    ppermute x3, waiting for transfers between devices, across(): return lax.ppermute(block, 'tm', [(i, i ^ distance) for i in range(4)])  1.17 us
  transfers between devices with their start and end apart: 13, of which 10 were waited for; matrix products, arithmetic and copies ran while one was open for 0% of the time, Pallas kernels for 17%

profile of v7, /device:TPU:17, one launch (start us, length us, event | category | flops | bytes accessed | tf_op | source)
XLA Modules:
  0.0 48.2 jit_solution(4087695008039999464)
XLA Ops:
  0.6 0.1 pad_add_fusion.where_ref
  0.7 2.0 %shard_map.86 = (f32[44,16,128]{2,1,0:T(8,128)S(1)}, f32[8,24,8,128]{3,2,1,0:T(8,128)S(1)}) custom-call(s32[3]{0:T(128)S(1)} %pad_add_fusion.where_ref, f32[24,16,128]{2,1,0:T(8,128)} %d_hbm.1, f32[3,24,16,128]{3,2,1,0:T(8,128)} %u_hbm.1, f32[1,24,16,128]{3,2,1,0:T(8,128)} %control_hbm.1, f32[1,24,16,128]{3,2,1,0:T(8,128)} %sg_hbm.1, ...), custom_call_target="tpu_custom_call" | custom-call | flops 1000 | bytes 1000 | tf_op jit(solution)/shard_map/pallas_call | solution.py:604
  2.8 0.7 %collective-permute-start.1 = (f32[8,24,8,128]{3,2,1,0:T(8,128)S(1)}, f32[8,24,8,128]{3,2,1,0:T(8,128)S(1)}, u32[]{:S(2)}, u32[]{:S(2)}) collective-permute-start(f32[8,24,8,128]{3,2,1,0:T(8,128)S(1)} %get-tuple-element.31), channel_id=1, source_target_pairs={{0,1},{1,0},{2,3},{3,2},{4,5},{5,4},{6,7},{7,6},{8,9},{9,8},{10,11... | collective-permute-start | bytes 2359304 | tf_op jit(solution)/shard_map/ppermute | solution.py:618
  3.5 1.2 %collective-permute-start = (f32[44,16,128]{2,1,0:T(8,128)S(1)}, f32[44,16,128]{2,1,0:T(8,128)S(1)}, u32[]{:S(2)}, u32[]{:S(2)}) collective-permute-start(f32[44,16,128]{2,1,0:T(8,128)S(1)} %get-tuple-element.30), channel_id=1, source_target_pairs={{0,2},{2,0},{1,3},{3,1},{4,6},{6,4},{5,7},{7,5},{8,10},{10,8},{9,1... | collective-permute-start | bytes 1081352 | tf_op jit(solution)/shard_map/ppermute | solution.py:618
  4.7 0.7 %collective-permute-done.1.side_ref = f32[8,24,8,128]{3,2,1,0:T(8,128)S(1)} collective-permute-done((f32[8,24,8,128]{3,2,1,0:T(8,128)S(1)}, f32[8,24,8,128]{3,2,1,0:T(8,128)S(1)}, u32[]{:S(2)}, u32[]{:S(2)}) %collective-permute-start.1) | collective-permute-done | bytes 786464 | tf_op jit(solution)/shard_map/ppermute | solution.py:618
  5.4 6.1 %shard_map.87 = (f32[11,744,128]{2,1,0:T(8,128)S(1)}, f32[4,7,48,128]{3,2,1,0:T(8,128)S(1)}, f32[4,144,128]{2,1,0:T(8,128)S(1)}, f32[34,16,128]{2,1,0:T(8,128)S(...) custom-call(s32[3]{0:T(128)S(1)} %pad_add_fusion.where_ref, ...), custom_call_target="tpu_custom_call" | custom-call | flops 1000 | bytes 1000 | tf_op jit(solution)/shard_map/pallas_call | solution.py:604
  11.5 2.0 %collective-permute-done.xr_ref = f32[44,16,128]{2,1,0:T(8,128)S(1)} collective-permute-done((f32[44,16,128]{2,1,0:T(8,128)S(1)}, f32[44,16,128]{2,1,0:T(8,128)S(1)}, u32[]{:S(2)}, u32[]{:S(2)}) %collective-permute-start) | collective-permute-done | bytes 360480 | tf_op jit(solution)/shard_map/ppermute | solution.py:618
  13.5 1.3 %collective-permute-start.3 = (f32[34,16,128]{2,1,0:T(8,128)S(1)}, f32[34,16,128]{2,1,0:T(8,128)S(1)}, u32[]{:S(2)}, u32[]{:S(2)}) collective-permute-start(f32[34,16,128]{2,1,0:T(8,128)S(1)} %get-tuple-element.38.za), channel_id=1, source_target_pairs={{0,4},{4,0},{8,12},{12,8},{1,5},{5,1},{9,13},{13,9},{2,6},{6,2},{1... | collective-permute-start | bytes 835592 | tf_op jit(solution)/shard_map/ppermute | solution.py:622
  14.8 1.2 %collective-permute-start.2 = (f32[44,8,128]{2,1,0:T(8,128)S(1)}, f32[44,8,128]{2,1,0:T(8,128)S(1)}, u32[]{:S(2)}, u32[]{:S(2)}) collective-permute-start(f32[44,8,128]{2,1,0:T(8,128)S(1)} %constant_dynamic-slice_fusion.8), channel_id=1, source_target_pairs={{0,1},{1,0},{2,3},{3,2},{4,5},{5,4},{6,7},{7,6},{8,9},{9,8},{10,11... | collective-permute-start | bytes 540680 | tf_op jit(solution)/shard_map/ppermute | solution.py:618
  16.0 1.0 %collective-permute-done.2.ys_ref = f32[44,8,128]{2,1,0:T(8,128)S(1)} collective-permute-done((f32[44,8,128]{2,1,0:T(8,128)S(1)}, f32[44,8,128]{2,1,0:T(8,128)S(1)}, u32[]{:S(2)}, u32[]{:S(2)}) %collective-permute-start.2) | collective-permute-done | bytes 180256 | tf_op jit(solution)/shard_map/ppermute | solution.py:618
  17.0 1.8 %shard_map.88 = (f32[11,744,128]{2,1,0:T(8,128)S(1)}, f32[14,16,128]{2,1,0:T(8,128)S(1)}, f32[6,16,128]{2,1,0:T(8,128)S(1)}, f32[6,16,128]{2,1,0:T(8,128)S(1)}, f32[6,16,128]{2,1,0:T(8,128)S(1)}) custom-call(s32[3]{0:T(128)S(1)} %pad_add_fusion.where_ref, f32[11,744,128]{2,1,0:T(8,128)S(1)} %get-tuple-element.33.coef_in, ...), custom_call_target="tpu_custom_call", output_to_operand_aliasing={{0}: (1, {})} | custom-call | flops 1000 | bytes 1000 | tf_op jit(solution)/shard_map/pallas_call | solution.py:604
  18.8 1.2 %collective-permute-start.7 = (f32[6,16,128]{2,1,0:T(8,128)S(1)}, f32[6,16,128]{2,1,0:T(8,128)S(1)}, u32[]{:S(2)}, u32[]{:S(2)}) collective-permute-start(f32[6,16,128]{2,1,0:T(8,128)S(1)} %get-tuple-element.41), channel_id=1, source_target_pairs={{0,6},{2,4},{4,2},{6,0},{8,14},{10,12},{12,10},{14,8},{1,7},{3,5},... | collective-permute-start | bytes 147464 | tf_op jit(solution)/shard_map/ppermute | solution.py:627
  20.0 0.3 collective-permute-start.6
  20.2 1.3 %collective-permute-start.4 = (f32[14,16,128]{2,1,0:T(8,128)S(1)}, f32[14,16,128]{2,1,0:T(8,128)S(1)}, u32[]{:S(2)}, u32[]{:S(2)}) collective-permute-start(f32[14,16,128]{2,1,0:T(8,128)S(1)} %get-tuple-element.39.zb), channel_id=1, source_target_pairs={{0,4},{4,0},{8,12},{12,8},{1,5},{5,1},{9,13},{13,9},{2,6},{6,2},{1... | collective-permute-start | bytes 344072 | tf_op jit(solution)/shard_map/ppermute | solution.py:622
  21.5 0.0 collective-permute-done.3.ra
  21.6 1.3 %collective-permute-start.5 = (f32[68,8,128]{2,1,0:T(8,128)S(1)}, f32[68,8,128]{2,1,0:T(8,128)S(1)}, u32[]{:S(2)}, u32[]{:S(2)}) collective-permute-start(f32[68,8,128]{2,1,0:T(8,128)S(1)} %pad_maximum_fusion), channel_id=1, source_target_pairs={{0,1},{1,0},{2,3},{3,2},{4,5},{5,4},{6,7},{7,6},{8,9},{9,8},{10,11... | collective-permute-start | bytes 835592 | tf_op jit(solution)/shard_map/ppermute | solution.py:618
  22.9 0.5 collective-permute-done.7.xzr
  23.3 0.4 collective-permute-done.6.xr
  23.7 0.3 collective-permute-done.5
  24.1 1.2 %collective-permute-done.4.rb = f32[14,16,128]{2,1,0:T(8,128)S(1)} collective-permute-done((f32[14,16,128]{2,1,0:T(8,128)S(1)}, f32[14,16,128]{2,1,0:T(8,128)S(1)}, u32[]{:S(2)}, u32[]{:S(2)}) %collective-permute-start.4) | collective-permute-done | bytes 114720 | tf_op jit(solution)/shard_map/ppermute | solution.py:622
  25.3 1.3 %collective-permute-start.8 = (f32[40,8,128]{2,1,0:T(8,128)S(1)}, f32[40,8,128]{2,1,0:T(8,128)S(1)}, u32[]{:S(2)}, u32[]{:S(2)}) collective-permute-start(f32[40,8,128]{2,1,0:T(8,128)S(1)} %pad_maximum_fusion.3), channel_id=1, source_target_pairs={{0,1},{1,0},{2,3},{3,2},{4,5},{5,4},{6,7},{7,6},{8,9},{9,8},{10,11... | collective-permute-start | bytes 491528 | tf_op jit(solution)/shard_map/ppermute | solution.py:618
  26.5 1.0 %collective-permute-done.8 = f32[40,8,128]{2,1,0:T(8,128)S(1)} collective-permute-done((f32[40,8,128]{2,1,0:T(8,128)S(1)}, f32[40,8,128]{2,1,0:T(8,128)S(1)}, u32[]{:S(2)}, u32[]{:S(2)}) %collective-permute-start.8) | collective-permute-done | bytes 163872 | tf_op jit(solution)/shard_map/ppermute | solution.py:618
  27.6 1.2 %shard_map.89 = (f32[24,16,128]{2,1,0:T(8,128)S(1)}, f32[7,16,128]{2,1,0:T(8,128)S(1)}, f32[792,128]{1,0:T(8,128)S(1)}, f32[792,128]{1,0:T(8,128)S(1)}, f32[792,128]{1,0:T(8,128)S(1)}) custom-call(s32[3]{0:T(128)S(1)} %pad_add_fusion.where_ref, f32[11,744,128]{2,1,0:T(8,128)S(1)} %get-tuple-element.37.coef_ref, f32[34,16,128]{2,1,0:T(8,128)S(1)} %get-tuple-element.38.za, ...), custom_call_target="tpu_custom_call" | custom-call | flops 1000 | bytes 1000 | tf_op jit(solution)/shard_map/pallas_call | solution.py:604
  28.8 0.1 collective-permute-start.9
  28.9 2.0 %collective-permute-start.10 = (f32[7,16,128]{2,1,0:T(8,128)S(1)}, f32[7,16,128]{2,1,0:T(8,128)S(1)}, u32[]{:S(2)}, u32[]{:S(2)}) collective-permute-start(f32[7,16,128]{2,1,0:T(8,128)S(1)} %get-tuple-element.45), channel_id=1, source_target_pairs={{0,14},{2,12},{4,10},{6,8},{8,6},{10,4},{12,2},{14,0},{1,15},{3,13... | collective-permute-start | bytes 172040 | tf_op jit(solution)/shard_map/ppermute | solution.py:627
  30.9 0.6 %shard_map.90 = (f32[24,16,128]{2,1,0:T(8,128)S(1)}, f32[5,16,128]{2,1,0:T(8,128)S(1)}) custom-call(s32[3]{0:T(128)S(1)} %pad_add_fusion.where_ref, f32[11,744,128]{2,1,0:T(8,128)S(1)} %get-tuple-element.37.coef_ref, f32[792,128]{1,0:T(8,128)S(1)} %get-tuple-element.46.h_ref, f32[792,128]{1,0:T(8,128)S(1)} %get-tuple-element.47.xa_ref, ...), custom_call_target="tpu_custom_call" | custom-call | flops 1000 | bytes 1000 | tf_op jit(solution)/shard_map/pallas_call | solution.py:604
  31.5 0.7 %collective-permute-start.11 = (f32[5,16,128]{2,1,0:T(8,128)S(1)}, f32[5,16,128]{2,1,0:T(8,128)S(1)}, u32[]{:S(2)}, u32[]{:S(2)}) collective-permute-start(f32[5,16,128]{2,1,0:T(8,128)S(1)} %get-tuple-element.51), channel_id=1, source_target_pairs={{0,2},{2,0},{1,3},{3,1},{4,6},{6,4},{5,7},{7,5},{8,10},{10,8},{9,1... | collective-permute-start | bytes 122888 | tf_op jit(solution)/shard_map/ppermute | solution.py:618
  32.2 9.7 %collective-permute-done.10 = f32[7,16,128]{2,1,0:T(8,128)S(1)} collective-permute-done((f32[7,16,128]{2,1,0:T(8,128)S(1)}, f32[7,16,128]{2,1,0:T(8,128)S(1)}, u32[]{:S(2)}, u32[]{:S(2)}) %collective-permute-start.10) | collective-permute-done | bytes 57376 | tf_op jit(solution)/shard_map/ppermute | solution.py:627
  42.0 0.0 collective-permute-done.9
  42.0 0.0 collective-permute-done.11
  42.1 1.6 %collective-permute-start.12 = (f32[60,8,128]{2,1,0:T(8,128)S(1)}, f32[60,8,128]{2,1,0:T(8,128)S(1)}, u32[]{:S(2)}, u32[]{:S(2)}) collective-permute-start(f32[60,8,128]{2,1,0:T(8,128)S(1)} %pad_maximum_fusion.2), channel_id=1, source_target_pairs={{0,1},{1,0},{2,3},{3,2},{4,5},{5,4},{6,7},{7,6},{8,9},{9,8},{10,11... | collective-permute-start | bytes 737288 | tf_op jit(solution)/shard_map/ppermute | solution.py:618
  43.6 1.1 %collective-permute-done.12 = f32[60,8,128]{2,1,0:T(8,128)S(1)} collective-permute-done((f32[60,8,128]{2,1,0:T(8,128)S(1)}, f32[60,8,128]{2,1,0:T(8,128)S(1)}, u32[]{:S(2)}, u32[]{:S(2)}) %collective-permute-start.12) | collective-permute-done | bytes 245792 | tf_op jit(solution)/shard_map/ppermute | solution.py:618
  44.8 3.4 %shard_map.91 = (f32[1,24,16,128]{3,2,1,0:T(8,128)}, f32[1,24,16,128]{3,2,1,0:T(8,128)}) custom-call(s32[3]{0:T(128)S(1)} %pad_add_fusion.where_ref, f32[11,744,128]{2,1,0:T(8,128)S(1)} %get-tuple-element.37.coef_ref, f32[31,16,128]{2,1,0:T(8,128)S(1)} %pad_maximum_fusion.1.msg, f32[31,8,128]{2,1,0:T(8,128)S(1)} %slice.38.msg_y, ...), custom_call_target="tpu_custom_call" | custom-call | flops 1000 | bytes 1000 | tf_op jit(solution)/shard_map/pallas_call | solution.py:604
  (20 shorter events, 0.2 us)
Async XLA Ops:
  2.8 2.7 %collective-permute-start.1 = (f32[8,24,8,128]{3,2,1,0:T(8,128)S(1)}, f32[8,24,8,128]{3,2,1,0:T(8,128)S(1)}, u32[]{:S(2)}, u32[]{:S(2)}) collective-permute-start(f32[8,24,8,128]{3,2,1,0:T(8,128)S(1)} %get-tuple-element.31), channel_id=1, source_target_pairs={{0,1},{1,0},{2,3},{3,2},{4,5},{5,4},{6,7},{7,6},{8,9},{9,8},{10,11... | collective-permute-start | bytes 2359304 | tf_op jit(solution)/shard_map/ppermute | solution.py:618
  3.5 10.0 %collective-permute-start = (f32[44,16,128]{2,1,0:T(8,128)S(1)}, f32[44,16,128]{2,1,0:T(8,128)S(1)}, u32[]{:S(2)}, u32[]{:S(2)}) collective-permute-start(f32[44,16,128]{2,1,0:T(8,128)S(1)} %get-tuple-element.30), channel_id=1, source_target_pairs={{0,2},{2,0},{1,3},{3,1},{4,6},{6,4},{5,7},{7,5},{8,10},{10,8},{9,1... | collective-permute-start | bytes 1081352 | tf_op jit(solution)/shard_map/ppermute | solution.py:618
  13.5 8.1 %collective-permute-start.3 = (f32[34,16,128]{2,1,0:T(8,128)S(1)}, f32[34,16,128]{2,1,0:T(8,128)S(1)}, u32[]{:S(2)}, u32[]{:S(2)}) collective-permute-start(f32[34,16,128]{2,1,0:T(8,128)S(1)} %get-tuple-element.38.za), channel_id=1, source_target_pairs={{0,4},{4,0},{8,12},{12,8},{1,5},{5,1},{9,13},{13,9},{2,6},{6,2},{1... | collective-permute-start | bytes 835592 | tf_op jit(solution)/shard_map/ppermute | solution.py:622
  14.8 2.2 %collective-permute-start.2 = (f32[44,8,128]{2,1,0:T(8,128)S(1)}, f32[44,8,128]{2,1,0:T(8,128)S(1)}, u32[]{:S(2)}, u32[]{:S(2)}) collective-permute-start(f32[44,8,128]{2,1,0:T(8,128)S(1)} %constant_dynamic-slice_fusion.8), channel_id=1, source_target_pairs={{0,1},{1,0},{2,3},{3,2},{4,5},{5,4},{6,7},{7,6},{8,9},{9,8},{10,11... | collective-permute-start | bytes 540680 | tf_op jit(solution)/shard_map/ppermute | solution.py:618
  18.8 4.5 %collective-permute-start.7 = (f32[6,16,128]{2,1,0:T(8,128)S(1)}, f32[6,16,128]{2,1,0:T(8,128)S(1)}, u32[]{:S(2)}, u32[]{:S(2)}) collective-permute-start(f32[6,16,128]{2,1,0:T(8,128)S(1)} %get-tuple-element.41), channel_id=1, source_target_pairs={{0,6},{2,4},{4,2},{6,0},{8,14},{10,12},{12,10},{14,8},{1,7},{3,5},... | collective-permute-start | bytes 147464 | tf_op jit(solution)/shard_map/ppermute | solution.py:627
  20.0 3.7 %collective-permute-start.6 = (f32[6,16,128]{2,1,0:T(8,128)S(1)}, f32[6,16,128]{2,1,0:T(8,128)S(1)}, u32[]{:S(2)}, u32[]{:S(2)}) collective-permute-start(f32[6,16,128]{2,1,0:T(8,128)S(1)} %get-tuple-element.41), channel_id=1, source_target_pairs={{0,2},{2,0},{1,3},{3,1},{4,6},{6,4},{5,7},{7,5},{8,10},{10,8},{9,1... | collective-permute-start | bytes 147464 | tf_op jit(solution)/shard_map/ppermute | solution.py:618
  20.2 5.0 %collective-permute-start.4 = (f32[14,16,128]{2,1,0:T(8,128)S(1)}, f32[14,16,128]{2,1,0:T(8,128)S(1)}, u32[]{:S(2)}, u32[]{:S(2)}) collective-permute-start(f32[14,16,128]{2,1,0:T(8,128)S(1)} %get-tuple-element.39.zb), channel_id=1, source_target_pairs={{0,4},{4,0},{8,12},{12,8},{1,5},{5,1},{9,13},{13,9},{2,6},{6,2},{1... | collective-permute-start | bytes 344072 | tf_op jit(solution)/shard_map/ppermute | solution.py:622
  21.6 2.5 %collective-permute-start.5 = (f32[68,8,128]{2,1,0:T(8,128)S(1)}, f32[68,8,128]{2,1,0:T(8,128)S(1)}, u32[]{:S(2)}, u32[]{:S(2)}) collective-permute-start(f32[68,8,128]{2,1,0:T(8,128)S(1)} %pad_maximum_fusion), channel_id=1, source_target_pairs={{0,1},{1,0},{2,3},{3,2},{4,5},{5,4},{6,7},{7,6},{8,9},{9,8},{10,11... | collective-permute-start | bytes 835592 | tf_op jit(solution)/shard_map/ppermute | solution.py:618
  25.3 2.3 %collective-permute-start.8 = (f32[40,8,128]{2,1,0:T(8,128)S(1)}, f32[40,8,128]{2,1,0:T(8,128)S(1)}, u32[]{:S(2)}, u32[]{:S(2)}) collective-permute-start(f32[40,8,128]{2,1,0:T(8,128)S(1)} %pad_maximum_fusion.3), channel_id=1, source_target_pairs={{0,1},{1,0},{2,3},{3,2},{4,5},{5,4},{6,7},{7,6},{8,9},{9,8},{10,11... | collective-permute-start | bytes 491528 | tf_op jit(solution)/shard_map/ppermute | solution.py:618
  28.8 13.1 %collective-permute-start.9 = (f32[24,16,128]{2,1,0:T(8,128)S(1)}, f32[24,16,128]{2,1,0:T(8,128)S(1)}, u32[]{:S(2)}, u32[]{:S(2)}) collective-permute-start(f32[24,16,128]{2,1,0:T(8,128)S(1)} %get-tuple-element.44), channel_id=1, source_target_pairs={{0,12},{4,8},{8,4},{12,0},{1,13},{5,9},{9,5},{13,1},{2,14},{6,10},... | collective-permute-start | bytes 589832 | tf_op jit(solution)/shard_map/ppermute | solution.py:622
  28.9 13.0 %collective-permute-start.10 = (f32[7,16,128]{2,1,0:T(8,128)S(1)}, f32[7,16,128]{2,1,0:T(8,128)S(1)}, u32[]{:S(2)}, u32[]{:S(2)}) collective-permute-start(f32[7,16,128]{2,1,0:T(8,128)S(1)} %get-tuple-element.45), channel_id=1, source_target_pairs={{0,14},{2,12},{4,10},{6,8},{8,6},{10,4},{12,2},{14,0},{1,15},{3,13... | collective-permute-start | bytes 172040 | tf_op jit(solution)/shard_map/ppermute | solution.py:627
  31.5 10.4 %collective-permute-start.11 = (f32[5,16,128]{2,1,0:T(8,128)S(1)}, f32[5,16,128]{2,1,0:T(8,128)S(1)}, u32[]{:S(2)}, u32[]{:S(2)}) collective-permute-start(f32[5,16,128]{2,1,0:T(8,128)S(1)} %get-tuple-element.51), channel_id=1, source_target_pairs={{0,2},{2,0},{1,3},{3,1},{4,6},{6,4},{5,7},{7,5},{8,10},{10,8},{9,1... | collective-permute-start | bytes 122888 | tf_op jit(solution)/shard_map/ppermute | solution.py:618
  42.1 2.7 %collective-permute-start.12 = (f32[60,8,128]{2,1,0:T(8,128)S(1)}, f32[60,8,128]{2,1,0:T(8,128)S(1)}, u32[]{:S(2)}, u32[]{:S(2)}) collective-permute-start(f32[60,8,128]{2,1,0:T(8,128)S(1)} %pad_maximum_fusion.2), channel_id=1, source_target_pairs={{0,1},{1,0},{2,3},{3,2},{4,5},{5,4},{6,7},{7,6},{8,9},{9,8},{10,11... | collective-permute-start | bytes 737288 | tf_op jit(solution)/shard_map/ppermute | solution.py:618
